TPU v7x, 128 devices: a whole 4x4x4 slice. The times are simulated.
128 devices in a mesh: row: 8 (over x_lo, y), col: 16 (over x_hi, z, core).
Axes of the slice: x: 4 (x_hi: 2, x_lo: 2; x = x_hi * 2 + x_lo), y: 4, z: 4, core: 2. Of those that a mesh axis runs over, the one named last changes fastest.
Arguments:
- block_input: bfloat16 [128, 1024, 512], P('row', 'col'), may hold values from -6 to 6
- cotangent: bfloat16 [128, 1024, 512], P('row', 'col'), may hold values from -6 to 6
- qkv_weight: bfloat16 [512, 1536], replicated, as said below
- out_weight: bfloat16 [512, 512], replicated, may hold values from -0.25 to 0.25
- bias_table: float32 [16, 225], replicated, may hold values from -4 to 4
- norm_gain: float32 [512], replicated, may hold values from 0.5 to 1.5
- norm_shift: float32 [512], replicated, may hold values from -1.5 to 1.5
Outputs:
- grad_input: bfloat16 [128, 1024, 512], P('row', 'col')
- grad_qkv: float32 [512, 1536], P(('row', 'col'))
- grad_out: float32 [512, 512], P(('row', 'col'))
- grad_table: float32 [16, 225], replicated
- grad_gain: float32 [512], replicated
- grad_shift: float32 [512], replicated
Inputs may be any that keep to these rules, and one draw needn't show every extreme that they name: `qkv_weight`: entries lie within -96 / sqrt(512) and 96 / sqrt(512).
All inputs are finite; a program needn't handle non-finite values.
Results may differ from a plain program's by a relative error of at most 0.012.
The roundings to bfloat16 on the way count: a program that leaves them out, or rounds other values in their place, can miss the bound.
Values may be sent and summed in bfloat16 or wider, within the bound.
No kernel may reach another device: no remote copies, remote signals or barrier semaphores. Data moves between devices by JAX's collectives and lax.ppermute only.
A program may use at most 128 MiB of HBM per device.

v0:
```python
import functools
import jax
import jax.numpy as jnp
from jax import lax
from jax.experimental import pallas as pl
from jax.experimental.pallas import tpu as pltpu
from jax.sharding import Mesh, PartitionSpec as P

GRID = 8
EPSILON = 1e-05
MEMBERS = GRID * GRID
PACK = 4


def dot(a, b, ca, cb):
    return lax.dot_general(a, b, (((ca,), (cb,)), ((), ())), preferred_element_type=jnp.float32)


def backward_kernel(
    core_ref, pair_ref, wqkv_ref, wout_ref, bias_ref, gain_ref, shift_ref,
    branch_ref, keep_ref, send_ref, gbias_ref, gvec_ref,
    proj, gatt, normed, dyp, hat, istd, gproj, att, bran, *, groups, width, head_dim,
):
    rows = groups * MEMBERS
    chunk = 256
    per = chunk // MEMBERS
    bf16, f32 = jnp.bfloat16, jnp.float32
    scale = head_dim ** (-0.5)

    def norm_step(c, carry):
        r = lax.broadcasted_iota(jnp.int32, (chunk, rows), 0)
        s = lax.broadcasted_iota(jnp.int32, (chunk, rows), 1)
        sel = (s == (r % MEMBERS) * groups + c * per + r // MEMBERS).astype(f32).astype(bf16)
        pair = pair_ref[...]
        xs = pair[:, :groups].reshape(rows, width)
        ds = pair[:, groups:].reshape(rows, width)
        x = dot(sel, xs, 1, 0)
        dy = dot(sel, ds, 1, 0).astype(bf16)
        here = pl.ds(pl.multiple_of(c * chunk, chunk), chunk)
        dyp[here, :] = dy
        centred = x - jnp.mean(x, axis=-1, keepdims=True)
        inv = lax.rsqrt(jnp.mean(centred * centred, axis=-1, keepdims=True) + EPSILON)
        normalized = centred * inv
        hat[here, :] = normalized
        istd[here, :] = jnp.broadcast_to(inv, (chunk, 128))
        nb = (normalized * gain_ref[...] + shift_ref[...]).astype(bf16)
        normed[here, :] = nb
        proj[here, :] = dot(nb, wqkv_ref[...], 1, 0).astype(bf16)
        gatt[here, :] = dot(dy, wout_ref[...], 1, 1).astype(bf16)
        return carry

    lax.fori_loop(0, rows // chunk, norm_step, 0)

    gbias_ref[...] = jnp.zeros_like(gbias_ref)
    lane = lax.broadcasted_iota(jnp.int32, (MEMBERS, 128), 1) // head_dim

    def spread(a):
        zero = jnp.zeros_like(a)
        return jnp.concatenate([jnp.where(lane == h, a, zero) for h in range(PACK)], axis=0)

    def gather(a):
        out = a[:MEMBERS]
        for h in range(1, PACK):
            out = jnp.where(lane == h, a[h * MEMBERS : (h + 1) * MEMBERS], out)
        return out

    def group_step(g, carry):
        here = pl.ds(pl.multiple_of(g * MEMBERS, MEMBERS), MEMBERS)
        for block in range(width // 128):
            cols = slice(block * 128, (block + 1) * 128)
            q = proj[here, cols]
            k = proj[here, width + block * 128 : width + (block + 1) * 128]
            v = proj[here, 2 * width + block * 128 : 2 * width + (block + 1) * 128]
            ga = gatt[here, cols]
            q_bd = spread(q)
            ga_bd = spread(ga)
            scores = dot(k, q_bd, 1, 1) * scale + bias_ref[block]
            gp = dot(v, ga_bd, 1, 1)
            e = jnp.exp(scores - jnp.max(scores, axis=0, keepdims=True))
            p = e / jnp.sum(e, axis=0, keepdims=True)
            pb = p.astype(bf16)
            gs = p * (gp - jnp.sum(gp * p, axis=0, keepdims=True))
            gbias_ref[block] += gs
            sg = (gs * scale).astype(bf16)
            att[here, cols] = gather(dot(pb, v, 0, 0)).astype(bf16)
            gproj[here, cols] = gather(dot(sg, k, 0, 0)).astype(bf16)
            gproj[here, width + block * 128 : width + (block + 1) * 128] = dot(sg, q_bd, 1, 0).astype(bf16)
            gproj[here, 2 * width + block * 128 : 2 * width + (block + 1) * 128] = dot(pb, ga_bd, 1, 0).astype(bf16)
        return carry

    lax.fori_loop(0, groups, group_step, 0)

    def back_step(c, carry):
        gg, gsh = carry
        here = pl.ds(pl.multiple_of(c * chunk, chunk), chunk)
        gn = dot(gproj[here, :], wqkv_ref[...], 1, 1)
        normalized = hat[here, :]
        prod = gn * normalized
        gg = gg + jnp.sum(prod.reshape(chunk // 8, 8, width), axis=0)
        gsh = gsh + jnp.sum(gn.reshape(chunk // 8, 8, width), axis=0)
        gh = gn * gain_ref[...]
        m1 = jnp.mean(gh, axis=-1, keepdims=True)
        m2 = jnp.mean(prod * gain_ref[...], axis=-1, keepdims=True)
        inv = istd[here, :][:, :1]
        bran[here, :] = (inv * (gh - m1 - normalized * m2)).astype(bf16)
        return gg, gsh

    zero = jnp.zeros((8, width), f32)
    gg, gsh = lax.fori_loop(0, rows // chunk, back_step, (zero, zero))
    gvec_ref[0:1, :] = jnp.sum(gg, axis=0, keepdims=True)
    gvec_ref[1:2, :] = jnp.sum(gsh, axis=0, keepdims=True)

    def out_step(c, carry):
        r = lax.broadcasted_iota(jnp.int32, (chunk, rows), 0)
        s = lax.broadcasted_iota(jnp.int32, (chunk, rows), 1)
        mem = chunk // groups
        sel = (s == (r % groups) * MEMBERS + c * mem + r // groups).astype(f32).astype(bf16)
        here = pl.ds(pl.multiple_of(c * mem, mem), mem)
        branch_ref[here] = dot(sel, bran[...], 1, 0).astype(bf16).reshape(mem, groups, width)
        return carry

    lax.fori_loop(0, rows // chunk, out_step, 0)

    half = 2 * width
    gw = dot(normed[...], gproj[...], 0, 0)
    go = dot(att[...], dyp[...], 0, 0)
    low = gw[:, :half]
    high = jnp.concatenate([gw[:, half:], go], axis=1)

    @pl.when(core_ref[0] == 0)
    def _():
        keep_ref[...] = low
        send_ref[...] = high.astype(bf16)

    @pl.when(core_ref[0] != 0)
    def _():
        keep_ref[...] = high
        send_ref[...] = low.astype(bf16)


def fused(core, pair, wqkv, wout, bias, gain, shift, head_dim=32):
    members, two_groups, width = pair.shape
    groups = two_groups // 2
    rows = groups * MEMBERS
    f32, bf16 = jnp.float32, jnp.bfloat16
    vm = pl.BlockSpec(memory_space=pltpu.VMEM)
    return pl.pallas_call(
        functools.partial(backward_kernel, groups=groups, width=width, head_dim=head_dim),
        out_shape=(
            jax.ShapeDtypeStruct((members, groups, width), bf16),
            jax.ShapeDtypeStruct((width, 2 * width), f32),
            jax.ShapeDtypeStruct((width, 2 * width), bf16),
            jax.ShapeDtypeStruct(bias.shape, f32),
            jax.ShapeDtypeStruct((8, width), f32),
        ),
        in_specs=[pl.BlockSpec(memory_space=pltpu.SMEM)] + [vm] * 6,
        out_specs=(vm,) * 5,
        scratch_shapes=[
            pltpu.VMEM((rows, 3 * width), bf16),
            pltpu.VMEM((rows, width), bf16),
            pltpu.VMEM((rows, width), bf16),
            pltpu.VMEM((rows, width), bf16),
            pltpu.VMEM((rows, width), f32),
            pltpu.VMEM((rows, 128), f32),
            pltpu.VMEM((rows, 3 * width), bf16),
            pltpu.VMEM((rows, width), bf16),
            pltpu.VMEM((rows, width), bf16),
        ],
        compiler_params=pltpu.CompilerParams(vmem_limit_bytes=56 * 1024 * 1024),
        name="fused_backward",
    )(core, pair, wqkv, wout, bias, gain.reshape(1, width), shift.reshape(1, width))


AXES = ("x_lo", "y", "x_hi", "z", "core")
CHIPS = AXES[:4]


def relative_onehot(members):
    span = 2 * GRID - 1
    second = jnp.arange(members, dtype=jnp.int32)[:, None]
    first = jnp.arange(members, dtype=jnp.int32)[None, :]
    row_delta = first // GRID - second // GRID + GRID - 1
    col_delta = first % GRID - second % GRID + GRID - 1
    rel_index = row_delta * span + col_delta
    offsets = jnp.arange(span * span, dtype=jnp.int32)
    return (rel_index[:, :, None] == offsets).astype(jnp.float32)


def swap(a, axis, mask):
    size = lax.axis_size(axis)
    return lax.ppermute(a, axis, [(i, i ^ mask) for i in range(size)])


def sum_everywhere(a):
    a = a + swap(a, "core", 1)
    for axis in ("z", "y", ("x_lo", "x_hi")):
        parts = [swap(a, axis, mask) for mask in (1, 2, 3)]
        a = (a + parts[0]) + (parts[1] + parts[2])
    return a


def local(block_input, cotangent, qkv_weight, out_weight, bias_table, norm_gain, norm_shift):
    tile_h, tile_w, width = block_input.shape
    heads, offsets = bias_table.shape
    chips = lax.axis_size(CHIPS)
    owned = tile_h * tile_w // chips
    devices = chips * lax.axis_size("core")
    core = lax.axis_index("core")
    onehot = relative_onehot(MEMBERS)
    bias = jnp.einsum(
        "bhr,kqr->bkhq",
        bias_table.reshape(heads // PACK, PACK, offsets),
        onehot,
        precision=lax.Precision.HIGHEST,
    ).reshape(heads // PACK, MEMBERS, PACK * MEMBERS)
    pair = jnp.concatenate(
        (block_input.reshape(chips, owned, width), cotangent.reshape(chips, owned, width)), axis=1
    )
    pair = lax.all_to_all(pair, CHIPS, split_axis=0, concat_axis=0, tiled=True)
    branch, keep, send, gbias, gvec = fused(
        core.reshape(1), pair, qkv_weight, out_weight, bias, norm_gain, norm_shift, width // heads
    )
    weights = (keep + swap(send, "core", 1).astype(jnp.float32)).astype(jnp.bfloat16)
    weights = weights.reshape(chips, width // chips, 2 * width)
    weights = lax.all_to_all(weights, CHIPS, split_axis=0, concat_axis=0, tiled=True)
    returned = lax.all_to_all(branch, CHIPS, split_axis=0, concat_axis=0, tiled=True)
    returned = returned.reshape(tile_h, tile_w, width)
    grad_input = (cotangent.astype(jnp.float32) + returned.astype(jnp.float32)).astype(jnp.bfloat16)

    factor = float(tile_h * tile_w * devices) ** (-0.5)
    table = jnp.einsum(
        "bkhq,kqr->bhr",
        gbias.reshape(heads // PACK, MEMBERS, PACK, MEMBERS),
        onehot,
        precision=lax.Precision.HIGHEST,
    )
    small = jnp.concatenate((table.reshape(-1), gvec[:2].reshape(-1)))
    small = jnp.pad(small, (0, -small.size % 128)).reshape(-1, 128)
    small = sum_everywhere(small).reshape(-1) * factor
    cut = heads * offsets

    part = jnp.sum(weights.astype(jnp.float32), axis=0) * factor
    share = part.shape[0] // 2
    mine = lax.dynamic_slice_in_dim(part, core * share, share, 0)
    other = swap(lax.dynamic_slice_in_dim(part, (1 - core) * share, share, 0), "core", 1)
    low = jnp.where(core == 0, mine, other)
    high = jnp.where(core == 0, other, mine)
    grad_qkv = jnp.concatenate((low, high[:, :width]), axis=1)
    grad_out = high[:, width:]
    return (
        grad_input,
        grad_qkv,
        grad_out,
        small[:cut].reshape(heads, offsets),
        small[cut : cut + width],
        small[cut + width : cut + 2 * width],
    )


def solution(mesh):
    fine = Mesh(mesh.devices.reshape(2, 4, 2, 4, 2), AXES)
    tile = P(("x_lo", "y"), ("x_hi", "z", "core"), None)
    return jax.shard_map(
        local,
        mesh=fine,
        in_specs=(tile, tile, P(), P(), P(), P(), P()),
        out_specs=(tile, P(AXES, None), P(AXES, None), P(), P(), P()),
        check_vma=False,
    )
```

profile of v0, /device:TPU:1, one launch (start us, length us, event | category | flops | bytes accessed | tf_op | source)
XLA Modules:
  0.0 146.4 jit_solution(17582315749859052238)
XLA Ops:
  0.6 3.1 %pad_maximum_fusion = bf16[64,32,512]{2,1,0:T(8,128)(2,1)} fusion(bf16[64,16,512]{2,1,0:T(8,128)(2,1)} %bitcast.43, bf16[64,16,512]{2,1,0:T(8,128)(2,1)} %bitcast.44), kind=kLoop, calls=%fused_computation.5 | loop fusion | flops 4194304 | bytes 4194304 | tf_op jit(solution)/shard_map/concatenate | solution.py:216
  3.7 12.1 %all-to-all-start = ((bf16[64,32,512]{2,1,0:T(8,128)(2,1)}), bf16[64,32,512]{2,1,0:T(8,128)(2,1)S(1)}, u32[]{:S(2)}, u32[]{:S(2)}) async-start(bf16[64,32,512]{2,1,0:T(8,128)(2,1)} %pad_maximum_fusion), calls=%async_computation | async-start | bytes 4194304 | tf_op jit(solution)/shard_map/all_to_all | solution.py:219
  16.0 3.2 %fusion.9 = f32[4,64,4,64]{3,2,0,1:T(4,128)S(1)} fusion(f32[4,4,225,1]{2,1,0,3:T(4,128)S(1)} %reshape.234, s32[64,64]{1,0:T(8,128)S(1)} %add_add_fusion), kind=kOutput, calls=%fused_computation.12 | convolution fusion | flops 177868800 | bytes 292928 | tf_op jit(solution)/shard_map/bhr,kqr->bkhq/dot_general | solution.py:210
  20.3 22.6 %all-to-all-done.pair_ref = bf16[64,32,512]{2,1,0:T(8,128)(2,1)S(1)} async-done(((bf16[64,32,512]{2,1,0:T(8,128)(2,1)}), bf16[64,32,512]{2,1,0:T(8,128)(2,1)S(1)}, u32[]{:S(2)}, u32[]{:S(2)}) %all-to-all-start) | async-done | bytes 2097184 | tf_op jit(solution)/shard_map/all_to_all | solution.py:219
  42.9 1.3 copy-done
  44.2 38.7 %fused_backward.1 = (bf16[64,16,512]{2,1,0:T(8,128)(2,1)}, f32[512,1024]{1,0:T(8,128)}, bf16[512,1024]{1,0:T(8,128)(2,1)}, f32[4,64,256]{2,1,0:T(8,128)}, f32[8,512]{1,0:T(8,128)}) custom-call(s32[1]{0:T(128)} %bitcast.core_ref, bf16[64,32,512]{2,1,0:T(8,128)(2,1)} %copy-done, bf16[512,1536]{1,0:T(8,128)(2,1)} %wqkv_ref.1, bf16[512,512]{1,0:T(8,128)(2,1)} %wout_ref.1, ...), custom_call_target="tpu_custom_call" | custom-call | tf_op jit(solution)/shard_map/fused_backward/pallas_call | solution.py:147
  82.9 2.7 %collective-permute-start = (bf16[512,1024]{1,0:T(8,128)(2,1)}, bf16[512,1024]{1,0:T(8,128)(2,1)S(1)}, u32[]{:S(2)}, u32[]{:S(2)}) collective-permute-start(bf16[512,1024]{1,0:T(8,128)(2,1)} %get-tuple-element.13), channel_id=1, source_target_pairs={{0,1},{1,0},{2,3},{3,2},{4,5},{5,4},{6,7},{7,6},{8,9},{9,8},{10,11... | collective-permute-start | bytes 3145736 | tf_op jit(solution)/shard_map/ppermute | solution.py:191
  85.7 2.5 %collective-permute-done = bf16[512,1024]{1,0:T(8,128)(2,1)S(1)} collective-permute-done((bf16[512,1024]{1,0:T(8,128)(2,1)}, bf16[512,1024]{1,0:T(8,128)(2,1)S(1)}, u32[]{:S(2)}, u32[]{:S(2)}) %collective-permute-start) | collective-permute-done | bytes 1048608 | tf_op jit(solution)/shard_map/ppermute | solution.py:191
  88.2 2.9 %fusion.15 = bf16[64,8,1024]{2,1,0:T(8,128)(2,1)} fusion(f32[512,1024]{1,0:T(8,128)} %get-tuple-element.12, bf16[512,1024]{1,0:T(8,128)(2,1)S(1)} %collective-permute-done), kind=kLoop, calls=%fused_computation.14 | loop fusion | flops 1572864 | bytes 4194304 | tf_op jit(solution)/shard_map/reshape | solution.py:224
  91.1 7.3 %all-to-all-start.2 = ((bf16[64,8,1024]{2,1,0:T(8,128)(2,1)}), bf16[64,8,1024]{2,1,0:T(8,128)(2,1)S(1)}, u32[]{:S(2)}, u32[]{:S(2)}) async-start(bf16[64,8,1024]{2,1,0:T(8,128)(2,1)} %fusion.15), calls=%async_computation.2 | async-start | bytes 2097152 | tf_op jit(solution)/shard_map/all_to_all | solution.py:225
  98.7 1.5 %fusion.12 = f32[4,4,225]{2,1,0:T(4,128)S(1)} fusion(f32[4,64,4,64]{3,2,1,0:T(4,128)S(1)} %reshape.227, s32[64,64]{1,0:T(8,128)S(1)} %add_add_fusion), kind=kOutput, calls=%fused_computation.13 | convolution fusion | flops 177868800 | bytes 292928 | tf_op jit(solution)/shard_map/bkhq,kqr->bhr/dot_general | solution.py:231
  101.9 0.8 collective-permute-done.2
  102.8 1.3 collective-permute-start.3
  104.1 2.4 %collective-permute-start.4 = (f32[37,128]{1,0:T(8,128)S(1)}, f32[37,128]{1,0:T(8,128)S(1)}, u32[]{:S(2)}, u32[]{:S(2)}) collective-permute-start(f32[37,128]{1,0:T(8,128)S(1)} %fusion.17), channel_id=1, source_target_pairs={{0,4},{2,6},{4,0},{6,2},{1,5},{3,7},{5,1},{7,3},{8,12},{10,14},{12... | collective-permute-start | bytes 56840 | tf_op jit(solution)/shard_map/ppermute | solution.py:191
  106.7 6.1 %collective-permute-done.4 = f32[37,128]{1,0:T(8,128)S(1)} collective-permute-done((f32[37,128]{1,0:T(8,128)S(1)}, f32[37,128]{1,0:T(8,128)S(1)}, u32[]{:S(2)}, u32[]{:S(2)}) %collective-permute-start.4) | collective-permute-done | bytes 18976 | tf_op jit(solution)/shard_map/ppermute | solution.py:191
  112.8 3.3 %collective-permute-done.5 = f32[37,128]{1,0:T(8,128)S(1)} collective-permute-done((f32[37,128]{1,0:T(8,128)S(1)}, f32[37,128]{1,0:T(8,128)S(1)}, u32[]{:S(2)}, u32[]{:S(2)}) %collective-permute-start.5) | collective-permute-done | bytes 18976 | tf_op jit(solution)/shard_map/ppermute | solution.py:191
  116.9 3.1 %collective-permute-start.8 = (f32[37,128]{1,0:T(8,128)S(1)}, f32[37,128]{1,0:T(8,128)S(1)}, u32[]{:S(2)}, u32[]{:S(2)}) collective-permute-start(f32[37,128]{1,0:T(8,128)S(1)} %add_add_fusion.2), channel_id=1, source_target_pairs={{0,48},{16,32},{32,16},{48,0},{1,49},{17,33},{33,17},{49,1},{2,50}... | collective-permute-start | bytes 56840 | tf_op jit(solution)/shard_map/ppermute | solution.py:191
  120.0 6.1 %all-to-all-start.1 = ((bf16[64,16,512]{2,1,0:T(8,128)(2,1)}), bf16[64,16,512]{2,1,0:T(8,128)(2,1)S(1)}, u32[]{:S(2)}, u32[]{:S(2)}) async-start(bf16[64,16,512]{2,1,0:T(8,128)(2,1)} %get-tuple-element.11), calls=%async_computation.1 | async-start | bytes 2097152 | tf_op jit(solution)/shard_map/all_to_all | solution.py:226
  126.2 1.2 collective-permute-start.10
  127.3 1.7 %collective-permute-start.11 = (f32[37,128]{1,0:T(8,128)S(1)}, f32[37,128]{1,0:T(8,128)S(1)}, u32[]{:S(2)}, u32[]{:S(2)}) collective-permute-start(f32[37,128]{1,0:T(8,128)S(1)} %add_add_fusion.1), channel_id=1, source_target_pairs={{0,72},{8,64},{64,8},{72,0},{1,73},{9,65},{65,9},{73,1},{2,74},{10... | collective-permute-start | bytes 56840 | tf_op jit(solution)/shard_map/ppermute | solution.py:191
  129.8 8.2 %collective-permute-done.10 = f32[37,128]{1,0:T(8,128)S(1)} collective-permute-done((f32[37,128]{1,0:T(8,128)S(1)}, f32[37,128]{1,0:T(8,128)S(1)}, u32[]{:S(2)}, u32[]{:S(2)}) %collective-permute-start.10) | collective-permute-done | bytes 18976 | tf_op jit(solution)/shard_map/ppermute | solution.py:191
  137.9 1.4 collective-permute-done.11
  141.4 2.5 %collective-permute-start.1 = (f32[4,1024]{1,0:T(4,128)S(1)}, f32[4,1024]{1,0:T(4,128)S(1)}, u32[]{:S(2)}, u32[]{:S(2)}) collective-permute-start(f32[4,1024]{1,0:T(4,128)S(1)} %constant_dynamic-slice_fusion), channel_id=1, source_target_pairs={{0,1},{1,0},{2,3},{3,2},{4,5},{5,4},{6,7},{7,6},{8,9},{9,8},{10,11... | collective-permute-start | bytes 49160 | tf_op jit(solution)/shard_map/ppermute | solution.py:191
  143.9 1.3 fusion.6
  (43 shorter events, 8.2 us)
Async XLA Ops:
  3.7 12.1 %copy-start.3 = (f32[16,225]{1,0:T(8,128)S(1)}, f32[16,225]{1,0:T(8,128)}, u32[]{:S(2)}) copy-start(f32[16,225]{1,0:T(8,128)} %param.11) | copy-start | bytes 43204
  3.7 39.2 %all-to-all-start = ((bf16[64,32,512]{2,1,0:T(8,128)(2,1)}), bf16[64,32,512]{2,1,0:T(8,128)(2,1)S(1)}, u32[]{:S(2)}, u32[]{:S(2)}) async-start(bf16[64,32,512]{2,1,0:T(8,128)(2,1)} %pad_maximum_fusion), calls=%async_computation | async-start | bytes 4194304 | tf_op jit(solution)/shard_map/all_to_all | solution.py:219
  42.9 1.3 copy-start
  82.9 5.2 %collective-permute-start = (bf16[512,1024]{1,0:T(8,128)(2,1)}, bf16[512,1024]{1,0:T(8,128)(2,1)S(1)}, u32[]{:S(2)}, u32[]{:S(2)}) collective-permute-start(bf16[512,1024]{1,0:T(8,128)(2,1)} %get-tuple-element.13), channel_id=1, source_target_pairs={{0,1},{1,0},{2,3},{3,2},{4,5},{5,4},{6,7},{7,6},{8,9},{9,8},{10,11... | collective-permute-start | bytes 3145736 | tf_op jit(solution)/shard_map/ppermute | solution.py:191
  91.1 7.3 %copy-start.2 = (f32[4,64,256]{2,1,0:T(8,128)S(1)}, f32[4,64,256]{2,1,0:T(8,128)}, u32[]{:S(2)}) copy-start(f32[4,64,256]{2,1,0:T(8,128)} %get-tuple-element.14) | copy-start | bytes 786436
  91.1 28.9 %all-to-all-start.2 = ((bf16[64,8,1024]{2,1,0:T(8,128)(2,1)}), bf16[64,8,1024]{2,1,0:T(8,128)(2,1)S(1)}, u32[]{:S(2)}, u32[]{:S(2)}) async-start(bf16[64,8,1024]{2,1,0:T(8,128)(2,1)} %fusion.15), calls=%async_computation.2 | async-start | bytes 2097152 | tf_op jit(solution)/shard_map/all_to_all | solution.py:225
  100.2 43.7 %copy-start.1 = (bf16[16,64,512]{2,1,0:T(8,128)(2,1)S(1)}, bf16[16,64,512]{2,1,0:T(8,128)(2,1)}, u32[]{:S(2)}) copy-start(bf16[16,64,512]{2,1,0:T(8,128)(2,1)} %param.8) | copy-start | bytes 3145732
  101.2 1.5 %collective-permute-start.2 = (f32[37,128]{1,0:T(8,128)S(1)}, f32[37,128]{1,0:T(8,128)S(1)}, u32[]{:S(2)}, u32[]{:S(2)}) collective-permute-start(f32[37,128]{1,0:T(8,128)S(1)} %fusion.16), channel_id=1, source_target_pairs={{0,1},{1,0},{2,3},{3,2},{4,5},{5,4},{6,7},{7,6},{8,9},{9,8},{10,11... | collective-permute-start | bytes 56840 | tf_op jit(solution)/shard_map/ppermute | solution.py:191
  102.8 3.9 %collective-permute-start.3 = (f32[37,128]{1,0:T(8,128)S(1)}, f32[37,128]{1,0:T(8,128)S(1)}, u32[]{:S(2)}, u32[]{:S(2)}) collective-permute-start(f32[37,128]{1,0:T(8,128)S(1)} %fusion.17), channel_id=1, source_target_pairs={{0,2},{2,0},{4,6},{6,4},{1,3},{3,1},{5,7},{7,5},{8,10},{10,8},{12,... | collective-permute-start | bytes 56840 | tf_op jit(solution)/shard_map/ppermute | solution.py:191
  104.1 8.7 %collective-permute-start.4 = (f32[37,128]{1,0:T(8,128)S(1)}, f32[37,128]{1,0:T(8,128)S(1)}, u32[]{:S(2)}, u32[]{:S(2)}) collective-permute-start(f32[37,128]{1,0:T(8,128)S(1)} %fusion.17), channel_id=1, source_target_pairs={{0,4},{2,6},{4,0},{6,2},{1,5},{3,7},{5,1},{7,3},{8,12},{10,14},{12... | collective-permute-start | bytes 56840 | tf_op jit(solution)/shard_map/ppermute | solution.py:191
  106.5 9.5 %collective-permute-start.5 = (f32[37,128]{1,0:T(8,128)S(1)}, f32[37,128]{1,0:T(8,128)S(1)}, u32[]{:S(2)}, u32[]{:S(2)}) collective-permute-start(f32[37,128]{1,0:T(8,128)S(1)} %fusion.17), channel_id=1, source_target_pairs={{0,6},{2,4},{4,2},{6,0},{1,7},{3,5},{5,3},{7,1},{8,14},{10,12},{12... | collective-permute-start | bytes 56840 | tf_op jit(solution)/shard_map/ppermute | solution.py:191
  116.1 10.0 %collective-permute-start.6 = (f32[37,128]{1,0:T(8,128)S(1)}, f32[37,128]{1,0:T(8,128)S(1)}, u32[]{:S(2)}, u32[]{:S(2)}) collective-permute-start(f32[37,128]{1,0:T(8,128)S(1)} %add_add_fusion.2), channel_id=1, source_target_pairs={{0,16},{16,0},{32,48},{48,32},{1,17},{17,1},{33,49},{49,33},{2,18}... | collective-permute-start | bytes 56840 | tf_op jit(solution)/shard_map/ppermute | solution.py:191
  116.2 10.0 %collective-permute-start.7 = (f32[37,128]{1,0:T(8,128)S(1)}, f32[37,128]{1,0:T(8,128)S(1)}, u32[]{:S(2)}, u32[]{:S(2)}) collective-permute-start(f32[37,128]{1,0:T(8,128)S(1)} %add_add_fusion.2), channel_id=1, source_target_pairs={{0,32},{16,48},{32,0},{48,16},{1,33},{17,49},{33,1},{49,17},{2,34}... | collective-permute-start | bytes 56840 | tf_op jit(solution)/shard_map/ppermute | solution.py:191
  116.9 9.2 %collective-permute-start.8 = (f32[37,128]{1,0:T(8,128)S(1)}, f32[37,128]{1,0:T(8,128)S(1)}, u32[]{:S(2)}, u32[]{:S(2)}) collective-permute-start(f32[37,128]{1,0:T(8,128)S(1)} %add_add_fusion.2), channel_id=1, source_target_pairs={{0,48},{16,32},{32,16},{48,0},{1,49},{17,33},{33,17},{49,1},{2,50}... | collective-permute-start | bytes 56840 | tf_op jit(solution)/shard_map/ppermute | solution.py:191
  120.0 23.9 %all-to-all-start.1 = ((bf16[64,16,512]{2,1,0:T(8,128)(2,1)}), bf16[64,16,512]{2,1,0:T(8,128)(2,1)S(1)}, u32[]{:S(2)}, u32[]{:S(2)}) async-start(bf16[64,16,512]{2,1,0:T(8,128)(2,1)} %get-tuple-element.11), calls=%async_computation.1 | async-start | bytes 2097152 | tf_op jit(solution)/shard_map/all_to_all | solution.py:226
  126.2 11.8 %collective-permute-start.10 = (f32[37,128]{1,0:T(8,128)S(1)}, f32[37,128]{1,0:T(8,128)S(1)}, u32[]{:S(2)}, u32[]{:S(2)}) collective-permute-start(f32[37,128]{1,0:T(8,128)S(1)} %add_add_fusion.1), channel_id=1, source_target_pairs={{0,64},{8,72},{64,0},{72,8},{1,65},{9,73},{65,1},{73,9},{2,66},{10... | collective-permute-start | bytes 56840 | tf_op jit(solution)/shard_map/ppermute | solution.py:191
  127.3 12.0 %collective-permute-start.11 = (f32[37,128]{1,0:T(8,128)S(1)}, f32[37,128]{1,0:T(8,128)S(1)}, u32[]{:S(2)}, u32[]{:S(2)}) collective-permute-start(f32[37,128]{1,0:T(8,128)S(1)} %add_add_fusion.1), channel_id=1, source_target_pairs={{0,72},{8,64},{64,8},{72,0},{1,73},{9,65},{65,9},{73,1},{2,74},{10... | collective-permute-start | bytes 56840 | tf_op jit(solution)/shard_map/ppermute | solution.py:191
  129.0 10.7 %collective-permute-start.9 = (f32[37,128]{1,0:T(8,128)S(1)}, f32[37,128]{1,0:T(8,128)S(1)}, u32[]{:S(2)}, u32[]{:S(2)}) collective-permute-start(f32[37,128]{1,0:T(8,128)S(1)} %add_add_fusion.1), channel_id=1, source_target_pairs={{0,8},{8,0},{64,72},{72,64},{1,9},{9,1},{65,73},{73,65},{2,10},{10... | collective-permute-start | bytes 56840 | tf_op jit(solution)/shard_map/ppermute | solution.py:191
  141.4 3.8 %collective-permute-start.1 = (f32[4,1024]{1,0:T(4,128)S(1)}, f32[4,1024]{1,0:T(4,128)S(1)}, u32[]{:S(2)}, u32[]{:S(2)}) collective-permute-start(f32[4,1024]{1,0:T(4,128)S(1)} %constant_dynamic-slice_fusion), channel_id=1, source_target_pairs={{0,1},{1,0},{2,3},{3,2},{4,5},{5,4},{6,7},{7,6},{8,9},{9,8},{10,11... | collective-permute-start | bytes 49160 | tf_op jit(solution)/shard_map/ppermute | solution.py:191
where the time goes:
time: 147 us; the launch traced here: 146 us
  waiting for transfers between devices  45.3 us (31%)
  starting transfers between devices  42.8 us (29%)
  Pallas kernels  38.7 us (26%)
  other arithmetic  8.47 us (6%)
  local copies, waits for them, and re-layouts  5.53 us (4%)
  matrix products  4.73 us (3%)
    pallas_call x1, Pallas kernels, fused(): pl.pallas_call(functools.partial(backward_kernel, groups=groups, width=wi...  38.7 us
    ppermute x12, waiting for transfers between devices, swap(): return lax.ppermute(a, axis, [(i, i ^ mask) for i in range(size)])  22.7 us
    all_to_all x1, waiting for transfers between devices, local(): pair = lax.all_to_all(pair, CHIPS, split_axis=0, concat_axis=0, tiled=True)  22.6 us
    ppermute x12, starting transfers between devices, swap(): return lax.ppermute(a, axis, [(i, i ^ mask) for i in range(size)])  17.3 us
    all_to_all x1, starting transfers between devices, local(): pair = lax.all_to_all(pair, CHIPS, split_axis=0, concat_axis=0, tiled=True)  12.1 us
    all_to_all x1, starting transfers between devices, local(): lax.all_to_all(weights, CHIPS, split_axis=0, concat_axis=0, tiled=True)  7.32 us
    all_to_all x1, starting transfers between devices, local(): lax.all_to_all(branch, CHIPS, split_axis=0, concat_axis=0, tiled=True)  6.08 us
    dot_general x1, matrix products, local(): jnp.einsum('bhr,kqr->bkhq', bias_table.reshape(heads // PACK, PACK, offse...  3.2 us
  transfers between devices with their start and end apart: 15, of which 9 were waited for; matrix products, arithmetic and copies ran while one was open for 7% of the time, Pallas kernels for 0%

commit v1 on v0

--- a/solution.py
+++ b/solution.py
@@ -19,13 +19,19 @@
 def backward_kernel(
     core_ref, pair_ref, wqkv_ref, wout_ref, bias_ref, gain_ref, shift_ref,
     branch_ref, keep_ref, send_ref, gbias_ref, gvec_ref,
-    proj, gatt, normed, dyp, hat, istd, gproj, att, bran, *, groups, width, head_dim,
+    proj, gatt, normed, dyp, hat, istd, gproj, att, bran, order, *, groups, width, head_dim,
 ):
     rows = groups * MEMBERS
     chunk = 256
     per = chunk // MEMBERS
     bf16, f32 = jnp.bfloat16, jnp.float32
     scale = head_dim ** (-0.5)
+    half = width // 2
+
+    f = lax.broadcasted_iota(jnp.int32, (width, width), 0)
+    r = lax.broadcasted_iota(jnp.int32, (width, width), 1)
+    chip = (((r // 8 % 2) * 4 + r // 16 % 4) * 2 + r // 4 % 2) * 4 + r // 64 % 4
+    order[...] = (f == chip * 8 + r // half * 4 + r % 4).astype(f32).astype(bf16)
 
     def norm_step(c, carry):
         r = lax.broadcasted_iota(jnp.int32, (chunk, rows), 0)
@@ -44,7 +50,7 @@
         hat[here, :] = normalized
         istd[here, :] = jnp.broadcast_to(inv, (chunk, 128))
         nb = (normalized * gain_ref[...] + shift_ref[...]).astype(bf16)
-        normed[here, :] = nb
+        normed[here, :] = dot(nb, order[...], 1, 0).astype(bf16)
         proj[here, :] = dot(nb, wqkv_ref[...], 1, 0).astype(bf16)
         gatt[here, :] = dot(dy, wout_ref[...], 1, 1).astype(bf16)
         return carry
@@ -121,21 +127,18 @@
 
     lax.fori_loop(0, rows // chunk, out_step, 0)
 
-    half = 2 * width
-    gw = dot(normed[...], gproj[...], 0, 0)
-    go = dot(att[...], dyp[...], 0, 0)
-    low = gw[:, :half]
-    high = jnp.concatenate([gw[:, half:], go], axis=1)
-
-    @pl.when(core_ref[0] == 0)
-    def _():
-        keep_ref[...] = low
-        send_ref[...] = high.astype(bf16)
-
-    @pl.when(core_ref[0] != 0)
-    def _():
-        keep_ref[...] = high
-        send_ref[...] = low.astype(bf16)
+    attended = dot(att[...], order[...], 1, 0).astype(bf16)
+
+    def put(ref, p):
+        rows_p = slice(p * half, (p + 1) * half)
+        ref[:, : 3 * width] = dot(normed[:, rows_p], gproj[...], 0, 0).astype(ref.dtype)
+        ref[:, 3 * width :] = dot(attended[:, rows_p], dyp[...], 0, 0).astype(ref.dtype)
+
+    for p in range(2):
+        @pl.when(core_ref[0] == p)
+        def _():
+            put(keep_ref, p)
+            put(send_ref, 1 - p)
 
 
 def fused(core, pair, wqkv, wout, bias, gain, shift, head_dim=32):
@@ -148,8 +151,8 @@
         functools.partial(backward_kernel, groups=groups, width=width, head_dim=head_dim),
         out_shape=(
             jax.ShapeDtypeStruct((members, groups, width), bf16),
-            jax.ShapeDtypeStruct((width, 2 * width), f32),
-            jax.ShapeDtypeStruct((width, 2 * width), bf16),
+            jax.ShapeDtypeStruct((width // 2, 4 * width), f32),
+            jax.ShapeDtypeStruct((width // 2, 4 * width), bf16),
             jax.ShapeDtypeStruct(bias.shape, f32),
             jax.ShapeDtypeStruct((8, width), f32),
         ),
@@ -165,10 +168,83 @@
             pltpu.VMEM((rows, 3 * width), bf16),
             pltpu.VMEM((rows, width), bf16),
             pltpu.VMEM((rows, width), bf16),
+            pltpu.VMEM((width, width), bf16),
         ],
         compiler_params=pltpu.CompilerParams(vmem_limit_bytes=56 * 1024 * 1024),
         name="fused_backward",
     )(core, pair, wqkv, wout, bias, gain.reshape(1, width), shift.reshape(1, width))
+
+
+def split_pair(a):
+    high = a.astype(jnp.bfloat16)
+    return high, (a - high.astype(jnp.float32)).astype(jnp.bfloat16)
+
+
+def stage_kernel(index_ref, *refs, arrivals, blocks, tail):
+    own_ref, small_ref = refs[:2]
+    arrived = refs[2 : 2 + arrivals]
+    outs = refs[2 + arrivals :]
+    f32 = jnp.float32
+    span = own_ref.shape[0]
+
+    def total(parts):
+        if len(parts) == 2:
+            return parts[0] + parts[1]
+        return (parts[0] + parts[1]) + (parts[2] + parts[3])
+
+    small = small_ref[...]
+    if arrivals == 3:
+        sent = [a[span : span + tail].astype(f32) + a[span + tail : span + 2 * tail].astype(f32) for a in arrived]
+        high, low = split_pair(small)
+        small = total([high.astype(f32) + low.astype(f32)] + sent)
+    else:
+        small = small + refs[2 + arrivals][...]
+        outs = refs[3 + arrivals :]
+    if blocks == 1:
+        outs[0][...] = total([own_ref[...]] + [a[:span].astype(f32) for a in arrived])
+        outs[1][...] = small
+        return
+    size = span // blocks
+    high, low = split_pair(small)
+    index = index_ref[0]
+    if size % 8:
+        whole = total([own_ref[...]] + [a[:span].astype(f32) for a in arrived])
+    for k in range(blocks):
+        if size % 8:
+            block = whole[:size]
+            for b in range(1, blocks):
+                block = jnp.where((index ^ k) == b, whole[b * size : (b + 1) * size], block)
+        else:
+            at = pl.ds(pl.multiple_of((index ^ k) * size, size), size)
+            block = total([own_ref[at, :]] + [a[at, :].astype(f32) for a in arrived])
+        if k == 0:
+            outs[0][...] = block
+            outs[1][...] = small
+        else:
+            outs[k + 1][:size] = block.astype(jnp.bfloat16)
+            outs[k + 1][size : size + tail] = high
+            outs[k + 1][size + tail : size + 2 * tail] = low
+
+
+def stage(index, own, small, arrived, blocks, small_arrived=()):
+    span, width = own.shape
+    tail = small.shape[0]
+    size = span // blocks
+    f32, bf16 = jnp.float32, jnp.bfloat16
+    vm = pl.BlockSpec(memory_space=pltpu.VMEM)
+    shapes = [jax.ShapeDtypeStruct((size, width), f32), jax.ShapeDtypeStruct((tail, width), f32)]
+    message = -(-(size + 2 * tail) // 16) * 16
+    shapes += [jax.ShapeDtypeStruct((message, width), bf16)] * (blocks - 1)
+    arrays = (own, small) + tuple(arrived) + tuple(small_arrived)
+    out = pl.pallas_call(
+        functools.partial(stage_kernel, arrivals=len(arrived), blocks=blocks, tail=tail),
+        out_shape=tuple(shapes),
+        in_specs=[pl.BlockSpec(memory_space=pltpu.SMEM)] + [vm] * len(arrays),
+        out_specs=(vm,) * len(shapes),
+        compiler_params=pltpu.CompilerParams(vmem_limit_bytes=32 * 1024 * 1024),
+        name=f"sum_in_{blocks}_blocks",
+    )(index.reshape(1), *arrays)
+    return out[0], out[1], out[2:]
 
 
 AXES = ("x_lo", "y", "x_hi", "z", "core")
@@ -189,14 +265,6 @@
 def swap(a, axis, mask):
     size = lax.axis_size(axis)
     return lax.ppermute(a, axis, [(i, i ^ mask) for i in range(size)])
-
-
-def sum_everywhere(a):
-    a = a + swap(a, "core", 1)
-    for axis in ("z", "y", ("x_lo", "x_hi")):
-        parts = [swap(a, axis, mask) for mask in (1, 2, 3)]
-        a = (a + parts[0]) + (parts[1] + parts[2])
-    return a
 
 
 def local(block_input, cotangent, qkv_weight, out_weight, bias_table, norm_gain, norm_shift):
@@ -220,9 +288,6 @@
     branch, keep, send, gbias, gvec = fused(
         core.reshape(1), pair, qkv_weight, out_weight, bias, norm_gain, norm_shift, width // heads
     )
-    weights = (keep + swap(send, "core", 1).astype(jnp.float32)).astype(jnp.bfloat16)
-    weights = weights.reshape(chips, width // chips, 2 * width)
-    weights = lax.all_to_all(weights, CHIPS, split_axis=0, concat_axis=0, tiled=True)
     returned = lax.all_to_all(branch, CHIPS, split_axis=0, concat_axis=0, tiled=True)
     returned = returned.reshape(tile_h, tile_w, width)
     grad_input = (cotangent.astype(jnp.float32) + returned.astype(jnp.float32)).astype(jnp.bfloat16)
@@ -235,22 +300,23 @@
         precision=lax.Precision.HIGHEST,
     )
     small = jnp.concatenate((table.reshape(-1), gvec[:2].reshape(-1)))
-    small = jnp.pad(small, (0, -small.size % 128)).reshape(-1, 128)
-    small = sum_everywhere(small).reshape(-1) * factor
+    columns = 4 * width
+    small = jnp.pad(small, (0, -small.size % columns)).reshape(-1, columns)
+    arrived, small_arrived = (swap(send, "core", 1),), (swap(small, "core", 1),)
+    share = keep
+    for axis in ("z", "y", ("x_lo", "x_hi")):
+        index = lax.axis_index(axis)
+        share, small, messages = stage(index, share, small, arrived, 4, small_arrived)
+        arrived = tuple(swap(message, axis, k + 1) for k, message in enumerate(messages))
+        small_arrived = ()
+    share, small, _ = stage(index, share, small, arrived, 1)
+    share = share * factor
+    small = small.reshape(-1) * factor
     cut = heads * offsets
-
-    part = jnp.sum(weights.astype(jnp.float32), axis=0) * factor
-    share = part.shape[0] // 2
-    mine = lax.dynamic_slice_in_dim(part, core * share, share, 0)
-    other = swap(lax.dynamic_slice_in_dim(part, (1 - core) * share, share, 0), "core", 1)
-    low = jnp.where(core == 0, mine, other)
-    high = jnp.where(core == 0, other, mine)
-    grad_qkv = jnp.concatenate((low, high[:, :width]), axis=1)
-    grad_out = high[:, width:]
     return (
         grad_input,
-        grad_qkv,
-        grad_out,
+        share[:, : 3 * width],
+        share[:, 3 * width :],
         small[:cut].reshape(heads, offsets),
         small[cut : cut + width],
         small[cut + width : cut + 2 * width],

time: 147 us -> 148 us (level)
  starting transfers between devices: 42.8 us -> 34.2 us
  waiting for transfers between devices: 45.3 us -> 49.4 us
  local copies, waits for them, and re-layouts: 5.53 us -> 8.74 us
  Pallas kernels: 38.7 us -> 41.4 us
  other arithmetic: 8.47 us -> 6.12 us
    all_to_all x1 -> x0, starting transfers between devices: 7.32 us -> none  [local(): lax.all_to_all(weights, CHIPS, split_axis=0, concat_axis=0, tiled=True)]
    ppermute x12 -> x11, waiting for transfers between devices: 22.7 us -> 26.8 us  [swap(): return lax.ppermute(a, axis, [(i, i ^ mask) for i in range(size)])]
    reshape x2 -> x0, other arithmetic: 3.01 us -> none  [the longest x1 2.93 us: local(): weights = weights.reshape(chips, width // chips, 2 * width)]
    ppermute x12 -> x11, starting transfers between devices: 17.3 us -> 14.3 us  [swap(): return lax.ppermute(a, axis, [(i, i ^ mask) for i in range(size)])]
    unnamed x10 -> x14, local copies, waits for them, and re-layouts: 2.11 us -> 3.88 us
    all_to_all x1, starting transfers between devices: 6.08 us -> 7.77 us  [local(): lax.all_to_all(branch, CHIPS, split_axis=0, concat_axis=0, tiled=True)]
    pallas_call x0 -> x4, Pallas kernels: none -> 1.59 us  [stage(): pl.pallas_call(functools.partial(stage_kernel, arrivals=len(arrived), blo...]
    convert_element_type x1, other arithmetic: 1.29 us -> 2.84 us  [local(): (cotangent.astype(jnp.float32) + returned.astype(jnp.float32)).astype(jnp...]
  transfers between devices with their start and end apart: 15 -> 13, of which waited for: 9 -> 8; matrix products, arithmetic and copies ran while one was open for 7% -> 8% of each run, Pallas kernels for 0% -> 1%
where the time goes in v1:
time: 148 us; the launch traced here: 146 us
  waiting for transfers between devices  49.4 us (33%)
  Pallas kernels  41.4 us (28%)
  starting transfers between devices  34.2 us (23%)
  local copies, waits for them, and re-layouts  8.74 us (6%)
  other arithmetic  6.12 us (4%)
  matrix products  5.77 us (4%)
    pallas_call x1, Pallas kernels, fused(): pl.pallas_call(functools.partial(backward_kernel, groups=groups, width=wi...  39.8 us
    ppermute x11, waiting for transfers between devices, swap(): return lax.ppermute(a, axis, [(i, i ^ mask) for i in range(size)])  26.8 us
    all_to_all x1, waiting for transfers between devices, local(): pair = lax.all_to_all(pair, CHIPS, split_axis=0, concat_axis=0, tiled=True)  22.6 us
    ppermute x11, starting transfers between devices, swap(): return lax.ppermute(a, axis, [(i, i ^ mask) for i in range(size)])  14.3 us
    all_to_all x1, starting transfers between devices, local(): pair = lax.all_to_all(pair, CHIPS, split_axis=0, concat_axis=0, tiled=True)  12.1 us
    all_to_all x1, starting transfers between devices, local(): lax.all_to_all(branch, CHIPS, split_axis=0, concat_axis=0, tiled=True)  7.77 us
    unnamed x14, local copies, waits for them, and re-layouts  3.88 us
    dot_general x1, matrix products, local(): jnp.einsum('bhr,kqr->bkhq', bias_table.reshape(heads // PACK, PACK, offse...  3.2 us
  transfers between devices with their start and end apart: 13, of which 8 were waited for; matrix products, arithmetic and copies ran while one was open for 8% of the time, Pallas kernels for 1%

profile of v1, /device:TPU:1, one launch (start us, length us, event | category | flops | bytes accessed | tf_op | source)
XLA Modules:
  0.0 146.3 jit_solution(15356624945076084750)
XLA Ops:
  0.6 3.1 %pad_maximum_fusion = bf16[64,32,512]{2,1,0:T(8,128)(2,1)} fusion(bf16[64,16,512]{2,1,0:T(8,128)(2,1)} %bitcast.35, bf16[64,16,512]{2,1,0:T(8,128)(2,1)} %bitcast.36), kind=kLoop, calls=%fused_computation.5 | loop fusion | flops 4194304 | bytes 4194304 | tf_op jit(solution)/shard_map/concatenate | solution.py:284
  3.7 12.1 %all-to-all-start = ((bf16[64,32,512]{2,1,0:T(8,128)(2,1)}), bf16[64,32,512]{2,1,0:T(8,128)(2,1)S(1)}, u32[]{:S(2)}, u32[]{:S(2)}) async-start(bf16[64,32,512]{2,1,0:T(8,128)(2,1)} %pad_maximum_fusion), calls=%async_computation | async-start | bytes 4194304 | tf_op jit(solution)/shard_map/all_to_all | solution.py:287
  16.0 3.2 %fusion.9 = f32[4,64,4,64]{3,2,0,1:T(4,128)S(1)} fusion(f32[4,4,225,1]{2,1,0,3:T(4,128)S(1)} %reshape.243, s32[64,64]{1,0:T(8,128)S(1)} %add_add_fusion), kind=kOutput, calls=%fused_computation.10 | convolution fusion | flops 177868800 | bytes 292928 | tf_op jit(solution)/shard_map/bhr,kqr->bkhq/dot_general | solution.py:278
  20.3 22.6 %all-to-all-done.pair_ref = bf16[64,32,512]{2,1,0:T(8,128)(2,1)S(1)} async-done(((bf16[64,32,512]{2,1,0:T(8,128)(2,1)}), bf16[64,32,512]{2,1,0:T(8,128)(2,1)S(1)}, u32[]{:S(2)}, u32[]{:S(2)}) %all-to-all-start) | async-done | bytes 2097184 | tf_op jit(solution)/shard_map/all_to_all | solution.py:287
  42.9 1.3 copy-done.3
  44.2 39.8 %fused_backward.1 = (bf16[64,16,512]{2,1,0:T(8,128)(2,1)}, f32[256,2048]{1,0:T(8,128)}, bf16[256,2048]{1,0:T(8,128)(2,1)}, f32[4,64,256]{2,1,0:T(8,128)}, f32[8,512]{1,0:T(8,128)}) custom-call(s32[1]{0:T(128)} %bitcast.core_ref, bf16[64,32,512]{2,1,0:T(8,128)(2,1)} %copy-done.3, bf16[512,1536]{1,0:T(8,128)(2,1)} %wqkv_ref.1, bf16[512,512]{1,0:T(8,128)(2,1)} %wout_ref.1, ...), custom_call_target="tpu_custom_call" | custom-call | tf_op jit(solution)/shard_map/fused_backward/pallas_call | solution.py:150
  84.0 2.8 %collective-permute-start = (bf16[256,2048]{1,0:T(8,128)(2,1)}, bf16[256,2048]{1,0:T(8,128)(2,1)S(1)}, u32[]{:S(2)}, u32[]{:S(2)}) collective-permute-start(bf16[256,2048]{1,0:T(8,128)(2,1)} %get-tuple-element.32), channel_id=1, source_target_pairs={{0,1},{1,0},{2,3},{3,2},{4,5},{5,4},{6,7},{7,6},{8,9},{9,8},{10,11... | collective-permute-start | bytes 3145736 | tf_op jit(solution)/shard_map/ppermute | solution.py:267
  86.8 7.8 %all-to-all-start.1 = ((bf16[64,16,512]{2,1,0:T(8,128)(2,1)}), bf16[64,16,512]{2,1,0:T(8,128)(2,1)}, u32[]{:S(2)}, u32[]{:S(2)}) async-start(bf16[64,16,512]{2,1,0:T(8,128)(2,1)} %get-tuple-element.28), calls=%async_computation.1 | async-start | bytes 2097152 | tf_op jit(solution)/shard_map/all_to_all | solution.py:291
  94.6 1.0 reshape.236
  95.6 2.6 %fusion.12 = f32[4,4,225]{2,1,0:T(4,128)S(1)} fusion(f32[4,64,4,64]{3,2,1,0:T(4,128)} %reshape.236, s32[64,64]{1,0:T(8,128)S(1)} %add_add_fusion), kind=kOutput, calls=%fused_computation.11 | convolution fusion | flops 177868800 | bytes 292928 | tf_op jit(solution)/shard_map/bkhq,kqr->bhr/dot_general | solution.py:296
  99.5 0.9 collective-permute-done.1.refs_3_
  100.4 1.1 sum_in_4_blocks.3
  102.3 1.0 collective-permute-start.2
  103.3 2.4 %collective-permute-start.3 = (bf16[80,2048]{1,0:T(8,128)(2,1)}, bf16[80,2048]{1,0:T(8,128)(2,1)S(1)}, u32[]{:S(2)}, u32[]{:S(2)}) collective-permute-start(bf16[80,2048]{1,0:T(8,128)(2,1)} %get-tuple-element.36), channel_id=1, source_target_pairs={{0,4},{2,6},{4,0},{6,2},{1,5},{3,7},{5,1},{7,3},{8,12},{10,14},{12... | collective-permute-start | bytes 983048 | tf_op jit(solution)/shard_map/ppermute | solution.py:267
  106.2 10.4 %collective-permute-done.2.refs_2_ = bf16[80,2048]{1,0:T(8,128)(2,1)S(1)} collective-permute-done((bf16[80,2048]{1,0:T(8,128)(2,1)}, bf16[80,2048]{1,0:T(8,128)(2,1)S(1)}, u32[]{:S(2)}, u32[]{:S(2)}) %collective-permute-start.2) | collective-permute-done | bytes 327712 | tf_op jit(solution)/shard_map/ppermute | solution.py:267
  116.6 8.5 %collective-permute-done.3.refs_3_ = bf16[80,2048]{1,0:T(8,128)(2,1)S(1)} collective-permute-done((bf16[80,2048]{1,0:T(8,128)(2,1)}, bf16[80,2048]{1,0:T(8,128)(2,1)S(1)}, u32[]{:S(2)}, u32[]{:S(2)}) %collective-permute-start.3) | collective-permute-done | bytes 327712 | tf_op jit(solution)/shard_map/ppermute | solution.py:267
  125.6 1.0 copy-done.2
  127.0 2.1 %collective-permute-start.6 = (bf16[32,2048]{1,0:T(8,128)(2,1)S(1)}, bf16[32,2048]{1,0:T(8,128)(2,1)S(1)}, u32[]{:S(2)}, u32[]{:S(2)}) collective-permute-start(bf16[32,2048]{1,0:T(8,128)(2,1)S(1)} %get-tuple-element.41), channel_id=1, source_target_pairs={{0,32},{16,48},{32,0},{48,16},{1,33},{17,49},{33,1},{49,17},{2,34}... | collective-permute-start | bytes 393224 | tf_op jit(solution)/shard_map/ppermute | solution.py:267
  129.1 1.7 %collective-permute-start.7 = (bf16[32,2048]{1,0:T(8,128)(2,1)S(1)}, bf16[32,2048]{1,0:T(8,128)(2,1)S(1)}, u32[]{:S(2)}, u32[]{:S(2)}) collective-permute-start(bf16[32,2048]{1,0:T(8,128)(2,1)S(1)} %get-tuple-element.42), channel_id=1, source_target_pairs={{0,48},{16,32},{32,16},{48,0},{1,49},{17,33},{33,17},{49,1},{2,50}... | collective-permute-start | bytes 393224 | tf_op jit(solution)/shard_map/ppermute | solution.py:267
  131.3 3.4 %collective-permute-done.6.refs_3_ = bf16[32,2048]{1,0:T(8,128)(2,1)S(1)} collective-permute-done((bf16[32,2048]{1,0:T(8,128)(2,1)S(1)}, bf16[32,2048]{1,0:T(8,128)(2,1)S(1)}, u32[]{:S(2)}, u32[]{:S(2)}) %collective-permute-start.6) | collective-permute-done | bytes 131104 | tf_op jit(solution)/shard_map/ppermute | solution.py:267
  134.7 2.5 %collective-permute-done.7.refs_4_ = bf16[32,2048]{1,0:T(8,128)(2,1)S(1)} collective-permute-done((bf16[32,2048]{1,0:T(8,128)(2,1)S(1)}, bf16[32,2048]{1,0:T(8,128)(2,1)S(1)}, u32[]{:S(2)}, u32[]{:S(2)}) %collective-permute-start.7) | collective-permute-done | bytes 131104 | tf_op jit(solution)/shard_map/ppermute | solution.py:267
  137.4 1.1 collective-permute-start.10
  139.4 1.4 collective-permute-start.9
  140.8 2.8 %fusion.6 = bf16[16,64,512]{2,1,0:T(8,128)(2,1)} fusion(bf16[16,64,512]{2,1,0:T(8,128)(2,1)} %param.8, bf16[16,64,512]{2,1,0:T(8,128)(2,1)} %bitcast.34), kind=kLoop, calls=%fused_computation.7 | loop fusion | flops 2097152 | bytes 3145728 | tf_op jit(solution)/shard_map/convert_element_type | solution.py:293
  (42 shorter events, 8.9 us)
Async XLA Ops:
  3.7 12.1 %copy-start.5 = (f32[16,225]{1,0:T(8,128)S(1)}, f32[16,225]{1,0:T(8,128)}, u32[]{:S(2)}) copy-start(f32[16,225]{1,0:T(8,128)} %param.11) | copy-start | bytes 43204
  3.7 39.2 %all-to-all-start = ((bf16[64,32,512]{2,1,0:T(8,128)(2,1)}), bf16[64,32,512]{2,1,0:T(8,128)(2,1)S(1)}, u32[]{:S(2)}, u32[]{:S(2)}) async-start(bf16[64,32,512]{2,1,0:T(8,128)(2,1)} %pad_maximum_fusion), calls=%async_computation | async-start | bytes 4194304 | tf_op jit(solution)/shard_map/all_to_all | solution.py:287
  42.9 1.3 copy-start.3
  84.0 10.6 %copy-start.4 = (f32[4,64,256]{2,1,0:T(8,128)S(1)}, f32[4,64,256]{2,1,0:T(8,128)}, u32[]{:S(2)}) copy-start(f32[4,64,256]{2,1,0:T(8,128)} %get-tuple-element.30) | copy-start | bytes 786436
  84.0 16.4 %collective-permute-start = (bf16[256,2048]{1,0:T(8,128)(2,1)}, bf16[256,2048]{1,0:T(8,128)(2,1)S(1)}, u32[]{:S(2)}, u32[]{:S(2)}) collective-permute-start(bf16[256,2048]{1,0:T(8,128)(2,1)} %get-tuple-element.32), channel_id=1, source_target_pairs={{0,1},{1,0},{2,3},{3,2},{4,5},{5,4},{6,7},{7,6},{8,9},{9,8},{10,11... | collective-permute-start | bytes 3145736 | tf_op jit(solution)/shard_map/ppermute | solution.py:267
  86.8 13.6 %copy-start = (f32[256,2048]{1,0:T(8,128)S(1)}, f32[256,2048]{1,0:T(8,128)}, u32[]{:S(2)}) copy-start(f32[256,2048]{1,0:T(8,128)} %get-tuple-element.29.refs_0_) | copy-start | bytes 6291460
  86.8 54.0 %all-to-all-start.1 = ((bf16[64,16,512]{2,1,0:T(8,128)(2,1)}), bf16[64,16,512]{2,1,0:T(8,128)(2,1)}, u32[]{:S(2)}, u32[]{:S(2)}) async-start(bf16[64,16,512]{2,1,0:T(8,128)(2,1)} %get-tuple-element.28), calls=%async_computation.1 | async-start | bytes 2097152 | tf_op jit(solution)/shard_map/all_to_all | solution.py:291
  99.1 1.3 collective-permute-start.1
  101.5 0.8 copy-start.1
  102.3 14.3 %collective-permute-start.2 = (bf16[80,2048]{1,0:T(8,128)(2,1)}, bf16[80,2048]{1,0:T(8,128)(2,1)S(1)}, u32[]{:S(2)}, u32[]{:S(2)}) collective-permute-start(bf16[80,2048]{1,0:T(8,128)(2,1)} %get-tuple-element.35), channel_id=1, source_target_pairs={{0,2},{2,0},{4,6},{6,4},{1,3},{3,1},{5,7},{7,5},{8,10},{10,8},{12,... | collective-permute-start | bytes 983048 | tf_op jit(solution)/shard_map/ppermute | solution.py:267
  103.3 21.8 %collective-permute-start.3 = (bf16[80,2048]{1,0:T(8,128)(2,1)}, bf16[80,2048]{1,0:T(8,128)(2,1)S(1)}, u32[]{:S(2)}, u32[]{:S(2)}) collective-permute-start(bf16[80,2048]{1,0:T(8,128)(2,1)} %get-tuple-element.36), channel_id=1, source_target_pairs={{0,4},{2,6},{4,0},{6,2},{1,5},{3,7},{5,1},{7,3},{8,12},{10,14},{12... | collective-permute-start | bytes 983048 | tf_op jit(solution)/shard_map/ppermute | solution.py:267
  105.7 19.9 %collective-permute-start.4 = (bf16[80,2048]{1,0:T(8,128)(2,1)}, bf16[80,2048]{1,0:T(8,128)(2,1)S(1)}, u32[]{:S(2)}, u32[]{:S(2)}) collective-permute-start(bf16[80,2048]{1,0:T(8,128)(2,1)} %get-tuple-element.37), channel_id=1, source_target_pairs={{0,6},{2,4},{4,2},{6,0},{1,7},{3,5},{5,3},{7,1},{8,14},{10,12},{12... | collective-permute-start | bytes 983048 | tf_op jit(solution)/shard_map/ppermute | solution.py:267
  125.6 1.0 copy-start.2
  126.9 4.5 %collective-permute-start.5 = (bf16[32,2048]{1,0:T(8,128)(2,1)S(1)}, bf16[32,2048]{1,0:T(8,128)(2,1)S(1)}, u32[]{:S(2)}, u32[]{:S(2)}) collective-permute-start(bf16[32,2048]{1,0:T(8,128)(2,1)S(1)} %get-tuple-element.40), channel_id=1, source_target_pairs={{0,16},{16,0},{32,48},{48,32},{1,17},{17,1},{33,49},{49,33},{2,18}... | collective-permute-start | bytes 393224 | tf_op jit(solution)/shard_map/ppermute | solution.py:267
  127.0 7.7 %collective-permute-start.6 = (bf16[32,2048]{1,0:T(8,128)(2,1)S(1)}, bf16[32,2048]{1,0:T(8,128)(2,1)S(1)}, u32[]{:S(2)}, u32[]{:S(2)}) collective-permute-start(bf16[32,2048]{1,0:T(8,128)(2,1)S(1)} %get-tuple-element.41), channel_id=1, source_target_pairs={{0,32},{16,48},{32,0},{48,16},{1,33},{17,49},{33,1},{49,17},{2,34}... | collective-permute-start | bytes 393224 | tf_op jit(solution)/shard_map/ppermute | solution.py:267
  129.1 8.1 %collective-permute-start.7 = (bf16[32,2048]{1,0:T(8,128)(2,1)S(1)}, bf16[32,2048]{1,0:T(8,128)(2,1)S(1)}, u32[]{:S(2)}, u32[]{:S(2)}) collective-permute-start(bf16[32,2048]{1,0:T(8,128)(2,1)S(1)} %get-tuple-element.42), channel_id=1, source_target_pairs={{0,48},{16,32},{32,16},{48,0},{1,49},{17,33},{33,17},{49,1},{2,50}... | collective-permute-start | bytes 393224 | tf_op jit(solution)/shard_map/ppermute | solution.py:267
  137.4 6.2 %collective-permute-start.10 = (bf16[16,2048]{1,0:T(8,128)(2,1)S(1)}, bf16[16,2048]{1,0:T(8,128)(2,1)S(1)}, u32[]{:S(2)}, u32[]{:S(2)}) collective-permute-start(bf16[16,2048]{1,0:T(8,128)(2,1)S(1)} %get-tuple-element.47), channel_id=1, source_target_pairs={{0,72},{8,64},{64,8},{72,0},{1,73},{9,65},{65,9},{73,1},{2,74},{10... | collective-permute-start | bytes 196616 | tf_op jit(solution)/shard_map/ppermute | solution.py:267
  138.5 5.1 %collective-permute-start.8 = (bf16[16,2048]{1,0:T(8,128)(2,1)S(1)}, bf16[16,2048]{1,0:T(8,128)(2,1)S(1)}, u32[]{:S(2)}, u32[]{:S(2)}) collective-permute-start(bf16[16,2048]{1,0:T(8,128)(2,1)S(1)} %get-tuple-element.45), channel_id=1, source_target_pairs={{0,8},{8,0},{64,72},{72,64},{1,9},{9,1},{65,73},{73,65},{2,10},{10... | collective-permute-start | bytes 196616 | tf_op jit(solution)/shard_map/ppermute | solution.py:267
  139.4 4.2 %collective-permute-start.9 = (bf16[16,2048]{1,0:T(8,128)(2,1)S(1)}, bf16[16,2048]{1,0:T(8,128)(2,1)S(1)}, u32[]{:S(2)}, u32[]{:S(2)}) collective-permute-start(bf16[16,2048]{1,0:T(8,128)(2,1)S(1)} %get-tuple-element.46), channel_id=1, source_target_pairs={{0,64},{8,72},{64,0},{72,8},{1,65},{9,73},{65,1},{73,9},{2,66},{10... | collective-permute-start | bytes 196616 | tf_op jit(solution)/shard_map/ppermute | solution.py:267

commit v2 on v0

v2 whole, which is shorter than its diff:
```python
import functools
import jax
import jax.numpy as jnp
from jax import lax
from jax.experimental import pallas as pl
from jax.experimental.pallas import tpu as pltpu
from jax.sharding import Mesh, PartitionSpec as P

GRID = 8
EPSILON = 1e-05
MEMBERS = GRID * GRID
PACK = 4
PARTS = 2


def dot(a, b, ca, cb):
    return lax.dot_general(a, b, (((ca,), (cb,)), ((), ())), preferred_element_type=jnp.float32)


def backward_kernel(*refs, groups, width, head_dim, last):
    pair_ref, wqkv_ref, wout_ref, bias_ref, gain_ref, shift_ref = refs[:6]
    if last:
        core_ref, before_ref, gbias_before, gvec_before = refs[6:10]
        branch_ref, keep_ref, send_ref, gbias_ref, gvec_ref = refs[10:15]
        proj, gatt, normed, dyp, hat, istd, gproj, att, dyf, before, before_sem = refs[15:]
        fetch = pltpu.make_async_copy(before_ref, before, before_sem)
        fetch.start()
    else:
        branch_ref, sums_ref, gbias_ref, gvec_ref = refs[6:10]
        proj, gatt, normed, dyp, hat, istd, gproj, att, dyf = refs[10:]
    rows = groups * MEMBERS
    chunk = 256
    per = chunk // MEMBERS
    bf16, f32 = jnp.bfloat16, jnp.float32
    scale = head_dim ** (-0.5)

    mem = chunk // groups

    lanes = width // 128

    def put(ref, at, value):
        for b in range(lanes):
            ref[b, at, :] = value[:, b * 128 : (b + 1) * 128]

    def take(ref, at):
        return jnp.concatenate([ref[b, at, :] for b in range(lanes)], axis=1)

    def hat_step(c, carry):
        here = pl.ds(pl.multiple_of(c * chunk, chunk), chunk)
        pair = pair_ref[pl.ds(pl.multiple_of(c * mem, mem), mem)].astype(f32)
        x = pair[:, 0].reshape(chunk, width)
        centred = x - jnp.mean(x, axis=-1, keepdims=True)
        inv = lax.rsqrt(jnp.mean(centred * centred, axis=-1, keepdims=True) + EPSILON)
        put(hat, here, centred * inv)
        istd[here, :] = jnp.broadcast_to(inv, (chunk, 128))
        put(dyf, here, pair[:, 1].reshape(chunk, width))
        return carry

    lax.fori_loop(0, rows // chunk, hat_step, 0)

    def by_group(ref, c):
        return jnp.concatenate(
            [take(ref, pl.ds(c * per + g, MEMBERS, stride=groups)) for g in range(per)], axis=0
        )

    def norm_step(c, carry):
        here = pl.ds(pl.multiple_of(c * chunk, chunk), chunk)
        nb = (by_group(hat, c) * gain_ref[...] + shift_ref[...]).astype(bf16)
        dy = by_group(dyf, c).astype(bf16)
        dyp[here, :] = dy
        normed[here, :] = nb
        proj[here, :] = dot(nb, wqkv_ref[...], 1, 0).astype(bf16)
        gatt[here, :] = dot(dy, wout_ref[...], 1, 1).astype(bf16)
        return carry

    lax.fori_loop(0, rows // chunk, norm_step, 0)

    gbias_ref[...] = gbias_before[...] if last else jnp.zeros_like(gbias_ref)
    lane = lax.broadcasted_iota(jnp.int32, (MEMBERS, 128), 1) // head_dim

    def spread(a):
        zero = jnp.zeros_like(a)
        return jnp.concatenate([jnp.where(lane == h, a, zero) for h in range(PACK)], axis=0)

    def gather(a):
        out = a[:MEMBERS]
        for h in range(1, PACK):
            out = jnp.where(lane == h, a[h * MEMBERS : (h + 1) * MEMBERS], out)
        return out

    blocks = range(width // 128)

    def group_step(g, carry):
        here = pl.ds(pl.multiple_of(g * MEMBERS, MEMBERS), MEMBERS)
        cols = [slice(b * 128, (b + 1) * 128) for b in blocks]
        kcols = [slice(width + b * 128, width + (b + 1) * 128) for b in blocks]
        vcols = [slice(2 * width + b * 128, 2 * width + (b + 1) * 128) for b in blocks]
        ks = [proj[here, c] for c in kcols]
        vs = [proj[here, c] for c in vcols]
        none = jnp.zeros_like(ks[0])
        ws = [jnp.concatenate([spread(proj[here, c]), spread(gatt[here, c])], axis=1) for c in cols]
        both = [
            dot(
                jnp.concatenate(
                    [jnp.concatenate([k, none], axis=1), jnp.concatenate([none, v], axis=1)], axis=0
                ),
                w, 1, 1,
            )
            for k, v, w in zip(ks, vs, ws)
        ]
        pds = []
        for b in blocks:
            scores = both[b][:MEMBERS] * scale + bias_ref[b]
            gp = both[b][MEMBERS:]
            e = jnp.exp(scores - jnp.max(scores, axis=0, keepdims=True))
            p = e * (1.0 / jnp.sum(e, axis=0, keepdims=True))
            gs = p * (gp - jnp.sum(gp * p, axis=0, keepdims=True))
            gbias_ref[b] += gs
            pds.append(jnp.concatenate([p.astype(bf16), (gs * scale).astype(bf16)], axis=0))
        keyed = [dot(pd, w, 1, 0) for pd, w in zip(pds, ws)]
        queried = [
            dot(
                pd,
                jnp.concatenate(
                    [jnp.concatenate([v, none], axis=1), jnp.concatenate([none, k], axis=1)], axis=0
                ),
                0, 0,
            )
            for k, v, pd in zip(ks, vs, pds)
        ]
        for b in blocks:
            att[here, cols[b]] = gather(queried[b][:, :128]).astype(bf16)
            gproj[here, cols[b]] = gather(queried[b][:, 128:]).astype(bf16)
            gproj[here, kcols[b]] = keyed[b][MEMBERS:, :128].astype(bf16)
            gproj[here, vcols[b]] = keyed[b][:MEMBERS, 128:].astype(bf16)
        return carry

    lax.fori_loop(0, groups, group_step, 0)

    def gn_step(c, carry):
        here = pl.ds(pl.multiple_of(c * chunk, chunk), chunk)
        gn = dot(gproj[here, :], wqkv_ref[...], 1, 1)
        for g in range(per):
            put(dyf, pl.ds(c * per + g, MEMBERS, stride=groups), gn[g * MEMBERS : (g + 1) * MEMBERS])
        return carry

    lax.fori_loop(0, rows // chunk, gn_step, 0)

    def back_step(c, carry):
        gg, gsh = carry
        here = pl.ds(pl.multiple_of(c * chunk, chunk), chunk)
        gn = take(dyf, here)
        normalized = take(hat, here)
        prod = gn * normalized
        gg = gg + jnp.sum(prod.reshape(chunk // 8, 8, width), axis=0)
        gsh = gsh + jnp.sum(gn.reshape(chunk // 8, 8, width), axis=0)
        gh = gn * gain_ref[...]
        m1 = jnp.mean(gh, axis=-1, keepdims=True)
        m2 = jnp.mean(prod * gain_ref[...], axis=-1, keepdims=True)
        inv = istd[here, :][:, :1]
        branch = (inv * (gh - m1 - normalized * m2)).astype(bf16)
        branch_ref[pl.ds(pl.multiple_of(c * mem, mem), mem)] = branch.reshape(mem, groups, width)
        return gg, gsh

    zero = jnp.zeros((8, width), f32)
    gg, gsh = lax.fori_loop(0, rows // chunk, back_step, (zero, zero))
    gvec = jnp.concatenate([jnp.sum(gg, axis=0, keepdims=True), jnp.sum(gsh, axis=0, keepdims=True)], axis=0)
    gvec_ref[...] = gvec + gvec_before[...] if last else gvec

    gw = dot(normed[...], gproj[...], 0, 0)
    go = dot(att[...], dyp[...], 0, 0)
    if not last:
        sums_ref[:, : 3 * width] = gw
        sums_ref[:, 3 * width :] = go
        return
    fetch.wait()
    half = 2 * width
    low = gw[:, :half] + before[:, :half]
    high = jnp.concatenate([gw[:, half:], go], axis=1) + before[:, half:]

    @pl.when(core_ref[0] == 0)
    def _():
        keep_ref[...] = low
        send_ref[...] = high.astype(bf16)

    @pl.when(core_ref[0] != 0)
    def _():
        keep_ref[...] = high
        send_ref[...] = low.astype(bf16)


VMEM = pl.BlockSpec(memory_space=pltpu.VMEM)
SMEM = pl.BlockSpec(memory_space=pltpu.SMEM)
ANY = pl.BlockSpec(memory_space=pl.ANY)


def backward(pair, wqkv, wout, bias, gain, shift, head_dim, core=None, before=None):
    members, _, groups, width = pair.shape
    rows = groups * MEMBERS
    last = before is not None
    f32, bf16 = jnp.float32, jnp.bfloat16
    if last:
        sums = (jax.ShapeDtypeStruct((width, 2 * width), f32), jax.ShapeDtypeStruct((width, 2 * width), bf16))
        more = (core.reshape(1),) + before
    else:
        sums = (jax.ShapeDtypeStruct((width, 4 * width), f32),)
        more = ()
    scratch = [
        pltpu.VMEM((rows, 3 * width), bf16),
        pltpu.VMEM((rows, width), bf16),
        pltpu.VMEM((rows, width), bf16),
        pltpu.VMEM((rows, width), bf16),
        pltpu.VMEM((width // 128, rows, 128), f32),
        pltpu.VMEM((rows, 128), f32),
        pltpu.VMEM((rows, 3 * width), bf16),
        pltpu.VMEM((rows, width), bf16),
        pltpu.VMEM((width // 128, rows, 128), f32),
    ]
    if last:
        scratch += [pltpu.VMEM((width, 4 * width), f32), pltpu.SemaphoreType.DMA]
    dense = 2 * rows * width * 10 * width
    return pl.pallas_call(
        functools.partial(backward_kernel, groups=groups, width=width, head_dim=head_dim, last=last),
        out_shape=(jax.ShapeDtypeStruct((members, groups, width), bf16),)
        + sums
        + (jax.ShapeDtypeStruct(bias.shape, f32), jax.ShapeDtypeStruct((2, width), f32)),
        in_specs=[VMEM] * 6 + ([SMEM, ANY, VMEM, VMEM] if last else []),
        out_specs=(VMEM,) * (5 if last else 4),
        scratch_shapes=scratch,
        compiler_params=pltpu.CompilerParams(vmem_limit_bytes=40 * 1024 * 1024),
        cost_estimate=pl.CostEstimate(flops=4 * dense, bytes_accessed=12 << 20, transcendentals=0),
        name="last_backward" if last else "first_backward",
    )(pair, wqkv, wout, bias, gain.reshape(1, width), shift.reshape(1, width), *more)


def pair_kernel(x_ref, dy_ref, *refs):
    outs, sems = refs[:-1], refs[-1]
    copies = []
    for c, out in enumerate(outs):
        for t, source in enumerate((x_ref, dy_ref)):
            copies.append(pltpu.make_async_copy(source.at[c], out.at[:, t], sems.at[c, t]))
    for copy in copies:
        copy.start()
    for copy in copies:
        copy.wait()


def pairs(x, dy):
    parts, chips, groups, width = x.shape
    return pl.pallas_call(
        pair_kernel,
        out_shape=(jax.ShapeDtypeStruct((chips, 2, groups, width), x.dtype),) * parts,
        in_specs=[ANY, ANY],
        out_specs=(ANY,) * parts,
        scratch_shapes=[pltpu.SemaphoreType.DMA((parts, 2))],
        name="pairs",
    )(x, dy)


def outgoing_kernel(first_ref, second_ref, keep_ref, recv_ref, out_ref):
    chips, _, groups, width = out_ref.shape
    out_ref[:, 0] = first_ref[...]
    out_ref[:, 1] = second_ref[...]
    for part in range(2):
        cols = slice(part * width, (part + 1) * width)
        total = (keep_ref[:, cols] + recv_ref[:, cols].astype(jnp.float32)).astype(jnp.bfloat16)
        out_ref[:, 2 + part] = total.reshape(chips, groups, width)


def outgoing(first, second, keep, recv):
    chips, groups, width = first.shape
    return pl.pallas_call(
        outgoing_kernel,
        out_shape=jax.ShapeDtypeStruct((chips, 4, groups, width), first.dtype),
        in_specs=[VMEM] * 4,
        out_specs=VMEM,
        compiler_params=pltpu.CompilerParams(vmem_limit_bytes=24 * 1024 * 1024),
        name="outgoing",
    )(first, second, keep, recv)


def final_kernel(got_ref, dy_ref, grad_ref, weights_ref, *, factor):
    f32 = jnp.float32
    chips, _, groups, width = got_ref.shape
    for part in range(2):
        grad_ref[part] = (dy_ref[part].astype(f32) + got_ref[:, part].astype(f32)).astype(grad_ref.dtype)
        total = got_ref[0, 2 + part].astype(f32)
        for chip in range(1, chips):
            total = total + got_ref[chip, 2 + part].astype(f32)
        weights_ref[:, part * width : (part + 1) * width] = total * factor


def final(got, dy, factor):
    chips, _, groups, width = got.shape
    return pl.pallas_call(
        functools.partial(final_kernel, factor=factor),
        out_shape=(
            jax.ShapeDtypeStruct(dy.shape, dy.dtype),
            jax.ShapeDtypeStruct((groups, 2 * width), jnp.float32),
        ),
        in_specs=[VMEM] * 2,
        out_specs=(VMEM,) * 2,
        compiler_params=pltpu.CompilerParams(vmem_limit_bytes=24 * 1024 * 1024),
        name="final",
    )(got, dy)


AXES = ("x_lo", "y", "x_hi", "z", "core")
CHIPS = AXES[:4]


def relative_onehot(members):
    span = 2 * GRID - 1
    second = jnp.arange(members, dtype=jnp.int32)[:, None]
    first = jnp.arange(members, dtype=jnp.int32)[None, :]
    row_delta = first // GRID - second // GRID + GRID - 1
    col_delta = first % GRID - second % GRID + GRID - 1
    rel_index = row_delta * span + col_delta
    offsets = jnp.arange(span * span, dtype=jnp.int32)
    return (rel_index[:, :, None] == offsets).astype(jnp.float32)


def swap(a, axis, mask):
    size = lax.axis_size(axis)
    return lax.ppermute(a, axis, [(i, i ^ mask) for i in range(size)])


def sum_everywhere(a):
    a = a + swap(a, "core", 1)
    for axis in ("z", "y", ("x_lo", "x_hi")):
        parts = [swap(a, axis, mask) for mask in (1, 2, 3)]
        a = (a + parts[0]) + (parts[1] + parts[2])
    return a


def local(block_input, cotangent, qkv_weight, out_weight, bias_table, norm_gain, norm_shift):
    tile_h, tile_w, width = block_input.shape
    heads, offsets = bias_table.shape
    chips = lax.axis_size(CHIPS)
    devices = chips * lax.axis_size("core")
    owned = tile_h * tile_w // chips // PARTS
    core = lax.axis_index("core")
    onehot = relative_onehot(MEMBERS)
    bias = jnp.einsum(
        "bhr,kqr->bkhq",
        bias_table.reshape(heads // PACK, PACK, offsets),
        onehot,
        precision=lax.Precision.HIGHEST,
    ).reshape(heads // PACK, MEMBERS, PACK * MEMBERS)
    shape = (PARTS, chips, owned, width)
    sent = pairs(block_input.reshape(shape), cotangent.reshape(shape))
    got = [lax.all_to_all(part, CHIPS, split_axis=0, concat_axis=0, tiled=True) for part in sent]
    common = (qkv_weight, out_weight, bias, norm_gain, norm_shift, width // heads)
    first, *sums = backward(got[0], *common)
    second, keep, send, gbias, gvec = backward(got[1], *common, core, tuple(sums))
    back = outgoing(first, second, keep, swap(send, "core", 1))
    back = lax.all_to_all(back, CHIPS, split_axis=0, concat_axis=0, tiled=True)
    factor = float(tile_h * tile_w * devices) ** (-0.5)
    table = jnp.einsum(
        "bkhq,kqr->bhr",
        gbias.reshape(heads // PACK, MEMBERS, PACK, MEMBERS),
        onehot,
        precision=lax.Precision.HIGHEST,
    )
    small = jnp.concatenate((table.reshape(-1), gvec.reshape(-1)))
    small = jnp.pad(small, (0, -small.size % 128)).reshape(-1, 128)
    small = sum_everywhere(small).reshape(-1) * factor
    cut = heads * offsets

    grad_input, part = final(back, cotangent.reshape(shape), factor)
    share = part.shape[0] // 2
    mine = lax.dynamic_slice_in_dim(part, core * share, share, 0)
    other = swap(lax.dynamic_slice_in_dim(part, (1 - core) * share, share, 0), "core", 1)
    low = jnp.where(core == 0, mine, other)
    high = jnp.where(core == 0, other, mine)
    grad_qkv = jnp.concatenate((low, high[:, :width]), axis=1)
    grad_out = high[:, width:]
    return (
        grad_input.reshape(tile_h, tile_w, width),
        grad_qkv,
        grad_out,
        small[:cut].reshape(heads, offsets),
        small[cut : cut + width],
        small[cut + width : cut + 2 * width],
    )


def solution(mesh):
    fine = Mesh(mesh.devices.reshape(2, 4, 2, 4, 2), AXES)
    tile = P(("x_lo", "y"), ("x_hi", "z", "core"), None)
    return jax.shard_map(
        local,
        mesh=fine,
        in_specs=(tile, tile, P(), P(), P(), P(), P()),
        out_specs=(tile, P(AXES, None), P(AXES, None), P(), P(), P()),
        check_vma=False,
    )
```

time: 147 us -> 201 us (1.37)
  Pallas kernels: 38.7 us -> 90.1 us
  starting transfers between devices: 42.8 us -> 56.3 us
  waiting for transfers between devices: 45.3 us -> 33 us
  local copies, waits for them, and re-layouts: 5.53 us -> 13.2 us
  other arithmetic: 8.47 us -> 0.96 us
    pallas_call x1 -> x5, Pallas kernels: 38.7 us -> 90.1 us  [the longest x1 64.7 us: pairs(): pl.pallas_call(pair_kernel, out_shape=(jax.ShapeDtypeStruct((chips, 2, gr...]
    ppermute x12, starting transfers between devices: 17.3 us -> 28 us  [swap(): return lax.ppermute(a, axis, [(i, i ^ mask) for i in range(size)])]
    unnamed x10 -> x25, local copies, waits for them, and re-layouts: 2.11 us -> 9.69 us
    all_to_all x3, waiting for transfers between devices: 22.6 us -> 15.8 us  [the longest x2 15.8 us: local(): lax.all_to_all(part, CHIPS, split_axis=0, concat_axis=0, tiled=True)]
    ppermute x12, waiting for transfers between devices: 22.7 us -> 17.2 us  [swap(): return lax.ppermute(a, axis, [(i, i ^ mask) for i in range(size)])]
    concatenate x1 -> x0, other arithmetic: 3.1 us -> none  [local(): jnp.concatenate((block_input.reshape(chips, owned, width), cotangent.resh...]
    reshape x1 -> x0, other arithmetic: 2.93 us -> none  [local(): weights = weights.reshape(chips, width // chips, 2 * width)]
    all_to_all x3, starting transfers between devices: 25.5 us -> 28.4 us  [the longest x2 18.3 us: local(): lax.all_to_all(part, CHIPS, split_axis=0, concat_axis=0, tiled=True)]
  transfers between devices with their start and end apart: 15 -> 15, of which waited for: 9 -> 9; matrix products, arithmetic and copies ran while one was open for 7% -> 5% of each run, Pallas kernels for 0% -> 5%
where the time goes in v2:
time: 201 us; the launch traced here: 200 us
  Pallas kernels  90.1 us (45%)
  starting transfers between devices  56.3 us (28%)
  waiting for transfers between devices  33 us (16%)
  local copies, waits for them, and re-layouts  13.2 us (7%)
  matrix products  5.77 us (3%)
    pallas_call x1, Pallas kernels, pairs(): pl.pallas_call(pair_kernel, out_shape=(jax.ShapeDtypeStruct((chips, 2, gr...  64.7 us
    ppermute x12, starting transfers between devices, swap(): return lax.ppermute(a, axis, [(i, i ^ mask) for i in range(size)])  28 us
    pallas_call x2, Pallas kernels, backward(): pl.pallas_call(functools.partial(backward_kernel, groups=groups, width=wi...  22.6 us
    all_to_all x2, starting transfers between devices, local(): lax.all_to_all(part, CHIPS, split_axis=0, concat_axis=0, tiled=True)  18.3 us
    ppermute x12, waiting for transfers between devices, swap(): return lax.ppermute(a, axis, [(i, i ^ mask) for i in range(size)])  17.2 us
    all_to_all x2, waiting for transfers between devices, local(): lax.all_to_all(part, CHIPS, split_axis=0, concat_axis=0, tiled=True)  15.8 us
    all_to_all x1, starting transfers between devices, local(): back = lax.all_to_all(back, CHIPS, split_axis=0, concat_axis=0, tiled=True)  10 us
    unnamed x25, local copies, waits for them, and re-layouts  9.69 us
  transfers between devices with their start and end apart: 15, of which 9 were waited for; matrix products, arithmetic and copies ran while one was open for 5% of the time, Pallas kernels for 5%

profile of v2, /device:TPU:1, one launch (start us, length us, event | category | flops | bytes accessed | tf_op | source)
XLA Modules:
  0.0 200.2 jit_solution(3034171509325776665)
XLA Ops:
  0.7 64.7 %pairs.1 = (bf16[64,2,8,512]{3,2,1,0:T(8,128)(2,1)}, bf16[64,2,8,512]{3,2,1,0:T(8,128)(2,1)}) custom-call(bf16[2,64,8,512]{3,2,1,0:T(8,128)(2,1)} %bitcast.43, bf16[2,64,8,512]{3,2,1,0:T(8,128)(2,1)} %bitcast.36), custom_call_target="tpu_custom_call" | custom-call | tf_op jit(solution)/shard_map/pairs/pallas_call | solution.py:250
  65.3 12.0 %all-to-all-start = ((bf16[64,2,8,512]{3,2,1,0:T(8,128)(2,1)}), bf16[64,2,8,512]{3,2,1,0:T(8,128)(2,1)S(1)}, u32[]{:S(2)}, u32[]{:S(2)}) async-start(bf16[64,2,8,512]{3,2,1,0:T(8,128)(2,1)} %get-tuple-element.19), calls=%async_computation | async-start | bytes 2097152 | tf_op jit(solution)/shard_map/all_to_all | solution.py:352
  77.5 15.8 %all-to-all-done.refs_0_ = bf16[64,2,8,512]{3,2,1,0:T(8,128)(2,1)S(1)} async-done(((bf16[64,2,8,512]{3,2,1,0:T(8,128)(2,1)}), bf16[64,2,8,512]{3,2,1,0:T(8,128)(2,1)S(1)}, u32[]{:S(2)}, u32[]{:S(2)}) %all-to-all-start) | async-done | bytes 1048608 | tf_op jit(solution)/shard_map/all_to_all | solution.py:352
  93.3 6.3 %all-to-all-start.1 = ((bf16[64,2,8,512]{3,2,1,0:T(8,128)(2,1)}), bf16[64,2,8,512]{3,2,1,0:T(8,128)(2,1)S(1)}, u32[]{:S(2)}, u32[]{:S(2)}) async-start(bf16[64,2,8,512]{3,2,1,0:T(8,128)(2,1)} %get-tuple-element.21), calls=%async_computation.1 | async-start | bytes 2097152 | tf_op jit(solution)/shard_map/all_to_all | solution.py:352
  99.6 3.2 %fusion.8 = f32[4,64,4,64]{3,2,0,1:T(4,128)S(1)} fusion(f32[4,4,225,1]{2,1,0,3:T(4,128)S(1)} %reshape.233, s32[64,64]{1,0:T(8,128)S(1)} %add_add_fusion), kind=kOutput, calls=%fused_computation.7 | convolution fusion | flops 177868800 | bytes 292928 | tf_op jit(solution)/shard_map/bhr,kqr->bkhq/dot_general | solution.py:344
  103.3 1.4 copy-done.1
  104.7 10.8 %first_backward.1 = (bf16[64,8,512]{2,1,0:T(8,128)(2,1)S(1)}, f32[512,2048]{1,0:T(8,128)S(1)}, f32[4,64,256]{2,1,0:T(8,128)S(1)}, f32[2,512]{1,0:T(2,128)S(1)}) custom-call(bf16[64,2,8,512]{3,2,1,0:T(8,128)(2,1)S(1)} %all-to-all-done.refs_0_, bf16[512,1536]{1,0:T(8,128)(2,1)S(1)} %copy-done.1, bf16[512,512]{1,0:T(8,128)(2,1)S(1)} %copy-done.3, ...), custom_call_target="tpu_custom_call" | custom-call | flops 10737418240 | bytes 12582912 | tf_op jit(solution)/shard_map/first_backward/pallas_call | solution.py:222
  115.5 2.0 copy-done.7
  118.2 1.4 copy-done.2
  120.7 2.2 %copy-done.8 = f32[512,2048]{1,0:T(8,128)S(1)} copy-done((f32[512,2048]{1,0:T(8,128)S(1)}, f32[512,2048]{1,0:T(8,128)}, u32[]{:S(2)}) %copy-start.8) | copy-done | bytes 4194328
  123.8 11.7 %last_backward.1 = (bf16[64,8,512]{2,1,0:T(8,128)(2,1)S(1)}, f32[512,1024]{1,0:T(8,128)S(1)}, bf16[512,1024]{1,0:T(8,128)(2,1)S(1)}, f32[4,64,256]{2,1,0:T(8,128)S(1)}, f32[2,512]{1,0:T(2,128)S(1)}) custom-call(bf16[64,2,8,512]{3,2,1,0:T(8,128)(2,1)S(1)} %all-to-all-done.1.refs_0_, bf16[512,1536]{1,0:T(8,128)(2,1)S(1)} %copy-done.2, ...), custom_call_target="tpu_custom_call" | custom-call | flops 10737418240 | bytes 12582912 | tf_op jit(solution)/shard_map/last_backward/pallas_call | solution.py:222
  135.6 2.3 %collective-permute-start = (bf16[512,1024]{1,0:T(8,128)(2,1)S(1)}, bf16[512,1024]{1,0:T(8,128)(2,1)S(1)}, u32[]{:S(2)}, u32[]{:S(2)}) collective-permute-start(bf16[512,1024]{1,0:T(8,128)(2,1)S(1)} %get-tuple-element.27), channel_id=1, source_target_pairs={{0,1},{1,0},{2,3},{3,2},{4,5},{5,4},{6,7},{7,6},{8,9},{9,8},{10,11... | collective-permute-start | bytes 3145736 | tf_op jit(solution)/shard_map/ppermute | solution.py:325
  137.9 2.3 %collective-permute-done.recv_ref = bf16[512,1024]{1,0:T(8,128)(2,1)S(1)} collective-permute-done((bf16[512,1024]{1,0:T(8,128)(2,1)S(1)}, bf16[512,1024]{1,0:T(8,128)(2,1)S(1)}, u32[]{:S(2)}, u32[]{:S(2)}) %collective-permute-start) | collective-permute-done | bytes 1048608 | tf_op jit(solution)/shard_map/ppermute | solution.py:325
  140.2 1.6 outgoing.1
  141.8 10.0 %all-to-all-start.2 = ((bf16[64,4,8,512]{3,2,1,0:T(8,128)(2,1)}), bf16[64,4,8,512]{3,2,1,0:T(8,128)(2,1)S(1)}, u32[]{:S(2)}, u32[]{:S(2)}) async-start(bf16[64,4,8,512]{3,2,1,0:T(8,128)(2,1)} %outgoing.1), calls=%async_computation.2 | async-start | bytes 4194304 | tf_op jit(solution)/shard_map/all_to_all | solution.py:357
  152.9 2.6 %fusion.11 = f32[4,4,225]{2,1,0:T(4,128)S(1)} fusion(f32[4,64,4,64]{3,2,1,0:T(4,128)} %reshape.227, s32[64,64]{1,0:T(8,128)S(1)} %add_add_fusion), kind=kOutput, calls=%fused_computation.8 | convolution fusion | flops 177868800 | bytes 292928 | tf_op jit(solution)/shard_map/bkhq,kqr->bhr/dot_general | solution.py:359
  157.2 2.8 %collective-permute-start.4 = (f32[37,128]{1,0:T(8,128)S(1)}, f32[37,128]{1,0:T(8,128)S(1)}, u32[]{:S(2)}, u32[]{:S(2)}) collective-permute-start(f32[37,128]{1,0:T(8,128)S(1)} %fusion.15), channel_id=1, source_target_pairs={{0,4},{2,6},{4,0},{6,2},{1,5},{3,7},{5,1},{7,3},{8,12},{10,14},{12... | collective-permute-start | bytes 56840 | tf_op jit(solution)/shard_map/ppermute | solution.py:325
  160.9 6.1 %collective-permute-done.4 = f32[37,128]{1,0:T(8,128)S(1)} collective-permute-done((f32[37,128]{1,0:T(8,128)S(1)}, f32[37,128]{1,0:T(8,128)S(1)}, u32[]{:S(2)}, u32[]{:S(2)}) %collective-permute-start.4) | collective-permute-done | bytes 18976 | tf_op jit(solution)/shard_map/ppermute | solution.py:325
  169.8 12.5 %collective-permute-start.8 = (f32[37,128]{1,0:T(8,128)S(1)}, f32[37,128]{1,0:T(8,128)S(1)}, u32[]{:S(2)}, u32[]{:S(2)}) collective-permute-start(f32[37,128]{1,0:T(8,128)S(1)} %add_add_fusion.2), channel_id=1, source_target_pairs={{0,48},{16,32},{32,16},{48,0},{1,49},{17,33},{33,17},{49,1},{2,50}... | collective-permute-start | bytes 56840 | tf_op jit(solution)/shard_map/ppermute | solution.py:325
  183.5 1.8 collective-permute-done.6
  186.3 1.9 collective-permute-start.11
  188.6 1.6 collective-permute-done.11
  190.2 2.2 %collective-permute-done.9 = f32[37,128]{1,0:T(8,128)S(1)} collective-permute-done((f32[37,128]{1,0:T(8,128)S(1)}, f32[37,128]{1,0:T(8,128)S(1)}, u32[]{:S(2)}, u32[]{:S(2)}) %collective-permute-start.9) | collective-permute-done | bytes 18976 | tf_op jit(solution)/shard_map/ppermute | solution.py:325
  193.6 4.0 %collective-permute-start.1 = (f32[4,1024]{1,0:T(4,128)S(1)}, f32[4,1024]{1,0:T(4,128)S(1)}, u32[]{:S(2)}, u32[]{:S(2)}) collective-permute-start(f32[4,1024]{1,0:T(4,128)S(1)} %constant_dynamic-slice_fusion), channel_id=1, source_target_pairs={{0,1},{1,0},{2,3},{3,2},{4,5},{5,4},{6,7},{7,6},{8,9},{9,8},{10,11... | collective-permute-start | bytes 49160 | tf_op jit(solution)/shard_map/ppermute | solution.py:325
  (57 shorter events, 16.2 us)
Async XLA Ops:
  0.6 76.7 %copy-start.11 = (f32[16,225]{1,0:T(8,128)S(1)}, f32[16,225]{1,0:T(8,128)}, u32[]{:S(2)}) copy-start(f32[16,225]{1,0:T(8,128)} %param.11) | copy-start | bytes 43204
  0.6 102.6 %copy-start.3 = (bf16[512,512]{1,0:T(8,128)(2,1)S(1)}, bf16[512,512]{1,0:T(8,128)(2,1)}, u32[]{:S(2)}) copy-start(bf16[512,512]{1,0:T(8,128)(2,1)} %refs_2_.3) | copy-start | bytes 1572868
  0.7 102.6 %copy-start.5 = (f32[512]{0:T(512)S(1)}, f32[512]{0:T(512)}, u32[]{:S(2)}) copy-start(f32[512]{0:T(512)} %param.12) | copy-start | bytes 6148
  0.7 102.6 %copy-start.6 = (f32[512]{0:T(512)S(1)}, f32[512]{0:T(512)}, u32[]{:S(2)}) copy-start(f32[512]{0:T(512)} %param.13) | copy-start | bytes 6148
  65.3 27.9 %all-to-all-start = ((bf16[64,2,8,512]{3,2,1,0:T(8,128)(2,1)}), bf16[64,2,8,512]{3,2,1,0:T(8,128)(2,1)S(1)}, u32[]{:S(2)}, u32[]{:S(2)}) async-start(bf16[64,2,8,512]{3,2,1,0:T(8,128)(2,1)} %get-tuple-element.19), calls=%async_computation | async-start | bytes 2097152 | tf_op jit(solution)/shard_map/all_to_all | solution.py:352
  93.3 24.9 %all-to-all-start.1 = ((bf16[64,2,8,512]{3,2,1,0:T(8,128)(2,1)}), bf16[64,2,8,512]{3,2,1,0:T(8,128)(2,1)S(1)}, u32[]{:S(2)}, u32[]{:S(2)}) async-start(bf16[64,2,8,512]{3,2,1,0:T(8,128)(2,1)} %get-tuple-element.21), calls=%async_computation.1 | async-start | bytes 2097152 | tf_op jit(solution)/shard_map/all_to_all | solution.py:352
  103.3 1.4 copy-start.1
  115.5 2.0 copy-start.7
  118.2 1.4 copy-start.2
  120.7 2.2 %copy-start.8 = (f32[512,2048]{1,0:T(8,128)S(1)}, f32[512,2048]{1,0:T(8,128)}, u32[]{:S(2)}) copy-start(f32[512,2048]{1,0:T(8,128)} %copy-done.7) | copy-start | bytes 12582916
  135.6 4.6 %collective-permute-start = (bf16[512,1024]{1,0:T(8,128)(2,1)S(1)}, bf16[512,1024]{1,0:T(8,128)(2,1)S(1)}, u32[]{:S(2)}, u32[]{:S(2)}) collective-permute-start(bf16[512,1024]{1,0:T(8,128)(2,1)S(1)} %get-tuple-element.27), channel_id=1, source_target_pairs={{0,1},{1,0},{2,3},{3,2},{4,5},{5,4},{6,7},{7,6},{8,9},{9,8},{10,11... | collective-permute-start | bytes 3145736 | tf_op jit(solution)/shard_map/ppermute | solution.py:325
  141.8 50.6 %copy-start = (bf16[16,64,512]{2,1,0:T(8,128)(2,1)S(1)}, bf16[16,64,512]{2,1,0:T(8,128)(2,1)}, u32[]{:S(2)}) copy-start(bf16[16,64,512]{2,1,0:T(8,128)(2,1)} %param.8) | copy-start | bytes 3145732
  141.8 50.6 %all-to-all-start.2 = ((bf16[64,4,8,512]{3,2,1,0:T(8,128)(2,1)}), bf16[64,4,8,512]{3,2,1,0:T(8,128)(2,1)S(1)}, u32[]{:S(2)}, u32[]{:S(2)}) async-start(bf16[64,4,8,512]{3,2,1,0:T(8,128)(2,1)} %outgoing.1), calls=%async_computation.2 | async-start | bytes 4194304 | tf_op jit(solution)/shard_map/all_to_all | solution.py:357
  155.6 1.5 collective-permute-start.2
  157.2 9.8 %collective-permute-start.4 = (f32[37,128]{1,0:T(8,128)S(1)}, f32[37,128]{1,0:T(8,128)S(1)}, u32[]{:S(2)}, u32[]{:S(2)}) collective-permute-start(f32[37,128]{1,0:T(8,128)S(1)} %fusion.15), channel_id=1, source_target_pairs={{0,4},{2,6},{4,0},{6,2},{1,5},{3,7},{5,1},{7,3},{8,12},{10,14},{12... | collective-permute-start | bytes 56840 | tf_op jit(solution)/shard_map/ppermute | solution.py:325
  160.0 7.0 %collective-permute-start.5 = (f32[37,128]{1,0:T(8,128)S(1)}, f32[37,128]{1,0:T(8,128)S(1)}, u32[]{:S(2)}, u32[]{:S(2)}) collective-permute-start(f32[37,128]{1,0:T(8,128)S(1)} %fusion.15), channel_id=1, source_target_pairs={{0,6},{2,4},{4,2},{6,0},{1,7},{3,5},{5,3},{7,1},{8,14},{10,12},{12... | collective-permute-start | bytes 56840 | tf_op jit(solution)/shard_map/ppermute | solution.py:325
  160.9 7.4 %collective-permute-start.3 = (f32[37,128]{1,0:T(8,128)S(1)}, f32[37,128]{1,0:T(8,128)S(1)}, u32[]{:S(2)}, u32[]{:S(2)}) collective-permute-start(f32[37,128]{1,0:T(8,128)S(1)} %fusion.15), channel_id=1, source_target_pairs={{0,2},{2,0},{4,6},{6,4},{1,3},{3,1},{5,7},{7,5},{8,10},{10,8},{12,... | collective-permute-start | bytes 56840 | tf_op jit(solution)/shard_map/ppermute | solution.py:325
  168.4 13.9 %collective-permute-start.7 = (f32[37,128]{1,0:T(8,128)S(1)}, f32[37,128]{1,0:T(8,128)S(1)}, u32[]{:S(2)}, u32[]{:S(2)}) collective-permute-start(f32[37,128]{1,0:T(8,128)S(1)} %add_add_fusion.2), channel_id=1, source_target_pairs={{0,32},{16,48},{32,0},{48,16},{1,33},{17,49},{33,1},{49,17},{2,34}... | collective-permute-start | bytes 56840 | tf_op jit(solution)/shard_map/ppermute | solution.py:325
  169.8 13.7 %collective-permute-start.8 = (f32[37,128]{1,0:T(8,128)S(1)}, f32[37,128]{1,0:T(8,128)S(1)}, u32[]{:S(2)}, u32[]{:S(2)}) collective-permute-start(f32[37,128]{1,0:T(8,128)S(1)} %add_add_fusion.2), channel_id=1, source_target_pairs={{0,48},{16,32},{32,16},{48,0},{1,49},{17,33},{33,17},{49,1},{2,50}... | collective-permute-start | bytes 56840 | tf_op jit(solution)/shard_map/ppermute | solution.py:325
  182.4 2.9 %collective-permute-start.6 = (f32[37,128]{1,0:T(8,128)S(1)}, f32[37,128]{1,0:T(8,128)S(1)}, u32[]{:S(2)}, u32[]{:S(2)}) collective-permute-start(f32[37,128]{1,0:T(8,128)S(1)} %add_add_fusion.2), channel_id=1, source_target_pairs={{0,16},{16,0},{32,48},{48,32},{1,17},{17,1},{33,49},{49,33},{2,18}... | collective-permute-start | bytes 56840 | tf_op jit(solution)/shard_map/ppermute | solution.py:325
  185.3 3.3 %collective-permute-start.10 = (f32[37,128]{1,0:T(8,128)S(1)}, f32[37,128]{1,0:T(8,128)S(1)}, u32[]{:S(2)}, u32[]{:S(2)}) collective-permute-start(f32[37,128]{1,0:T(8,128)S(1)} %add_add_fusion.1), channel_id=1, source_target_pairs={{0,64},{8,72},{64,0},{72,8},{1,65},{9,73},{65,1},{73,9},{2,66},{10... | collective-permute-start | bytes 56840 | tf_op jit(solution)/shard_map/ppermute | solution.py:325
  186.3 3.8 %collective-permute-start.11 = (f32[37,128]{1,0:T(8,128)S(1)}, f32[37,128]{1,0:T(8,128)S(1)}, u32[]{:S(2)}, u32[]{:S(2)}) collective-permute-start(f32[37,128]{1,0:T(8,128)S(1)} %add_add_fusion.1), channel_id=1, source_target_pairs={{0,72},{8,64},{64,8},{72,0},{1,73},{9,65},{65,9},{73,1},{2,74},{10... | collective-permute-start | bytes 56840 | tf_op jit(solution)/shard_map/ppermute | solution.py:325
  188.2 4.1 %collective-permute-start.9 = (f32[37,128]{1,0:T(8,128)S(1)}, f32[37,128]{1,0:T(8,128)S(1)}, u32[]{:S(2)}, u32[]{:S(2)}) collective-permute-start(f32[37,128]{1,0:T(8,128)S(1)} %add_add_fusion.1), channel_id=1, source_target_pairs={{0,8},{8,0},{64,72},{72,64},{1,9},{9,1},{65,73},{73,65},{2,10},{10... | collective-permute-start | bytes 56840 | tf_op jit(solution)/shard_map/ppermute | solution.py:325
  193.6 5.4 %collective-permute-start.1 = (f32[4,1024]{1,0:T(4,128)S(1)}, f32[4,1024]{1,0:T(4,128)S(1)}, u32[]{:S(2)}, u32[]{:S(2)}) collective-permute-start(f32[4,1024]{1,0:T(4,128)S(1)} %constant_dynamic-slice_fusion), channel_id=1, source_target_pairs={{0,1},{1,0},{2,3},{3,2},{4,5},{5,4},{6,7},{7,6},{8,9},{9,8},{10,11... | collective-permute-start | bytes 49160 | tf_op jit(solution)/shard_map/ppermute | solution.py:325
  (3 other events, 2.7 us)

commit v3 on v2

--- a/solution.py
+++ b/solution.py
@@ -20,16 +20,15 @@
 def backward_kernel(*refs, groups, width, head_dim, last):
     pair_ref, wqkv_ref, wout_ref, bias_ref, gain_ref, shift_ref = refs[:6]
     if last:
-        core_ref, before_ref, gbias_before, gvec_before = refs[6:10]
-        branch_ref, keep_ref, send_ref, gbias_ref, gvec_ref = refs[10:15]
-        proj, gatt, normed, dyp, hat, istd, gproj, att, dyf, before, before_sem = refs[15:]
-        fetch = pltpu.make_async_copy(before_ref, before, before_sem)
-        fetch.start()
+        gbias_before, gvec_before = refs[6:8]
+        branch_ref, small_ref, normed, gproj, att, dyp = refs[8:14]
+        proj, gatt, hat, istd, dyf, gbias_ref = refs[14:]
     else:
         branch_ref, sums_ref, gbias_ref, gvec_ref = refs[6:10]
-        proj, gatt, normed, dyp, hat, istd, gproj, att, dyf = refs[10:]
+        normed, gproj, att, dyp, proj, gatt, hat, istd, dyf = refs[10:]
     rows = groups * MEMBERS
     chunk = 256
+    heads = width // head_dim
     per = chunk // MEMBERS
     bf16, f32 = jnp.bfloat16, jnp.float32
     scale = head_dim ** (-0.5)
@@ -165,95 +164,140 @@
     zero = jnp.zeros((8, width), f32)
     gg, gsh = lax.fori_loop(0, rows // chunk, back_step, (zero, zero))
     gvec = jnp.concatenate([jnp.sum(gg, axis=0, keepdims=True), jnp.sum(gsh, axis=0, keepdims=True)], axis=0)
-    gvec_ref[...] = gvec + gvec_before[...] if last else gvec
-
-    gw = dot(normed[...], gproj[...], 0, 0)
-    go = dot(att[...], dyp[...], 0, 0)
-    if not last:
-        sums_ref[:, : 3 * width] = gw
-        sums_ref[:, 3 * width :] = go
-        return
-    fetch.wait()
-    half = 2 * width
-    low = gw[:, :half] + before[:, :half]
-    high = jnp.concatenate([gw[:, half:], go], axis=1) + before[:, half:]
-
-    @pl.when(core_ref[0] == 0)
-    def _():
-        keep_ref[...] = low
-        send_ref[...] = high.astype(bf16)
-
-    @pl.when(core_ref[0] != 0)
-    def _():
-        keep_ref[...] = high
-        send_ref[...] = low.astype(bf16)
+    if last:
+        small_ref[...] = jnp.zeros_like(small_ref)
+        small_ref[:heads, :] = offset_sums(gbias_ref)
+        gvec = gvec + gvec_before[...]
+        for i in range(2):
+            for part in range(width // 256):
+                row = heads + i * (width // 256) + part
+                small_ref[row : row + 1, :] = gvec[i : i + 1, part * 256 : (part + 1) * 256]
+    else:
+        gvec_ref[...] = gvec
+        sums_ref[:, : 3 * width] = dot(normed[...], gproj[...], 0, 0)
+        sums_ref[:, 3 * width :] = dot(att[...], dyp[...], 0, 0)
+
+
+def offset_sums(gbias_ref):
+    f32, bf16 = jnp.float32, jnp.bfloat16
+    blocks, members, lanes = gbias_ref.shape
+    i = lax.broadcasted_iota(jnp.int32, (lanes, 2 * lanes), 0)
+    o = lax.broadcasted_iota(jnp.int32, (lanes, 2 * lanes), 1)
+    query = i % members
+    place = (i // members) * 128 + query // GRID * 16 + query % GRID
+    wide = (o == place).astype(f32).astype(bf16)
+    frames = []
+    for b in range(blocks):
+        value = gbias_ref[b]
+        high = value.astype(bf16)
+        rest = value - high.astype(f32)
+        low = rest.astype(bf16)
+        lowest = (rest - low.astype(f32)).astype(bf16)
+        spread = dot(jnp.concatenate([high, low, lowest], axis=0), wide, 1, 0)
+        spread = spread[:members] + (spread[members : 2 * members] + spread[2 * members :])
+        frames += [spread[None, :, h * 128 : (h + 1) * 128] for h in range(PACK)]
+    frame = jnp.concatenate(frames, axis=0)
+    heads = frame.shape[0]
+    frame = jnp.concatenate([frame, jnp.zeros_like(frame)], axis=2).reshape(heads * members, 256)
+    column = GRID - 1 - lax.broadcasted_iota(jnp.int32, frame.shape, 0) % GRID
+    for bit in (1, 2, 4):
+        frame = jnp.where((column & bit) != 0, pltpu.roll(frame, bit, 1), frame)
+    frame = jnp.sum(frame.reshape(heads * GRID, GRID, 256), axis=1)
+    row = GRID - 1 - lax.broadcasted_iota(jnp.int32, frame.shape, 0) % GRID
+    for bit in (1, 2, 4):
+        frame = jnp.where((row & bit) != 0, pltpu.roll(frame, 16 * bit, 1), frame)
+    return jnp.sum(frame.reshape(heads, GRID, 256), axis=1)
 
 
 VMEM = pl.BlockSpec(memory_space=pltpu.VMEM)
 SMEM = pl.BlockSpec(memory_space=pltpu.SMEM)
-ANY = pl.BlockSpec(memory_space=pl.ANY)
-
-
-def backward(pair, wqkv, wout, bias, gain, shift, head_dim, core=None, before=None):
+
+
+def backward(pair, wqkv, wout, bias, gain, shift, head_dim, before=None):
     members, _, groups, width = pair.shape
     rows = groups * MEMBERS
     last = before is not None
     f32, bf16 = jnp.float32, jnp.bfloat16
-    if last:
-        sums = (jax.ShapeDtypeStruct((width, 2 * width), f32), jax.ShapeDtypeStruct((width, 2 * width), bf16))
-        more = (core.reshape(1),) + before
-    else:
-        sums = (jax.ShapeDtypeStruct((width, 4 * width), f32),)
-        more = ()
+    shape = jax.ShapeDtypeStruct
+    kept = [(rows, width), (rows, 3 * width), (rows, width), (rows, width)]
     scratch = [
         pltpu.VMEM((rows, 3 * width), bf16),
         pltpu.VMEM((rows, width), bf16),
-        pltpu.VMEM((rows, width), bf16),
-        pltpu.VMEM((rows, width), bf16),
         pltpu.VMEM((width // 128, rows, 128), f32),
         pltpu.VMEM((rows, 128), f32),
-        pltpu.VMEM((rows, 3 * width), bf16),
-        pltpu.VMEM((rows, width), bf16),
         pltpu.VMEM((width // 128, rows, 128), f32),
     ]
+    outs = [shape((members, groups, width), bf16)]
     if last:
-        scratch += [pltpu.VMEM((width, 4 * width), f32), pltpu.SemaphoreType.DMA]
-    dense = 2 * rows * width * 10 * width
+        outs += [shape((24, 256), f32)] + [shape(k, bf16) for k in kept]
+        scratch += [pltpu.VMEM(bias.shape, f32)]
+    else:
+        outs += [shape((width, 4 * width), f32), shape(bias.shape, f32), shape((2, width), f32)]
+        scratch = [pltpu.VMEM(k, bf16) for k in kept] + scratch
     return pl.pallas_call(
         functools.partial(backward_kernel, groups=groups, width=width, head_dim=head_dim, last=last),
-        out_shape=(jax.ShapeDtypeStruct((members, groups, width), bf16),)
-        + sums
-        + (jax.ShapeDtypeStruct(bias.shape, f32), jax.ShapeDtypeStruct((2, width), f32)),
-        in_specs=[VMEM] * 6 + ([SMEM, ANY, VMEM, VMEM] if last else []),
-        out_specs=(VMEM,) * (5 if last else 4),
+        out_shape=tuple(outs),
+        in_specs=[VMEM] * (8 if last else 6),
+        out_specs=(VMEM,) * len(outs),
         scratch_shapes=scratch,
-        compiler_params=pltpu.CompilerParams(vmem_limit_bytes=40 * 1024 * 1024),
-        cost_estimate=pl.CostEstimate(flops=4 * dense, bytes_accessed=12 << 20, transcendentals=0),
+        compiler_params=pltpu.CompilerParams(vmem_limit_bytes=24 * 1024 * 1024),
+        cost_estimate=pl.CostEstimate(flops=10_000_000_000, bytes_accessed=8 << 20, transcendentals=0),
         name="last_backward" if last else "first_backward",
-    )(pair, wqkv, wout, bias, gain.reshape(1, width), shift.reshape(1, width), *more)
-
-
-def pair_kernel(x_ref, dy_ref, *refs):
-    outs, sems = refs[:-1], refs[-1]
-    copies = []
-    for c, out in enumerate(outs):
-        for t, source in enumerate((x_ref, dy_ref)):
-            copies.append(pltpu.make_async_copy(source.at[c], out.at[:, t], sems.at[c, t]))
-    for copy in copies:
-        copy.start()
-    for copy in copies:
-        copy.wait()
-
-
-def pairs(x, dy):
-    parts, chips, groups, width = x.shape
+    )(pair, wqkv, wout, bias, gain.reshape(1, width), shift.reshape(1, width), *(before or ()))
+
+
+def weights_kernel(core_ref, normed, gproj, att, dyp, before, keep_ref, send_ref):
+    width = normed.shape[1]
+    half = 2 * width
+    gw = dot(normed[...], gproj[...], 0, 0)
+    go = dot(att[...], dyp[...], 0, 0)
+    low = gw[:, :half] + before[:, :half]
+    high = jnp.concatenate([gw[:, half:], go], axis=1) + before[:, half:]
+
+    @pl.when(core_ref[0] == 0)
+    def _():
+        keep_ref[...] = low
+        send_ref[...] = high.astype(send_ref.dtype)
+
+    @pl.when(core_ref[0] != 0)
+    def _():
+        keep_ref[...] = high
+        send_ref[...] = low.astype(send_ref.dtype)
+
+
+def weight_halves(core, normed, gproj, att, dyp, before):
+    width = normed.shape[1]
+    return pl.pallas_call(
+        weights_kernel,
+        out_shape=(
+            jax.ShapeDtypeStruct((width, 2 * width), jnp.float32),
+            jax.ShapeDtypeStruct((width, 2 * width), jnp.bfloat16),
+        ),
+        in_specs=[SMEM] + [VMEM] * 5,
+        out_specs=(VMEM,) * 2,
+        compiler_params=pltpu.CompilerParams(vmem_limit_bytes=24 * 1024 * 1024),
+        cost_estimate=pl.CostEstimate(flops=3_000_000_000, bytes_accessed=4 << 20, transcendentals=0),
+        name="weight_halves",
+    )(core.reshape(1), normed, gproj, att, dyp, before)
+
+
+def pair_kernel(x_ref, dy_ref, out_ref):
+    out_ref[:, 0] = x_ref[0]
+    out_ref[:, 1] = dy_ref[0]
+
+
+def pair_of(x, dy, part):
+    _, chips, groups, width = x.shape
+    steps = 4
+    source = pl.BlockSpec((1, chips // steps, groups, width), lambda i: (part, i, 0, 0))
     return pl.pallas_call(
         pair_kernel,
-        out_shape=(jax.ShapeDtypeStruct((chips, 2, groups, width), x.dtype),) * parts,
-        in_specs=[ANY, ANY],
-        out_specs=(ANY,) * parts,
-        scratch_shapes=[pltpu.SemaphoreType.DMA((parts, 2))],
-        name="pairs",
+        grid=(steps,),
+        out_shape=jax.ShapeDtypeStruct((chips, 2, groups, width), x.dtype),
+        in_specs=[source, source],
+        out_specs=pl.BlockSpec((chips // steps, 2, groups, width), lambda i: (i, 0, 0, 0)),
+        cost_estimate=pl.CostEstimate(flops=0, bytes_accessed=2 << 20, transcendentals=0),
+        name="pair",
     )(x, dy)
 
 
@@ -325,12 +369,9 @@
     return lax.ppermute(a, axis, [(i, i ^ mask) for i in range(size)])
 
 
-def sum_everywhere(a):
-    a = a + swap(a, "core", 1)
-    for axis in ("z", "y", ("x_lo", "x_hi")):
-        parts = [swap(a, axis, mask) for mask in (1, 2, 3)]
-        a = (a + parts[0]) + (parts[1] + parts[2])
-    return a
+def sum_over(a, axis):
+    parts = [swap(a, axis, mask) for mask in (1, 2, 3)]
+    return (a + parts[0]) + (parts[1] + parts[2])
 
 
 def local(block_input, cotangent, qkv_weight, out_weight, bias_table, norm_gain, norm_shift):
@@ -348,25 +389,25 @@
         precision=lax.Precision.HIGHEST,
     ).reshape(heads // PACK, MEMBERS, PACK * MEMBERS)
     shape = (PARTS, chips, owned, width)
-    sent = pairs(block_input.reshape(shape), cotangent.reshape(shape))
+    x, dy = block_input.reshape(shape), cotangent.reshape(shape)
+    sent = [pair_of(x, dy, part) for part in range(PARTS)]
+    sent[1], bias = lax.optimization_barrier((sent[1], bias))
     got = [lax.all_to_all(part, CHIPS, split_axis=0, concat_axis=0, tiled=True) for part in sent]
     common = (qkv_weight, out_weight, bias, norm_gain, norm_shift, width // heads)
-    first, *sums = backward(got[0], *common)
-    second, keep, send, gbias, gvec = backward(got[1], *common, core, tuple(sums))
+    first, sums, gbias, gvec = backward(got[0], *common)
+    second, small, *operands = backward(got[1], *common, (gbias, gvec))
+    keep, send = weight_halves(core, *operands, sums)
+    small = small + swap(small, "core", 1)
+    small = sum_over(small, "z")
     back = outgoing(first, second, keep, swap(send, "core", 1))
+    back, small = lax.optimization_barrier((back, small))
     back = lax.all_to_all(back, CHIPS, split_axis=0, concat_axis=0, tiled=True)
+    for axis in ("y", ("x_lo", "x_hi")):
+        small = sum_over(small, axis)
     factor = float(tile_h * tile_w * devices) ** (-0.5)
-    table = jnp.einsum(
-        "bkhq,kqr->bhr",
-        gbias.reshape(heads // PACK, MEMBERS, PACK, MEMBERS),
-        onehot,
-        precision=lax.Precision.HIGHEST,
-    )
-    small = jnp.concatenate((table.reshape(-1), gvec.reshape(-1)))
-    small = jnp.pad(small, (0, -small.size % 128)).reshape(-1, 128)
-    small = sum_everywhere(small).reshape(-1) * factor
-    cut = heads * offsets
-
+    small = small * factor
+    table = small[:heads].reshape(heads, 16, 16)[:, : 2 * GRID - 1, : 2 * GRID - 1]
+    vectors = small[heads : heads + 4].reshape(2, width)
     grad_input, part = final(back, cotangent.reshape(shape), factor)
     share = part.shape[0] // 2
     mine = lax.dynamic_slice_in_dim(part, core * share, share, 0)
@@ -379,9 +420,9 @@
         grad_input.reshape(tile_h, tile_w, width),
         grad_qkv,
         grad_out,
-        small[:cut].reshape(heads, offsets),
-        small[cut : cut + width],
-        small[cut + width : cut + 2 * width],
+        table.reshape(heads, offsets),
+        vectors[0],
+        vectors[1],
     )
 
 

time: 201 us -> 133 us (0.66)
  Pallas kernels: 90.1 us -> 33.1 us
  local copies, waits for them, and re-layouts: 13.2 us -> 9.43 us
  matrix products: 5.77 us -> 3.2 us
  waiting for transfers between devices: 33 us -> 30.8 us
  starting transfers between devices: 56.3 us -> 54.1 us
    pallas_call x1 -> x3, Pallas kernels: 64.7 us -> 8.38 us  [the longest x2 6.85 us: pair_of(): pl.pallas_call(pair_kernel, grid=(steps,), out_shape=jax.ShapeDtypeStruct...]
    all_to_all x2, waiting for transfers between devices: 15.8 us -> 8.76 us  [local(): lax.all_to_all(part, CHIPS, split_axis=0, concat_axis=0, tiled=True)]
    ppermute x12, waiting for transfers between devices: 17.2 us -> 22 us  [swap(): return lax.ppermute(a, axis, [(i, i ^ mask) for i in range(size)])]
    dot_general x1 -> x0, matrix products: 2.57 us -> none  [local(): jnp.einsum('bkhq,kqr->bhr', gbias.reshape(heads // PACK, MEMBERS, PACK, M...]
    unnamed x25, local copies, waits for them, and re-layouts: 9.69 us -> 7.61 us
  transfers between devices with their start and end apart: 15 -> 15, of which waited for: 9 -> 10; matrix products, arithmetic and copies ran while one was open for 5% -> 4% of each run, Pallas kernels for 5% -> 11%
where the time goes in v3:
time: 133 us; the launch traced here: 132 us
  starting transfers between devices  54.1 us (41%)
  Pallas kernels  33.1 us (25%)
  waiting for transfers between devices  30.8 us (23%)
  local copies, waits for them, and re-layouts  9.43 us (7%)
  matrix products  3.2 us (2%)
    ppermute x12, starting transfers between devices, swap(): return lax.ppermute(a, axis, [(i, i ^ mask) for i in range(size)])  27.2 us
    ppermute x12, waiting for transfers between devices, swap(): return lax.ppermute(a, axis, [(i, i ^ mask) for i in range(size)])  22 us
    pallas_call x2, Pallas kernels, backward(): pl.pallas_call(functools.partial(backward_kernel, groups=groups, width=wi...  21.9 us
    all_to_all x2, starting transfers between devices, local(): lax.all_to_all(part, CHIPS, split_axis=0, concat_axis=0, tiled=True)  18.4 us
    all_to_all x2, waiting for transfers between devices, local(): lax.all_to_all(part, CHIPS, split_axis=0, concat_axis=0, tiled=True)  8.76 us
    all_to_all x1, starting transfers between devices, local(): back = lax.all_to_all(back, CHIPS, split_axis=0, concat_axis=0, tiled=True)  8.42 us
    unnamed x25, local copies, waits for them, and re-layouts  7.61 us
    pallas_call x2, Pallas kernels, pair_of(): pl.pallas_call(pair_kernel, grid=(steps,), out_shape=jax.ShapeDtypeStruct...  6.85 us
  transfers between devices with their start and end apart: 15, of which 10 were waited for; matrix products, arithmetic and copies ran while one was open for 4% of the time, Pallas kernels for 11%

profile of v3, /device:TPU:1, one launch (start us, length us, event | category | flops | bytes accessed | tf_op | source)
XLA Modules:
  0.0 132.2 jit_solution(16575337635112588821)
XLA Ops:
  0.6 3.4 %pair.2 = bf16[64,2,8,512]{3,2,1,0:T(8,128)(2,1)} custom-call(bf16[2,64,8,512]{3,2,1,0:T(8,128)(2,1)} %bitcast.32, bf16[2,64,8,512]{3,2,1,0:T(8,128)(2,1)} %bitcast.25), custom_call_target="tpu_custom_call" | custom-call | bytes 2097152 | tf_op jit(solution)/shard_map/pair/pallas_call | solution.py:293
  4.0 12.1 %all-to-all-start = ((bf16[64,2,8,512]{3,2,1,0:T(8,128)(2,1)}), bf16[64,2,8,512]{3,2,1,0:T(8,128)(2,1)S(1)}, u32[]{:S(2)}, u32[]{:S(2)}) async-start(bf16[64,2,8,512]{3,2,1,0:T(8,128)(2,1)} %pair.2), calls=%async_computation | async-start | bytes 2097152 | tf_op jit(solution)/shard_map/all_to_all | solution.py:395
  16.2 3.4 %pair.3 = bf16[64,2,8,512]{3,2,1,0:T(8,128)(2,1)} custom-call(bf16[2,64,8,512]{3,2,1,0:T(8,128)(2,1)} %bitcast.33, bf16[2,64,8,512]{3,2,1,0:T(8,128)(2,1)} %bitcast.26), custom_call_target="tpu_custom_call" | custom-call | bytes 2097152 | tf_op jit(solution)/shard_map/pair/pallas_call | solution.py:293
  19.7 3.2 %fusion.4 = f32[4,64,4,64]{3,2,0,1:T(4,128)S(1)} fusion(f32[4,4,225,1]{2,1,0,3:T(4,128)S(1)} %reshape.223, s32[64,64]{1,0:T(8,128)S(1)} %add_add_fusion), kind=kOutput, calls=%fused_computation.4 | convolution fusion | flops 177868800 | bytes 292928 | tf_op jit(solution)/shard_map/bhr,kqr->bkhq/dot_general | solution.py:385
  23.3 8.8 %all-to-all-done.refs_0_ = bf16[64,2,8,512]{3,2,1,0:T(8,128)(2,1)S(1)} async-done(((bf16[64,2,8,512]{3,2,1,0:T(8,128)(2,1)}), bf16[64,2,8,512]{3,2,1,0:T(8,128)(2,1)S(1)}, u32[]{:S(2)}, u32[]{:S(2)}) %all-to-all-start) | async-done | bytes 1048608 | tf_op jit(solution)/shard_map/all_to_all | solution.py:395
  32.1 6.3 %all-to-all-start.1 = ((bf16[64,2,8,512]{3,2,1,0:T(8,128)(2,1)}), bf16[64,2,8,512]{3,2,1,0:T(8,128)(2,1)S(1)}, u32[]{:S(2)}, u32[]{:S(2)}) async-start(bf16[64,2,8,512]{3,2,1,0:T(8,128)(2,1)} %pair.3), calls=%async_computation.1 | async-start | bytes 2097152 | tf_op jit(solution)/shard_map/all_to_all | solution.py:395
  39.9 10.8 %first_backward.1 = (bf16[64,8,512]{2,1,0:T(8,128)(2,1)S(1)}, f32[512,2048]{1,0:T(8,128)S(1)}, f32[4,64,256]{2,1,0:T(8,128)S(1)}, f32[2,512]{1,0:T(2,128)S(1)}) custom-call(bf16[64,2,8,512]{3,2,1,0:T(8,128)(2,1)S(1)} %all-to-all-done.refs_0_, bf16[512,1536]{1,0:T(8,128)(2,1)S(1)} %copy-done.1, bf16[512,512]{1,0:T(8,128)(2,1)S(1)} %copy-done.3, ...), custom_call_target="tpu_custom_call" | custom-call | flops 10000000000 | bytes 8388608 | tf_op jit(solution)/shard_map/first_backward/pallas_call | solution.py:237
  50.7 2.0 %copy-done.6 = f32[512,2048]{1,0:T(8,128)} copy-done((f32[512,2048]{1,0:T(8,128)}, f32[512,2048]{1,0:T(8,128)S(1)}, u32[]{:S(2)}) %copy-start.6) | copy-done | bytes 4194328
  55.8 11.1 %last_backward.1 = (bf16[64,8,512]{2,1,0:T(8,128)(2,1)S(1)}, f32[24,256]{1,0:T(8,128)S(1)}, bf16[512,512]{1,0:T(8,128)(2,1)S(1)}, bf16[512,1536]{1,0:T(8,128)(2,...) custom-call(bf16[64,2,8,512]{3,2,1,0:T(8,128)(2,1)S(1)} %all-to-all-done.1.refs_0_, ...), custom_call_target="tpu_custom_call" | custom-call | flops 10000000000 | bytes 8388608 | tf_op jit(solution)/shard_map/last_backward/pallas_call | solution.py:237
  66.8 1.5 %weight_halves.1 = (f32[512,1024]{1,0:T(8,128)S(1)}, bf16[512,1024]{1,0:T(8,128)(2,1)S(1)}) custom-call(s32[1]{0:T(128)} %bitcast.7.core_ref, bf16[512,512]{1,0:T(8,128)(2,1)S(1)} %get-tuple-element.30.normed, bf16[512,1536]{1,0:T(8,128)(2,1)S(1)} %get-tuple-element.31.gproj, bf16[512,512]{1,0:T(8,128)(2,1)S(1)} %get-tuple-element.32.att, ...), custom_call_target="tpu_custom_call" | custom-call | flops 3000000000 | bytes 4194304 | tf_op jit(solution)/shard_map/weight_halves/pallas_call | solution.py:270
  68.4 4.2 %collective-permute-start = (bf16[512,1024]{1,0:T(8,128)(2,1)S(1)}, bf16[512,1024]{1,0:T(8,128)(2,1)S(1)}, u32[]{:S(2)}, u32[]{:S(2)}) collective-permute-start(bf16[512,1024]{1,0:T(8,128)(2,1)S(1)} %get-tuple-element.36), channel_id=1, source_target_pairs={{0,1},{1,0},{2,3},{3,2},{4,5},{5,4},{6,7},{7,6},{8,9},{9,8},{10,11... | collective-permute-start | bytes 3145736 | tf_op jit(solution)/shard_map/ppermute | solution.py:369
  72.9 2.0 %collective-permute-done.1 = f32[24,256]{1,0:T(8,128)S(1)} collective-permute-done((f32[24,256]{1,0:T(8,128)S(1)}, f32[24,256]{1,0:T(8,128)S(1)}, u32[]{:S(2)}, u32[]{:S(2)}) %collective-permute-start.1) | collective-permute-done | bytes 24608 | tf_op jit(solution)/shard_map/ppermute | solution.py:369
  76.1 1.5 %collective-permute-start.4 = (f32[24,256]{1,0:T(8,128)S(1)}, f32[24,256]{1,0:T(8,128)S(1)}, u32[]{:S(2)}, u32[]{:S(2)}) collective-permute-start(f32[24,256]{1,0:T(8,128)S(1)} %add.95), channel_id=1, source_target_pairs={{0,6},{2,4},{4,2},{6,0},{1,7},{3,5},{5,3},{7,1},{8,14},{10,12},{12... | collective-permute-start | bytes 73736 | tf_op jit(solution)/shard_map/ppermute | solution.py:369
  77.6 1.5 %collective-permute-done.3 = f32[24,256]{1,0:T(8,128)S(1)} collective-permute-done((f32[24,256]{1,0:T(8,128)S(1)}, f32[24,256]{1,0:T(8,128)S(1)}, u32[]{:S(2)}, u32[]{:S(2)}) %collective-permute-start.3) | collective-permute-done | bytes 24608 | tf_op jit(solution)/shard_map/ppermute | solution.py:369
  80.3 1.6 %outgoing.1 = bf16[64,4,8,512]{3,2,1,0:T(8,128)(2,1)} custom-call(bf16[64,8,512]{2,1,0:T(8,128)(2,1)S(1)} %get-tuple-element.25.first_ref, bf16[64,8,512]{2,1,0:T(8,128)(2,1)S(1)} %get-tuple-element.29.second_ref, f32[512,1024]{1,0:T(8,128)S(1)} %get-tuple-element.35.keep_ref, bf16[512,1024]{1,0:T(8,128)(2,1)S(1)} %collective-permute-done.recv_ref), custom_call_target="tpu_custom_call" | custom-call | tf_op jit(solution)/shard_map/outgoing/pallas_call | solution.py:316
  81.9 8.4 %all-to-all-start.2 = ((bf16[64,4,8,512]{3,2,1,0:T(8,128)(2,1)}), bf16[64,4,8,512]{3,2,1,0:T(8,128)(2,1)S(1)}, u32[]{:S(2)}, u32[]{:S(2)}) async-start(bf16[64,4,8,512]{3,2,1,0:T(8,128)(2,1)} %outgoing.1), calls=%async_computation.2 | async-start | bytes 4194304 | tf_op jit(solution)/shard_map/all_to_all | solution.py:404
  90.4 2.6 %collective-permute-start.7 = (f32[24,256]{1,0:T(8,128)S(1)}, f32[24,256]{1,0:T(8,128)S(1)}, u32[]{:S(2)}, u32[]{:S(2)}) collective-permute-start(f32[24,256]{1,0:T(8,128)S(1)} %add_add_fusion.2), channel_id=1, source_target_pairs={{0,32},{16,48},{32,0},{48,16},{1,33},{17,49},{33,1},{49,17},{2,34}... | collective-permute-start | bytes 73736 | tf_op jit(solution)/shard_map/ppermute | solution.py:369
  93.8 5.8 %collective-permute-done.7 = f32[24,256]{1,0:T(8,128)S(1)} collective-permute-done((f32[24,256]{1,0:T(8,128)S(1)}, f32[24,256]{1,0:T(8,128)S(1)}, u32[]{:S(2)}, u32[]{:S(2)}) %collective-permute-start.7) | collective-permute-done | bytes 24608 | tf_op jit(solution)/shard_map/ppermute | solution.py:369
  99.6 4.8 %collective-permute-done.8 = f32[24,256]{1,0:T(8,128)S(1)} collective-permute-done((f32[24,256]{1,0:T(8,128)S(1)}, f32[24,256]{1,0:T(8,128)S(1)}, u32[]{:S(2)}, u32[]{:S(2)}) %collective-permute-start.8) | collective-permute-done | bytes 24608 | tf_op jit(solution)/shard_map/ppermute | solution.py:369
  104.4 3.4 %collective-permute-done.6 = f32[24,256]{1,0:T(8,128)S(1)} collective-permute-done((f32[24,256]{1,0:T(8,128)S(1)}, f32[24,256]{1,0:T(8,128)S(1)}, u32[]{:S(2)}, u32[]{:S(2)}) %collective-permute-start.6) | collective-permute-done | bytes 24608 | tf_op jit(solution)/shard_map/ppermute | solution.py:369
  107.8 8.3 %collective-permute-start.10 = (f32[24,256]{1,0:T(8,128)S(1)}, f32[24,256]{1,0:T(8,128)S(1)}, u32[]{:S(2)}, u32[]{:S(2)}) collective-permute-start(f32[24,256]{1,0:T(8,128)S(1)} %add_add_fusion.1), channel_id=1, source_target_pairs={{0,64},{8,72},{64,0},{72,8},{1,65},{9,73},{65,1},{73,9},{2,66},{10... | collective-permute-start | bytes 73736 | tf_op jit(solution)/shard_map/ppermute | solution.py:369
  116.1 4.5 %collective-permute-start.11 = (f32[24,256]{1,0:T(8,128)S(1)}, f32[24,256]{1,0:T(8,128)S(1)}, u32[]{:S(2)}, u32[]{:S(2)}) collective-permute-start(f32[24,256]{1,0:T(8,128)S(1)} %add_add_fusion.1), channel_id=1, source_target_pairs={{0,72},{8,64},{64,8},{72,0},{1,73},{9,65},{65,9},{73,1},{2,74},{10... | collective-permute-start | bytes 73736 | tf_op jit(solution)/shard_map/ppermute | solution.py:369
  121.8 3.2 %collective-permute-done.9 = f32[24,256]{1,0:T(8,128)S(1)} collective-permute-done((f32[24,256]{1,0:T(8,128)S(1)}, f32[24,256]{1,0:T(8,128)S(1)}, u32[]{:S(2)}, u32[]{:S(2)}) %collective-permute-start.9) | collective-permute-done | bytes 24608 | tf_op jit(solution)/shard_map/ppermute | solution.py:369
  126.3 2.7 %collective-permute-start.5 = (f32[4,1024]{1,0:T(4,128)S(1)}, f32[4,1024]{1,0:T(4,128)S(1)}, u32[]{:S(2)}, u32[]{:S(2)}) collective-permute-start(f32[4,1024]{1,0:T(4,128)S(1)} %constant_dynamic-slice_fusion), channel_id=1, source_target_pairs={{0,1},{1,0},{2,3},{3,2},{4,5},{5,4},{6,7},{7,6},{8,9},{9,8},{10,11... | collective-permute-start | bytes 49160 | tf_op jit(solution)/shard_map/ppermute | solution.py:369
  (55 shorter events, 14.2 us)
Async XLA Ops:
  4.0 15.5 %copy-start.10 = (f32[16,225]{1,0:T(8,128)S(1)}, f32[16,225]{1,0:T(8,128)}, u32[]{:S(2)}) copy-start(f32[16,225]{1,0:T(8,128)} %param.11) | copy-start | bytes 43204
  4.0 28.1 %all-to-all-start = ((bf16[64,2,8,512]{3,2,1,0:T(8,128)(2,1)}), bf16[64,2,8,512]{3,2,1,0:T(8,128)(2,1)S(1)}, u32[]{:S(2)}, u32[]{:S(2)}) async-start(bf16[64,2,8,512]{3,2,1,0:T(8,128)(2,1)} %pair.2), calls=%async_computation | async-start | bytes 2097152 | tf_op jit(solution)/shard_map/all_to_all | solution.py:395
  19.7 18.8 %copy-start.3 = (bf16[512,512]{1,0:T(8,128)(2,1)S(1)}, bf16[512,512]{1,0:T(8,128)(2,1)}, u32[]{:S(2)}) copy-start(bf16[512,512]{1,0:T(8,128)(2,1)} %refs_2_.3) | copy-start | bytes 1572868
  19.7 18.8 %copy-start.4 = (f32[512]{0:T(512)S(1)}, f32[512]{0:T(512)}, u32[]{:S(2)}) copy-start(f32[512]{0:T(512)} %param.12) | copy-start | bytes 6148
  19.7 18.8 %copy-start.5 = (f32[512]{0:T(512)S(1)}, f32[512]{0:T(512)}, u32[]{:S(2)}) copy-start(f32[512]{0:T(512)} %param.13) | copy-start | bytes 6148
  32.1 21.3 %all-to-all-start.1 = ((bf16[64,2,8,512]{3,2,1,0:T(8,128)(2,1)}), bf16[64,2,8,512]{3,2,1,0:T(8,128)(2,1)S(1)}, u32[]{:S(2)}, u32[]{:S(2)}) async-start(bf16[64,2,8,512]{3,2,1,0:T(8,128)(2,1)} %pair.3), calls=%async_computation.1 | async-start | bytes 2097152 | tf_op jit(solution)/shard_map/all_to_all | solution.py:395
  38.5 1.4 %copy-start.1 = (bf16[512,1536]{1,0:T(8,128)(2,1)S(1)}, bf16[512,1536]{1,0:T(8,128)(2,1)}, u32[]{:S(2)}) copy-start(bf16[512,1536]{1,0:T(8,128)(2,1)} %refs_1_.3) | copy-start | bytes 4718596
  50.7 2.0 %copy-start.6 = (f32[512,2048]{1,0:T(8,128)}, f32[512,2048]{1,0:T(8,128)S(1)}, u32[]{:S(2)}) copy-start(f32[512,2048]{1,0:T(8,128)S(1)} %get-tuple-element.34.before) | copy-start | bytes 12582916
  53.4 1.4 %copy-start.2 = (bf16[512,1536]{1,0:T(8,128)(2,1)S(1)}, bf16[512,1536]{1,0:T(8,128)(2,1)}, u32[]{:S(2)}) copy-start(bf16[512,1536]{1,0:T(8,128)(2,1)} %refs_1_.3) | copy-start | bytes 4718596
  55.8 11.1 %copy-start.7 = (f32[512,2048]{1,0:T(8,128)S(1)}, f32[512,2048]{1,0:T(8,128)}, u32[]{:S(2)}) copy-start(f32[512,2048]{1,0:T(8,128)} %copy-done.6) | copy-start | bytes 12582916
  68.4 11.9 %collective-permute-start = (bf16[512,1024]{1,0:T(8,128)(2,1)S(1)}, bf16[512,1024]{1,0:T(8,128)(2,1)S(1)}, u32[]{:S(2)}, u32[]{:S(2)}) collective-permute-start(bf16[512,1024]{1,0:T(8,128)(2,1)S(1)} %get-tuple-element.36), channel_id=1, source_target_pairs={{0,1},{1,0},{2,3},{3,2},{4,5},{5,4},{6,7},{7,6},{8,9},{9,8},{10,11... | collective-permute-start | bytes 3145736 | tf_op jit(solution)/shard_map/ppermute | solution.py:369
  72.6 2.3 %collective-permute-start.1 = (f32[24,256]{1,0:T(8,128)S(1)}, f32[24,256]{1,0:T(8,128)S(1)}, u32[]{:S(2)}, u32[]{:S(2)}) collective-permute-start(f32[24,256]{1,0:T(8,128)S(1)} %get-tuple-element.37), channel_id=1, source_target_pairs={{0,1},{1,0},{2,3},{3,2},{4,5},{5,4},{6,7},{7,6},{8,9},{9,8},{10,11... | collective-permute-start | bytes 73736 | tf_op jit(solution)/shard_map/ppermute | solution.py:369
  74.9 4.2 %collective-permute-start.3 = (f32[24,256]{1,0:T(8,128)S(1)}, f32[24,256]{1,0:T(8,128)S(1)}, u32[]{:S(2)}, u32[]{:S(2)}) collective-permute-start(f32[24,256]{1,0:T(8,128)S(1)} %add.95), channel_id=1, source_target_pairs={{0,4},{2,6},{4,0},{6,2},{1,5},{3,7},{5,1},{7,3},{8,12},{10,14},{12... | collective-permute-start | bytes 73736 | tf_op jit(solution)/shard_map/ppermute | solution.py:369
  76.1 4.1 %collective-permute-start.4 = (f32[24,256]{1,0:T(8,128)S(1)}, f32[24,256]{1,0:T(8,128)S(1)}, u32[]{:S(2)}, u32[]{:S(2)}) collective-permute-start(f32[24,256]{1,0:T(8,128)S(1)} %add.95), channel_id=1, source_target_pairs={{0,6},{2,4},{4,2},{6,0},{1,7},{3,5},{5,3},{7,1},{8,14},{10,12},{12... | collective-permute-start | bytes 73736 | tf_op jit(solution)/shard_map/ppermute | solution.py:369
  77.6 2.7 %collective-permute-start.2 = (f32[24,256]{1,0:T(8,128)S(1)}, f32[24,256]{1,0:T(8,128)S(1)}, u32[]{:S(2)}, u32[]{:S(2)}) collective-permute-start(f32[24,256]{1,0:T(8,128)S(1)} %add.95), channel_id=1, source_target_pairs={{0,2},{2,0},{4,6},{6,4},{1,3},{3,1},{5,7},{7,5},{8,10},{10,8},{12,... | collective-permute-start | bytes 73736 | tf_op jit(solution)/shard_map/ppermute | solution.py:369
  81.9 43.1 %copy-start = (bf16[16,64,512]{2,1,0:T(8,128)(2,1)S(1)}, bf16[16,64,512]{2,1,0:T(8,128)(2,1)}, u32[]{:S(2)}) copy-start(bf16[16,64,512]{2,1,0:T(8,128)(2,1)} %param.8) | copy-start | bytes 3145732
  81.9 43.1 %all-to-all-start.2 = ((bf16[64,4,8,512]{3,2,1,0:T(8,128)(2,1)}), bf16[64,4,8,512]{3,2,1,0:T(8,128)(2,1)S(1)}, u32[]{:S(2)}, u32[]{:S(2)}) async-start(bf16[64,4,8,512]{3,2,1,0:T(8,128)(2,1)} %outgoing.1), calls=%async_computation.2 | async-start | bytes 4194304 | tf_op jit(solution)/shard_map/all_to_all | solution.py:404
  90.4 9.3 %collective-permute-start.7 = (f32[24,256]{1,0:T(8,128)S(1)}, f32[24,256]{1,0:T(8,128)S(1)}, u32[]{:S(2)}, u32[]{:S(2)}) collective-permute-start(f32[24,256]{1,0:T(8,128)S(1)} %add_add_fusion.2), channel_id=1, source_target_pairs={{0,32},{16,48},{32,0},{48,16},{1,33},{17,49},{33,1},{49,17},{2,34}... | collective-permute-start | bytes 73736 | tf_op jit(solution)/shard_map/ppermute | solution.py:369
  93.0 11.4 %collective-permute-start.8 = (f32[24,256]{1,0:T(8,128)S(1)}, f32[24,256]{1,0:T(8,128)S(1)}, u32[]{:S(2)}, u32[]{:S(2)}) collective-permute-start(f32[24,256]{1,0:T(8,128)S(1)} %add_add_fusion.2), channel_id=1, source_target_pairs={{0,48},{16,32},{32,16},{48,0},{1,49},{17,33},{33,17},{49,1},{2,50}... | collective-permute-start | bytes 73736 | tf_op jit(solution)/shard_map/ppermute | solution.py:369
  93.8 13.9 %collective-permute-start.6 = (f32[24,256]{1,0:T(8,128)S(1)}, f32[24,256]{1,0:T(8,128)S(1)}, u32[]{:S(2)}, u32[]{:S(2)}) collective-permute-start(f32[24,256]{1,0:T(8,128)S(1)} %add_add_fusion.2), channel_id=1, source_target_pairs={{0,16},{16,0},{32,48},{48,32},{1,17},{17,1},{33,49},{49,33},{2,18}... | collective-permute-start | bytes 73736 | tf_op jit(solution)/shard_map/ppermute | solution.py:369
  107.8 13.9 %collective-permute-start.10 = (f32[24,256]{1,0:T(8,128)S(1)}, f32[24,256]{1,0:T(8,128)S(1)}, u32[]{:S(2)}, u32[]{:S(2)}) collective-permute-start(f32[24,256]{1,0:T(8,128)S(1)} %add_add_fusion.1), channel_id=1, source_target_pairs={{0,64},{8,72},{64,0},{72,8},{1,65},{9,73},{65,1},{73,9},{2,66},{10... | collective-permute-start | bytes 73736 | tf_op jit(solution)/shard_map/ppermute | solution.py:369
  116.1 5.7 %collective-permute-start.11 = (f32[24,256]{1,0:T(8,128)S(1)}, f32[24,256]{1,0:T(8,128)S(1)}, u32[]{:S(2)}, u32[]{:S(2)}) collective-permute-start(f32[24,256]{1,0:T(8,128)S(1)} %add_add_fusion.1), channel_id=1, source_target_pairs={{0,72},{8,64},{64,8},{72,0},{1,73},{9,65},{65,9},{73,1},{2,74},{10... | collective-permute-start | bytes 73736 | tf_op jit(solution)/shard_map/ppermute | solution.py:369
  120.6 4.4 %collective-permute-start.9 = (f32[24,256]{1,0:T(8,128)S(1)}, f32[24,256]{1,0:T(8,128)S(1)}, u32[]{:S(2)}, u32[]{:S(2)}) collective-permute-start(f32[24,256]{1,0:T(8,128)S(1)} %add_add_fusion.1), channel_id=1, source_target_pairs={{0,8},{8,0},{64,72},{72,64},{1,9},{9,1},{65,73},{73,65},{2,10},{10... | collective-permute-start | bytes 73736 | tf_op jit(solution)/shard_map/ppermute | solution.py:369
  126.3 4.7 %collective-permute-start.5 = (f32[4,1024]{1,0:T(4,128)S(1)}, f32[4,1024]{1,0:T(4,128)S(1)}, u32[]{:S(2)}, u32[]{:S(2)}) collective-permute-start(f32[4,1024]{1,0:T(4,128)S(1)} %constant_dynamic-slice_fusion), channel_id=1, source_target_pairs={{0,1},{1,0},{2,3},{3,2},{4,5},{5,4},{6,7},{7,6},{8,9},{9,8},{10,11... | collective-permute-start | bytes 49160 | tf_op jit(solution)/shard_map/ppermute | solution.py:369
  (2 other events, 1.7 us)

commit v4 on v3

v4 whole, which is shorter than its diff:
```python
import functools
import jax
import jax.numpy as jnp
from jax import lax
from jax.experimental import pallas as pl
from jax.experimental.pallas import tpu as pltpu
from jax.sharding import Mesh, PartitionSpec as P

GRID = 8
EPSILON = 1e-05
MEMBERS = GRID * GRID
PACK = 4
PARTS = 2
CHUNK = 256


def dot(a, b, ca, cb):
    return lax.dot_general(a, b, (((ca,), (cb,)), ((), ())), preferred_element_type=jnp.float32)


def put(ref, at, value):
    for b in range(ref.shape[0]):
        ref[b, at, :] = value[:, b * 128 : (b + 1) * 128]


def take(ref, at):
    return jnp.concatenate([ref[b, at, :] for b in range(ref.shape[0])], axis=1)


def forward_and_scores(
    pair_ref, wqkv_ref, wout_ref, bias_ref, gain_ref, shift_ref, gbias_ref,
    normed, gproj, att, dyp, hat, istd, proj, gatt, dyf, head_dim, fetches,
):
    width = gproj.shape[1] // 3
    rows, groups, chunk = gproj.shape[0], gproj.shape[0] // MEMBERS, CHUNK
    per, mem = chunk // MEMBERS, chunk // groups
    bf16, f32 = jnp.bfloat16, jnp.float32
    scale = head_dim ** (-0.5)

    def hat_step(c, carry):
        here = pl.ds(pl.multiple_of(c * chunk, chunk), chunk)
        pair = pair_ref[pl.ds(pl.multiple_of(c * mem, mem), mem)].astype(f32)
        x = pair[:, 0].reshape(chunk, width)
        centred = x - jnp.mean(x, axis=-1, keepdims=True)
        inv = lax.rsqrt(jnp.mean(centred * centred, axis=-1, keepdims=True) + EPSILON)
        put(hat, here, centred * inv)
        istd[here, :] = jnp.broadcast_to(inv, (chunk, 128))
        put(dyf, here, pair[:, 1].reshape(chunk, width))
        return carry

    lax.fori_loop(0, rows // chunk, hat_step, 0)
    for fetch in fetches:
        fetch.wait()

    def by_group(ref, c):
        return jnp.concatenate(
            [take(ref, pl.ds(c * per + g, MEMBERS, stride=groups)) for g in range(per)], axis=0
        )

    def norm_step(c, carry):
        here = pl.ds(pl.multiple_of(c * chunk, chunk), chunk)
        nb = (by_group(hat, c) * gain_ref[...] + shift_ref[...]).astype(bf16)
        dy = by_group(dyf, c).astype(bf16)
        dyp[here, :] = dy
        normed[here, :] = nb
        proj[here, :] = dot(nb, wqkv_ref[...], 1, 0).astype(bf16)
        gatt[here, :] = dot(dy, wout_ref[...], 1, 1).astype(bf16)
        return carry

    lax.fori_loop(0, rows // chunk, norm_step, 0)

    lane = lax.broadcasted_iota(jnp.int32, (MEMBERS, 128), 1) // head_dim

    def spread(a):
        zero = jnp.zeros_like(a)
        return jnp.concatenate([jnp.where(lane == h, a, zero) for h in range(PACK)], axis=0)

    def gather(a):
        out = a[:MEMBERS]
        for h in range(1, PACK):
            out = jnp.where(lane == h, a[h * MEMBERS : (h + 1) * MEMBERS], out)
        return out

    blocks = range(width // 128)

    def group_step(g, carry):
        here = pl.ds(pl.multiple_of(g * MEMBERS, MEMBERS), MEMBERS)
        cols = [slice(b * 128, (b + 1) * 128) for b in blocks]
        kcols = [slice(width + b * 128, width + (b + 1) * 128) for b in blocks]
        vcols = [slice(2 * width + b * 128, 2 * width + (b + 1) * 128) for b in blocks]
        ks = [proj[here, c] for c in kcols]
        vs = [proj[here, c] for c in vcols]
        none = jnp.zeros_like(ks[0])
        ws = [jnp.concatenate([spread(proj[here, c]), spread(gatt[here, c])], axis=1) for c in cols]
        both = [
            dot(
                jnp.concatenate(
                    [jnp.concatenate([k, none], axis=1), jnp.concatenate([none, v], axis=1)], axis=0
                ),
                w, 1, 1,
            )
            for k, v, w in zip(ks, vs, ws)
        ]
        pds = []
        for b in blocks:
            scores = both[b][:MEMBERS] * scale + bias_ref[b]
            gp = both[b][MEMBERS:]
            e = jnp.exp(scores - jnp.max(scores, axis=0, keepdims=True))
            p = e * (1.0 / jnp.sum(e, axis=0, keepdims=True))
            gs = p * (gp - jnp.sum(gp * p, axis=0, keepdims=True))
            gbias_ref[b] += gs
            pds.append(jnp.concatenate([p.astype(bf16), (gs * scale).astype(bf16)], axis=0))
        keyed = [dot(pd, w, 1, 0) for pd, w in zip(pds, ws)]
        queried = [
            dot(
                pd,
                jnp.concatenate(
                    [jnp.concatenate([v, none], axis=1), jnp.concatenate([none, k], axis=1)], axis=0
                ),
                0, 0,
            )
            for k, v, pd in zip(ks, vs, pds)
        ]
        for b in blocks:
            att[here, cols[b]] = gather(queried[b][:, :128]).astype(bf16)
            gproj[here, cols[b]] = gather(queried[b][:, 128:]).astype(bf16)
            gproj[here, kcols[b]] = keyed[b][MEMBERS:, :128].astype(bf16)
            gproj[here, vcols[b]] = keyed[b][:MEMBERS, 128:].astype(bf16)
        return carry

    lax.fori_loop(0, groups, group_step, 0)


def back_to_input(wqkv_ref, gain_ref, branch_ref, gproj, hat, istd, dyf):
    width = gproj.shape[1] // 3
    rows, groups, chunk = gproj.shape[0], gproj.shape[0] // MEMBERS, CHUNK
    per, mem = chunk // MEMBERS, chunk // groups
    bf16, f32 = jnp.bfloat16, jnp.float32

    def gn_step(c, carry):
        here = pl.ds(pl.multiple_of(c * chunk, chunk), chunk)
        gn = dot(gproj[here, :], wqkv_ref[...], 1, 1)
        for g in range(per):
            put(dyf, pl.ds(c * per + g, MEMBERS, stride=groups), gn[g * MEMBERS : (g + 1) * MEMBERS])
        return carry

    lax.fori_loop(0, rows // chunk, gn_step, 0)

    def back_step(c, carry):
        gg, gsh = carry
        here = pl.ds(pl.multiple_of(c * chunk, chunk), chunk)
        gn = take(dyf, here)
        normalized = take(hat, here)
        prod = gn * normalized
        gg = gg + jnp.sum(prod.reshape(chunk // 8, 8, width), axis=0)
        gsh = gsh + jnp.sum(gn.reshape(chunk // 8, 8, width), axis=0)
        gh = gn * gain_ref[...]
        m1 = jnp.mean(gh, axis=-1, keepdims=True)
        m2 = jnp.mean(prod * gain_ref[...], axis=-1, keepdims=True)
        inv = istd[here, :][:, :1]
        branch = (inv * (gh - m1 - normalized * m2)).astype(bf16)
        branch_ref[pl.ds(pl.multiple_of(c * mem, mem), mem)] = branch.reshape(mem, groups, width)
        return gg, gsh

    zero = jnp.zeros((8, width), f32)
    gg, gsh = lax.fori_loop(0, rows // chunk, back_step, (zero, zero))
    return jnp.sum(gg, axis=0, keepdims=True), jnp.sum(gsh, axis=0, keepdims=True)


def offset_sums(gbias_ref):
    f32, bf16 = jnp.float32, jnp.bfloat16
    blocks, members, lanes = gbias_ref.shape
    i = lax.broadcasted_iota(jnp.int32, (lanes, 2 * lanes), 0)
    o = lax.broadcasted_iota(jnp.int32, (lanes, 2 * lanes), 1)
    query = i % members
    place = (i // members) * 128 + query // GRID * 16 + query % GRID
    wide = (o == place).astype(f32).astype(bf16)
    frames = []
    for b in range(blocks):
        value = gbias_ref[b]
        high = value.astype(bf16)
        rest = value - high.astype(f32)
        low = rest.astype(bf16)
        lowest = (rest - low.astype(f32)).astype(bf16)
        spread = dot(jnp.concatenate([high, low, lowest], axis=0), wide, 1, 0)
        spread = spread[:members] + (spread[members : 2 * members] + spread[2 * members :])
        frames += [spread[None, :, h * 128 : (h + 1) * 128] for h in range(PACK)]
    frame = jnp.concatenate(frames, axis=0)
    heads = frame.shape[0]
    frame = jnp.concatenate([frame, jnp.zeros_like(frame)], axis=2).reshape(heads * members, 256)
    column = GRID - 1 - lax.broadcasted_iota(jnp.int32, frame.shape, 0) % GRID
    for bit in (1, 2, 4):
        frame = jnp.where((column & bit) != 0, pltpu.roll(frame, bit, 1), frame)
    frame = jnp.sum(frame.reshape(heads * GRID, GRID, 256), axis=1)
    row = GRID - 1 - lax.broadcasted_iota(jnp.int32, frame.shape, 0) % GRID
    for bit in (1, 2, 4):
        frame = jnp.where((row & bit) != 0, pltpu.roll(frame, 16 * bit, 1), frame)
    return jnp.sum(frame.reshape(heads, GRID, 256), axis=1)


def first_kernel(
    pair_ref, wqkv_hbm, wout_hbm, bias_ref, gain_ref, shift_ref,
    branch_ref, sums_hbm, gbias_hbm, gvec_ref,
    wqkv_ref, wout_ref, sums_ref, gbias_ref, normed, gproj, att, dyp, hat, istd, proj, gatt, dyf, sems, *, head_dim,
):
    width = wout_ref.shape[0]
    fetches = [
        pltpu.make_async_copy(wqkv_hbm, wqkv_ref, sems.at[0]),
        pltpu.make_async_copy(wout_hbm, wout_ref, sems.at[1]),
    ]
    for fetch in fetches:
        fetch.start()
    gbias_ref[...] = jnp.zeros_like(gbias_ref)
    forward_and_scores(
        pair_ref, wqkv_ref, wout_ref, bias_ref, gain_ref, shift_ref, gbias_ref,
        normed, gproj, att, dyp, hat, istd, proj, gatt, dyf, head_dim, fetches,
    )
    sums_ref[:, : 3 * width] = dot(normed[...], gproj[...], 0, 0)
    sums_ref[:, 3 * width :] = dot(att[...], dyp[...], 0, 0)
    stores = [
        pltpu.make_async_copy(sums_ref, sums_hbm, sems.at[2]),
        pltpu.make_async_copy(gbias_ref, gbias_hbm, sems.at[3]),
    ]
    for store in stores:
        store.start()
    gain_sum, shift_sum = back_to_input(wqkv_ref, gain_ref, branch_ref, gproj, hat, istd, dyf)
    gvec_ref[0:1, :] = gain_sum
    gvec_ref[1:2, :] = shift_sum
    for store in stores:
        store.wait()


def second_kernel(
    core_ref, pair_ref, wqkv_hbm, wout_hbm, bias_ref, gain_ref, shift_ref, sums_hbm, gbias_hbm,
    keep_ref, send_ref, gbias_ref, gproj, hat, istd,
    wqkv_ref, wout_ref, sums_ref, gbias_before, normed, att, dyp, proj, gatt, dyf, sems, *, head_dim,
):
    fetches = [
        pltpu.make_async_copy(wqkv_hbm, wqkv_ref, sems.at[0]),
        pltpu.make_async_copy(wout_hbm, wout_ref, sems.at[1]),
        pltpu.make_async_copy(gbias_hbm, gbias_before, sems.at[2]),
    ]
    late = pltpu.make_async_copy(sums_hbm, sums_ref, sems.at[3])
    for fetch in fetches:
        fetch.start()
    late.start()
    gbias_ref[...] = jnp.zeros_like(gbias_ref)
    forward_and_scores(
        pair_ref, wqkv_ref, wout_ref, bias_ref, gain_ref, shift_ref, gbias_ref,
        normed, gproj, att, dyp, hat, istd, proj, gatt, dyf, head_dim, fetches,
    )
    gbias_ref[...] += gbias_before[...]
    late.wait()
    half = sums_ref.shape[1] // 2
    gw = dot(normed[...], gproj[...], 0, 0)
    go = dot(att[...], dyp[...], 0, 0)
    low = gw[:, :half] + sums_ref[:, :half]
    high = jnp.concatenate([gw[:, half:], go], axis=1) + sums_ref[:, half:]

    @pl.when(core_ref[0] == 0)
    def _():
        keep_ref[...] = low
        send_ref[...] = high.astype(send_ref.dtype)

    @pl.when(core_ref[0] != 0)
    def _():
        keep_ref[...] = high
        send_ref[...] = low.astype(send_ref.dtype)


def third_kernel(
    wqkv_hbm, gain_ref, gproj, hat, istd, gbias_ref, gvec_ref, branch_ref, small_ref, wqkv_ref, dyf, sem, *, heads
):
    fetch = pltpu.make_async_copy(wqkv_hbm, wqkv_ref, sem)
    fetch.start()
    table = offset_sums(gbias_ref)
    small_ref[:heads, :] = table[:, :128]
    small_ref[heads : 2 * heads, :] = table[:, 128:]
    fetch.wait()
    sums = back_to_input(wqkv_ref, gain_ref, branch_ref, gproj, hat, istd, dyf)
    lanes = hat.shape[0]
    for i in range(2):
        total = sums[i] + gvec_ref[i : i + 1, :]
        for b in range(lanes):
            row = 2 * heads + i * lanes + b
            small_ref[row : row + 1, :] = total[:, b * 128 : (b + 1) * 128]


VMEM = pl.BlockSpec(memory_space=pltpu.VMEM)
SMEM = pl.BlockSpec(memory_space=pltpu.SMEM)
HBM = pl.BlockSpec(memory_space=pltpu.HBM)
MIB = 1024 * 1024


def shaped(*shape, dtype=jnp.float32):
    return jax.ShapeDtypeStruct(shape, dtype)


def cost(flops, size):
    return pl.CostEstimate(flops=flops, bytes_accessed=size, transcendentals=0)


def part_buffers(rows, width):
    bf16, f32 = jnp.bfloat16, jnp.float32
    tall, lanes = (rows, width), (width // 128, rows, 128)
    return [
        (tall, bf16), ((rows, 3 * width), bf16), (tall, bf16), (tall, bf16), (lanes, f32), ((rows, 128), f32),
        ((rows, 3 * width), bf16), (tall, bf16), (lanes, f32),
    ]


def first_part(pair, wqkv, wout, bias, gain, shift, head_dim):
    members, _, groups, width = pair.shape
    sums = (width, 4 * width)
    return pl.pallas_call(
        functools.partial(first_kernel, head_dim=head_dim),
        out_shape=(
            shaped(members, groups, width, dtype=pair.dtype), shaped(*sums), shaped(*bias.shape), shaped(2, width)
        ),
        in_specs=[VMEM, HBM, HBM, VMEM, VMEM, VMEM],
        out_specs=(VMEM, HBM, HBM, VMEM),
        scratch_shapes=[
            pltpu.VMEM(wqkv.shape, wqkv.dtype), pltpu.VMEM(wout.shape, wout.dtype),
            pltpu.VMEM(sums, jnp.float32), pltpu.VMEM(bias.shape, jnp.float32),
        ]
        + [pltpu.VMEM(*b) for b in part_buffers(groups * MEMBERS, width)]
        + [pltpu.SemaphoreType.DMA((4,))],
        compiler_params=pltpu.CompilerParams(vmem_limit_bytes=28 * MIB),
        cost_estimate=cost(10_000_000_000, 8 << 20),
        name="first_part",
    )(pair, wqkv, wout, bias, gain.reshape(1, width), shift.reshape(1, width))


def second_part(core, pair, wqkv, wout, bias, gain, shift, sums, gbias, head_dim):
    members, _, groups, width = pair.shape
    bf16, f32 = jnp.bfloat16, jnp.float32
    normed, gproj, att, dyp, hat, istd, proj, gatt, dyf = part_buffers(groups * MEMBERS, width)
    return pl.pallas_call(
        functools.partial(second_kernel, head_dim=head_dim),
        out_shape=(shaped(width, 2 * width), shaped(width, 2 * width, dtype=bf16), shaped(*bias.shape))
        + tuple(jax.ShapeDtypeStruct(*b) for b in (gproj, hat, istd)),
        in_specs=[SMEM, VMEM, HBM, HBM, VMEM, VMEM, VMEM, HBM, HBM],
        out_specs=(VMEM,) * 6,
        scratch_shapes=[
            pltpu.VMEM(wqkv.shape, wqkv.dtype), pltpu.VMEM(wout.shape, wout.dtype),
            pltpu.VMEM(sums.shape, f32), pltpu.VMEM(bias.shape, f32),
        ]
        + [pltpu.VMEM(*b) for b in (normed, att, dyp, proj, gatt, dyf)]
        + [pltpu.SemaphoreType.DMA((4,))],
        compiler_params=pltpu.CompilerParams(vmem_limit_bytes=28 * MIB),
        cost_estimate=cost(10_000_000_000, 8 << 20),
        name="second_part",
    )(core.reshape(1), pair, wqkv, wout, bias, gain.reshape(1, width), shift.reshape(1, width), sums, gbias)


def second_back(wqkv, gain, gproj, hat, istd, gbias, gvec, groups, heads):
    rows, width = istd.shape[0], gain.shape[0]
    return pl.pallas_call(
        functools.partial(third_kernel, heads=heads),
        out_shape=(
            shaped(MEMBERS, groups, width, dtype=gproj.dtype), shaped(2 * heads + 2 * width // 128, 128)
        ),
        in_specs=[HBM] + [VMEM] * 6,
        out_specs=(VMEM,) * 2,
        scratch_shapes=[
            pltpu.VMEM(wqkv.shape, wqkv.dtype), pltpu.VMEM(hat.shape, jnp.float32), pltpu.SemaphoreType.DMA
        ],
        compiler_params=pltpu.CompilerParams(vmem_limit_bytes=20 * MIB),
        cost_estimate=cost(4_000_000_000, 4 << 20),
        name="second_back",
    )(wqkv, gain.reshape(1, width), gproj, hat, istd, gbias, gvec)


def pair_kernel(x_ref, dy_ref, out_ref):
    out_ref[:, 0] = x_ref[0]
    out_ref[:, 1] = dy_ref[0]


def pair_of(x, dy, part):
    _, chips, groups, width = x.shape
    steps = 2
    source = pl.BlockSpec((1, chips // steps, groups, width), lambda i: (part, i, 0, 0))
    return pl.pallas_call(
        pair_kernel,
        grid=(steps,),
        out_shape=shaped(chips, 2, groups, width, dtype=x.dtype),
        in_specs=[source, source],
        out_specs=pl.BlockSpec((chips // steps, 2, groups, width), lambda i: (i, 0, 0, 0)),
        cost_estimate=cost(0, 2 << 20),
        name="pair",
    )(x, dy)


def outgoing_kernel(first_ref, second_ref, keep_ref, recv_ref, small_ref, out_ref):
    chips, _, groups, _ = out_ref.shape
    lanes = first_ref.shape[2] // 128
    for b in range(lanes):
        cols = slice(b * 128, (b + 1) * 128)
        out_ref[:, b] = first_ref[:, :, cols]
        out_ref[:, lanes + b] = second_ref[:, :, cols]
    for b in range(2 * lanes):
        cols = slice(b * 128, (b + 1) * 128)
        total = (keep_ref[:, cols] + recv_ref[:, cols].astype(jnp.float32)).astype(jnp.bfloat16)
        out_ref[:, 2 * lanes + b] = total.reshape(chips, groups, 128)
    for i in range(small_ref.shape[0] // groups):
        value = small_ref[i * groups : (i + 1) * groups, :].astype(jnp.bfloat16)
        out_ref[:, 4 * lanes + i] = jnp.broadcast_to(value[None], (chips, groups, 128))


def outgoing(first, second, keep, recv, small):
    chips, groups, width = first.shape
    slots = 4 * (width // 128) + small.shape[0] // groups
    return pl.pallas_call(
        outgoing_kernel,
        out_shape=shaped(chips, slots, groups, 128, dtype=first.dtype),
        in_specs=[VMEM] * 5,
        out_specs=VMEM,
        compiler_params=pltpu.CompilerParams(vmem_limit_bytes=20 * MIB),
        cost_estimate=cost(0, 6 << 20),
        name="outgoing",
    )(first, second, keep, recv, small)


def final_kernel(core_ref, got_ref, dy_ref, grad_ref, keep_ref, send_ref, *, factor):
    f32 = jnp.float32
    chips, slots, groups, _ = got_ref.shape
    lanes = dy_ref.shape[3] // 128
    for part in range(PARTS):
        for b in range(lanes):
            cols = slice(b * 128, (b + 1) * 128)
            branch = got_ref[:, part * lanes + b].astype(f32)
            grad_ref[part, :, :, cols] = (dy_ref[part, :, :, cols].astype(f32) + branch).astype(grad_ref.dtype)
    total = got_ref[0, 2 * lanes :].astype(f32)
    for chip in range(1, chips):
        total = total + got_ref[chip, 2 * lanes :].astype(f32)
    total = total * factor
    share = groups // 2
    for b in range(2 * lanes):
        rows = slice(b * share, (b + 1) * share)
        low, high = total[b, :share], total[b, share:]
        keep_ref[rows, :] = jnp.where(core_ref[0] == 0, low, high)
        send_ref[rows, :] = jnp.where(core_ref[0] == 0, high, low)
    for i in range(2 * lanes, slots - 2 * lanes):
        rows = slice(2 * lanes * share + (i - 2 * lanes) * groups, 2 * lanes * share + (i - 2 * lanes + 1) * groups)
        keep_ref[rows, :] = total[i]
        send_ref[rows, :] = total[i]


def final(core, got, dy, factor):
    chips, slots, groups, _ = got.shape
    lanes = dy.shape[3] // 128
    rows = 2 * lanes * (groups // 2) + (slots - 4 * lanes) * groups
    return pl.pallas_call(
        functools.partial(final_kernel, factor=factor),
        out_shape=(jax.ShapeDtypeStruct(dy.shape, dy.dtype), shaped(rows, 128), shaped(rows, 128)),
        in_specs=[SMEM, VMEM, VMEM],
        out_specs=(VMEM,) * 3,
        compiler_params=pltpu.CompilerParams(vmem_limit_bytes=16 * MIB),
        cost_estimate=cost(0, 6 << 20),
        name="final",
    )(core.reshape(1), got, dy)


def finish_kernel(core_ref, keep_ref, recv_ref, qkv_ref, out_ref, table_ref, gain_ref, shift_ref):
    width = out_ref.shape[1]
    lanes = width // 128
    share, heads = out_ref.shape[0], table_ref.shape[0]
    first = core_ref[0] == 0
    for b in range(4 * lanes):
        rows = slice(b % (2 * lanes) * share, (b % (2 * lanes) + 1) * share)
        mine, other = keep_ref[rows, :], recv_ref[rows, :]
        value = jnp.where(first, mine, other) if b < 2 * lanes else jnp.where(first, other, mine)
        if b < 3 * lanes:
            qkv_ref[:, b * 128 : (b + 1) * 128] = value
        else:
            out_ref[:, (b - 3 * lanes) * 128 : (b - 3 * lanes + 1) * 128] = value
    at = 2 * lanes * share
    small = keep_ref[at:, :] + recv_ref[at:, :]
    table = jnp.concatenate([small[:heads], small[heads : 2 * heads]], axis=1)
    side = 2 * GRID - 1
    for i in range(side):
        table_ref[:, i * side : (i + 1) * side] = table[:, i * 16 : i * 16 + side]
    for ref, row in ((gain_ref, 2 * heads), (shift_ref, 2 * heads + lanes)):
        for b in range(lanes):
            ref[:, b * 128 : (b + 1) * 128] = small[row + b : row + b + 1, :]


def finish(core, keep, recv, width, heads, offsets):
    share = (keep.shape[0] - 2 * heads - 2 * width // 128) // (2 * width // 128)
    return pl.pallas_call(
        finish_kernel,
        out_shape=(
            shaped(share, 3 * width), shaped(share, width), shaped(heads, offsets), shaped(1, width), shaped(1, width)
        ),
        in_specs=[SMEM, VMEM, VMEM],
        out_specs=(VMEM,) * 5,
        name="finish",
    )(core.reshape(1), keep, recv)


AXES = ("x_lo", "y", "x_hi", "z", "core")
CHIPS = AXES[:4]


def relative_onehot(members):
    span = 2 * GRID - 1
    second = jnp.arange(members, dtype=jnp.int32)[:, None]
    first = jnp.arange(members, dtype=jnp.int32)[None, :]
    row_delta = first // GRID - second // GRID + GRID - 1
    col_delta = first % GRID - second % GRID + GRID - 1
    rel_index = row_delta * span + col_delta
    offsets = jnp.arange(span * span, dtype=jnp.int32)
    return (rel_index[:, :, None] == offsets).astype(jnp.float32)


def swap(a, axis, mask):
    size = lax.axis_size(axis)
    return lax.ppermute(a, axis, [(i, i ^ mask) for i in range(size)])


def local(block_input, cotangent, qkv_weight, out_weight, bias_table, norm_gain, norm_shift):
    tile_h, tile_w, width = block_input.shape
    heads, offsets = bias_table.shape
    chips = lax.axis_size(CHIPS)
    devices = chips * lax.axis_size("core")
    owned = tile_h * tile_w // chips // PARTS
    core = lax.axis_index("core")
    onehot = relative_onehot(MEMBERS)
    bias = jnp.einsum(
        "bhr,kqr->bkhq",
        bias_table.reshape(heads // PACK, PACK, offsets),
        onehot,
        precision=lax.Precision.HIGHEST,
    ).reshape(heads // PACK, MEMBERS, PACK * MEMBERS)
    shape = (PARTS, chips, owned, width)
    x, dy = block_input.reshape(shape), cotangent.reshape(shape)
    sent = [pair_of(x, dy, part) for part in range(PARTS)]
    exchange = functools.partial(lax.all_to_all, axis_name=CHIPS, split_axis=0, concat_axis=0, tiled=True)
    got = [exchange(sent[0])]
    got[0], sent[1], bias = lax.optimization_barrier((got[0], sent[1], bias))
    got.append(exchange(sent[1]))
    head_dim = width // heads
    common = (qkv_weight, out_weight, bias, norm_gain, norm_shift)
    first, sums, gbias, gvec = first_part(got[0], *common, head_dim)
    keep, send, gbias, gproj, hat, istd = second_part(core, got[1], *common, sums, gbias, head_dim)
    recv = swap(send, "core", 1)
    second, small = second_back(qkv_weight, norm_gain, gproj, hat, istd, gbias, gvec, owned, heads)
    back = outgoing(first, second, keep, recv, small)
    back = exchange(back)
    factor = float(tile_h * tile_w * devices) ** (-0.5)
    grad_input, mine, theirs = final(core, back, dy, factor)
    grad_qkv, grad_out, table, gain, shift = finish(core, mine, swap(theirs, "core", 1), width, heads, offsets)
    return (
        grad_input.reshape(tile_h, tile_w, width),
        grad_qkv,
        grad_out,
        table,
        gain.reshape(width),
        shift.reshape(width),
    )


def solution(mesh):
    fine = Mesh(mesh.devices.reshape(2, 4, 2, 4, 2), AXES)
    tile = P(("x_lo", "y"), ("x_hi", "z", "core"), None)
    return jax.shard_map(
        local,
        mesh=fine,
        in_specs=(tile, tile, P(), P(), P(), P(), P()),
        out_specs=(tile, P(AXES, None), P(AXES, None), P(), P(), P()),
        check_vma=False,
    )
```

time: 133 us -> 128 us (0.962)
  blocking collectives: 0 us -> 45.5 us
  starting transfers between devices: 54.1 us -> 24.5 us
  waiting for transfers between devices: 30.8 us -> 11 us
    all_to_all x0 -> x1, blocking collectives: none -> 45.5 us  [local(): back = exchange(back)]
    ppermute x12 -> x2, starting transfers between devices: 27.2 us -> 6.02 us  [swap(): return lax.ppermute(a, axis, [(i, i ^ mask) for i in range(size)])]
    ppermute x12 -> x2, waiting for transfers between devices: 22 us -> 0.87 us  [swap(): return lax.ppermute(a, axis, [(i, i ^ mask) for i in range(size)])]
    all_to_all x3 -> x2, starting transfers between devices: 26.9 us -> 18.4 us  [the longest x1 12.1 us: local(): got = [exchange(sent[0])]]
    unnamed x25 -> x28, local copies, waits for them, and re-layouts: 7.61 us -> 9.82 us
    all_to_all x3 -> x2, waiting for transfers between devices: 8.76 us -> 10.1 us  [the longest x1 10.1 us: local(): got = [exchange(sent[0])]]
    pallas_call x6 -> x7, Pallas kernels: 31.9 us -> 30.9 us  [the longest x1 11.4 us: first_part(): pl.pallas_call(functools.partial(first_kernel, head_dim=head_dim), out_sh...]
  transfers between devices with their start and end apart: 15 -> 4, of which waited for: 10 -> 2; matrix products, arithmetic and copies ran while one was open for 4% -> 3% of each run, Pallas kernels for 11% -> 13%
where the time goes in v4:
time: 128 us; the launch traced here: 127 us
  blocking collectives  45.5 us (36%)
  Pallas kernels  32.2 us (25%)
  starting transfers between devices  24.5 us (19%)
  waiting for transfers between devices  11 us (9%)
  local copies, waits for them, and re-layouts  10.2 us (8%)
  matrix products  3.2 us (2%)
    all_to_all x1, blocking collectives, local(): back = exchange(back)  45.5 us
    all_to_all x1, starting transfers between devices, local(): got = [exchange(sent[0])]  12.1 us
    pallas_call x1, Pallas kernels, first_part(): pl.pallas_call(functools.partial(first_kernel, head_dim=head_dim), out_sh...  11.4 us
    all_to_all x1, waiting for transfers between devices, local(): got = [exchange(sent[0])]  10.1 us
    unnamed x28, local copies, waits for them, and re-layouts  9.82 us
    pallas_call x1, Pallas kernels, second_part(): pl.pallas_call(functools.partial(second_kernel, head_dim=head_dim), out_s...  9.75 us
    all_to_all x1, starting transfers between devices, local(): got.append(exchange(sent[1]))  6.34 us
    ppermute x2, starting transfers between devices, swap(): return lax.ppermute(a, axis, [(i, i ^ mask) for i in range(size)])  6.02 us
  transfers between devices with their start and end apart: 4, of which 2 were waited for; matrix products, arithmetic and copies ran while one was open for 3% of the time, Pallas kernels for 13%

profile of v4, /device:TPU:1, one launch (start us, length us, event | category | flops | bytes accessed | tf_op | source)
XLA Modules:
  0.0 127.4 jit_solution(11279144375127833719)
XLA Ops:
  0.6 2.0 %pair.2 = bf16[64,2,8,512]{3,2,1,0:T(8,128)(2,1)} custom-call(bf16[2,64,8,512]{3,2,1,0:T(8,128)(2,1)} %bitcast.28, bf16[2,64,8,512]{3,2,1,0:T(8,128)(2,1)} %bitcast.20), custom_call_target="tpu_custom_call" | custom-call | bytes 2097152 | tf_op jit(solution)/shard_map/pair/pallas_call | solution.py:383
  2.7 12.1 %all-to-all-start = ((bf16[64,2,8,512]{3,2,1,0:T(8,128)(2,1)}), bf16[64,2,8,512]{3,2,1,0:T(8,128)(2,1)S(1)}, u32[]{:S(2)}, u32[]{:S(2)}) async-start(bf16[64,2,8,512]{3,2,1,0:T(8,128)(2,1)} %pair.2), calls=%async_computation | async-start | bytes 2097152 | tf_op jit(solution)/shard_map/all_to_all | solution.py:539
  14.8 2.1 %pair.3 = bf16[64,2,8,512]{3,2,1,0:T(8,128)(2,1)} custom-call(bf16[2,64,8,512]{3,2,1,0:T(8,128)(2,1)} %bitcast.29, bf16[2,64,8,512]{3,2,1,0:T(8,128)(2,1)} %bitcast.21), custom_call_target="tpu_custom_call" | custom-call | bytes 2097152 | tf_op jit(solution)/shard_map/pair/pallas_call | solution.py:383
  17.0 3.2 %fusion.4 = f32[4,64,4,64]{3,2,0,1:T(4,128)S(1)} fusion(f32[4,4,225,1]{2,1,0,3:T(4,128)S(1)} %reshape.220, s32[64,64]{1,0:T(8,128)S(1)} %add_add_fusion), kind=kOutput, calls=%fused_computation.4 | convolution fusion | flops 177868800 | bytes 292928 | tf_op jit(solution)/shard_map/bhr,kqr->bkhq/dot_general | solution.py:529
  20.6 10.1 %all-to-all-done.pair_ref = bf16[64,2,8,512]{3,2,1,0:T(8,128)(2,1)S(1)} async-done(((bf16[64,2,8,512]{3,2,1,0:T(8,128)(2,1)}), bf16[64,2,8,512]{3,2,1,0:T(8,128)(2,1)S(1)}, u32[]{:S(2)}, u32[]{:S(2)}) %all-to-all-start) | async-done | bytes 1048608 | tf_op jit(solution)/shard_map/all_to_all | solution.py:539
  30.7 6.3 %all-to-all-start.1 = ((bf16[64,2,8,512]{3,2,1,0:T(8,128)(2,1)}), bf16[64,2,8,512]{3,2,1,0:T(8,128)(2,1)S(1)}, u32[]{:S(2)}, u32[]{:S(2)}) async-start(bf16[64,2,8,512]{3,2,1,0:T(8,128)(2,1)} %pair.3), calls=%async_computation.1 | async-start | bytes 2097152 | tf_op jit(solution)/shard_map/all_to_all | solution.py:541
  37.1 1.4 %copy-done.2 = bf16[512,1536]{1,0:T(8,128)(2,1)S(1)} copy-done((bf16[512,1536]{1,0:T(8,128)(2,1)S(1)}, bf16[512,1536]{1,0:T(8,128)(2,1)}, u32[]{:S(2)}) %copy-start.2) | copy-done | bytes 1572888
  38.5 11.4 %first_part.1 = (bf16[64,8,512]{2,1,0:T(8,128)(2,1)S(1)}, f32[512,2048]{1,0:T(8,128)S(1)}, f32[4,64,256]{2,1,0:T(8,128)S(1)}, f32[2,512]{1,0:T(2,128)S(1)}) custom-call(bf16[64,2,8,512]{3,2,1,0:T(8,128)(2,1)S(1)} %all-to-all-done.pair_ref, bf16[512,1536]{1,0:T(8,128)(2,1)S(1)} %copy-done.2, bf16[512,512]{1,0:T(8,128)(2,1)S(1)} %copy-done.5, ...), custom_call_target="tpu_custom_call" | custom-call | flops 10000000000 | bytes 8388608 | tf_op jit(solution)/shard_map/first_part/pallas_call | solution.py:315
  49.9 1.9 %copy-done.8 = f32[512,2048]{1,0:T(8,128)} copy-done((f32[512,2048]{1,0:T(8,128)}, f32[512,2048]{1,0:T(8,128)S(1)}, u32[]{:S(2)}) %copy-start.8) | copy-done | bytes 4194328
  51.9 0.7 copy-done.10
  52.6 1.4 %copy-done.3 = bf16[512,1536]{1,0:T(8,128)(2,1)S(1)} copy-done((bf16[512,1536]{1,0:T(8,128)(2,1)S(1)}, bf16[512,1536]{1,0:T(8,128)(2,1)}, u32[]{:S(2)}) %copy-start.3) | copy-done | bytes 1572888
  54.0 2.2 %copy-done.9 = f32[512,2048]{1,0:T(8,128)S(1)} copy-done((f32[512,2048]{1,0:T(8,128)S(1)}, f32[512,2048]{1,0:T(8,128)}, u32[]{:S(2)}) %copy-start.9) | copy-done | bytes 4194328
  56.2 0.9 copy-done.11
  57.1 9.8 %second_part.1 = (f32[512,1024]{1,0:T(8,128)S(1)}, bf16[512,1024]{1,0:T(8,128)(2,1)S(1)}, f32[4,64,256]{2,1,0:T(8,128)S(1)}, bf16[512,1536]{1,0:T(8,128)(2,1)S(1...) custom-call(s32[1]{0:T(128)} %bitcast.core_ref, bf16[64,2,8,512]{3,2,1,0:T(8,128)(2,1)S(1)} %all-to-all-done.1.pair_ref, ...), custom_call_target="tpu_custom_call" | custom-call | flops 10000000000 | bytes 8388608 | tf_op jit(solution)/shard_map/second_part/pallas_call | solution.py:338
  66.9 3.9 %collective-permute-start = (bf16[512,1024]{1,0:T(8,128)(2,1)S(1)}, bf16[512,1024]{1,0:T(8,128)(2,1)S(1)}, u32[]{:S(2)}, u32[]{:S(2)}) collective-permute-start(bf16[512,1024]{1,0:T(8,128)(2,1)S(1)} %get-tuple-element.42), channel_id=1, source_target_pairs={{0,1},{1,0},{2,3},{3,2},{4,5},{5,4},{6,7},{7,6},{8,9},{9,8},{10,11... | collective-permute-start | bytes 3145736 | tf_op jit(solution)/shard_map/ppermute | solution.py:518
  70.8 3.6 %second_back.1 = (bf16[64,8,512]{2,1,0:T(8,128)(2,1)S(1)}, f32[40,128]{1,0:T(8,128)S(1)}) custom-call(bf16[512,1536]{1,0:T(8,128)(2,1)S(1)} %copy-done.4, f32[1,512]{1,0:T(1,128)S(1)} %bitcast.27, bf16[512,1536]{1,0:T(8,128)(2,1)S(1)} %get-tuple-element.35.gproj, f32[4,512,128]{2,1,0:T(8,128)S(1)} %get-tuple-element.36.hat, ...), custom_call_target="tpu_custom_call" | custom-call | flops 4000000000 | bytes 4194304 | tf_op jit(solution)/shard_map/second_back/pallas_call | solution.py:358
  74.4 0.5 outgoing.1
  74.9 45.5 %all_to_all.15.got_ref = bf16[64,21,8,128]{3,2,1,0:T(8,128)(2,1)S(1)} all-to-all(bf16[64,21,8,128]{3,2,1,0:T(8,128)(2,1)S(1)} %outgoing.1), channel_id=1, replica_groups=mesh['x_lo'=2,'y'=4,'x_hi'=2,'z'=4,'core'=2] {'x_lo','y','x_hi','z'}, dimensions={0} | all-to-all | bytes 5505024 | tf_op jit(solution)/shard_map/all_to_all | solution.py:549
  120.4 1.3 final.1
  121.7 0.6 copy-done.1
  122.3 2.2 %collective-permute-start.1 = (f32[72,128]{1,0:T(8,128)S(1)}, f32[72,128]{1,0:T(8,128)S(1)}, u32[]{:S(2)}, u32[]{:S(2)}) collective-permute-start(f32[72,128]{1,0:T(8,128)S(1)} %get-tuple-element.46), channel_id=1, source_target_pairs={{0,1},{1,0},{2,3},{3,2},{4,5},{5,4},{6,7},{7,6},{8,9},{9,8},{10,11... | collective-permute-start | bytes 110600 | tf_op jit(solution)/shard_map/ppermute | solution.py:518
  124.5 0.9 collective-permute-done.1.recv_ref
  125.3 0.6 copy-done.12
  126.0 1.5 %finish.1 = (f32[4,1536]{1,0:T(4,128)}, f32[4,512]{1,0:T(4,128)}, f32[16,225]{1,0:T(8,128)}, f32[1,512]{1,0:T(1,128)}, f32[1,512]{1,0:T(1,128)}) custom-call(s32[1]{0:T(128)} %bitcast.core_ref, f32[72,128]{1,0:T(8,128)} %copy-done.1, f32[72,128]{1,0:T(8,128)} %copy-done.12), custom_call_target="tpu_custom_call" | custom-call | tf_op jit(solution)/shard_map/finish/pallas_call | solution.py:490
  (27 shorter events, 0.5 us)
Async XLA Ops:
  2.7 14.2 %copy-start.13 = (f32[16,225]{1,0:T(8,128)S(1)}, f32[16,225]{1,0:T(8,128)}, u32[]{:S(2)}) copy-start(f32[16,225]{1,0:T(8,128)} %param.11) | copy-start | bytes 43204
  2.7 28.1 %all-to-all-start = ((bf16[64,2,8,512]{3,2,1,0:T(8,128)(2,1)}), bf16[64,2,8,512]{3,2,1,0:T(8,128)(2,1)S(1)}, u32[]{:S(2)}, u32[]{:S(2)}) async-start(bf16[64,2,8,512]{3,2,1,0:T(8,128)(2,1)} %pair.2), calls=%async_computation | async-start | bytes 2097152 | tf_op jit(solution)/shard_map/all_to_all | solution.py:539
  16.9 20.2 %copy-start.5 = (bf16[512,512]{1,0:T(8,128)(2,1)S(1)}, bf16[512,512]{1,0:T(8,128)(2,1)}, u32[]{:S(2)}) copy-start(bf16[512,512]{1,0:T(8,128)(2,1)} %wout_hbm.3) | copy-start | bytes 1572868
  16.9 20.2 %copy-start.6 = (f32[512]{0:T(512)S(1)}, f32[512]{0:T(512)}, u32[]{:S(2)}) copy-start(f32[512]{0:T(512)} %param.13) | copy-start | bytes 6148
  16.9 20.2 %copy-start.7 = (f32[512]{0:T(512)S(1)}, f32[512]{0:T(512)}, u32[]{:S(2)}) copy-start(f32[512]{0:T(512)} %param.12) | copy-start | bytes 6148
  30.7 21.8 %all-to-all-start.1 = ((bf16[64,2,8,512]{3,2,1,0:T(8,128)(2,1)}), bf16[64,2,8,512]{3,2,1,0:T(8,128)(2,1)S(1)}, u32[]{:S(2)}, u32[]{:S(2)}) async-start(bf16[64,2,8,512]{3,2,1,0:T(8,128)(2,1)} %pair.3), calls=%async_computation.1 | async-start | bytes 2097152 | tf_op jit(solution)/shard_map/all_to_all | solution.py:541
  37.1 1.4 %copy-start.2 = (bf16[512,1536]{1,0:T(8,128)(2,1)S(1)}, bf16[512,1536]{1,0:T(8,128)(2,1)}, u32[]{:S(2)}) copy-start(bf16[512,1536]{1,0:T(8,128)(2,1)} %wqkv_hbm.5) | copy-start | bytes 4718596
  49.9 1.9 %copy-start.8 = (f32[512,2048]{1,0:T(8,128)}, f32[512,2048]{1,0:T(8,128)S(1)}, u32[]{:S(2)}) copy-start(f32[512,2048]{1,0:T(8,128)S(1)} %get-tuple-element.33.sums_hbm) | copy-start | bytes 12582916
  51.9 0.7 copy-start.10
  52.6 1.4 %copy-start.3 = (bf16[512,1536]{1,0:T(8,128)(2,1)S(1)}, bf16[512,1536]{1,0:T(8,128)(2,1)}, u32[]{:S(2)}) copy-start(bf16[512,1536]{1,0:T(8,128)(2,1)} %wqkv_hbm.5) | copy-start | bytes 4718596
  54.0 2.2 %copy-start.9 = (f32[512,2048]{1,0:T(8,128)S(1)}, f32[512,2048]{1,0:T(8,128)}, u32[]{:S(2)}) copy-start(f32[512,2048]{1,0:T(8,128)} %copy-done.8) | copy-start | bytes 12582916
  56.2 0.9 copy-start.11
  57.1 13.6 %copy-start.4 = (bf16[512,1536]{1,0:T(8,128)(2,1)S(1)}, bf16[512,1536]{1,0:T(8,128)(2,1)}, u32[]{:S(2)}) copy-start(bf16[512,1536]{1,0:T(8,128)(2,1)} %wqkv_hbm.5) | copy-start | bytes 4718596
  66.9 7.5 %collective-permute-start = (bf16[512,1024]{1,0:T(8,128)(2,1)S(1)}, bf16[512,1024]{1,0:T(8,128)(2,1)S(1)}, u32[]{:S(2)}, u32[]{:S(2)}) collective-permute-start(bf16[512,1024]{1,0:T(8,128)(2,1)S(1)} %get-tuple-element.42), channel_id=1, source_target_pairs={{0,1},{1,0},{2,3},{3,2},{4,5},{5,4},{6,7},{7,6},{8,9},{9,8},{10,11... | collective-permute-start | bytes 3145736 | tf_op jit(solution)/shard_map/ppermute | solution.py:518
  74.9 45.6 %copy-start = (bf16[16,64,512]{2,1,0:T(8,128)(2,1)S(1)}, bf16[16,64,512]{2,1,0:T(8,128)(2,1)}, u32[]{:S(2)}) copy-start(bf16[16,64,512]{2,1,0:T(8,128)(2,1)} %param.8) | copy-start | bytes 3145732
  121.7 0.6 copy-start.1
  122.3 3.0 %collective-permute-start.1 = (f32[72,128]{1,0:T(8,128)S(1)}, f32[72,128]{1,0:T(8,128)S(1)}, u32[]{:S(2)}, u32[]{:S(2)}) collective-permute-start(f32[72,128]{1,0:T(8,128)S(1)} %get-tuple-element.46), channel_id=1, source_target_pairs={{0,1},{1,0},{2,3},{3,2},{4,5},{5,4},{6,7},{7,6},{8,9},{9,8},{10,11... | collective-permute-start | bytes 110600 | tf_op jit(solution)/shard_map/ppermute | solution.py:518
  125.3 0.6 copy-start.12

commit v5 on v4

v5 whole, which is shorter than its diff:
```python
import functools
import jax
import jax.numpy as jnp
from jax import lax
from jax.experimental import pallas as pl
from jax.experimental.pallas import tpu as pltpu
from jax.sharding import Mesh, PartitionSpec as P

GRID = 8
EPSILON = 1e-05
MEMBERS = GRID * GRID
PACK = 4
CHUNK = 256


def dot(a, b, ca, cb):
    return lax.dot_general(a, b, (((ca,), (cb,)), ((), ())), preferred_element_type=jnp.float32)


def put(ref, at, value):
    for b in range(ref.shape[0]):
        ref[b, at, :] = value[:, b * 128 : (b + 1) * 128]


def take(ref, at):
    return jnp.concatenate([ref[b, at, :] for b in range(ref.shape[0])], axis=1)


def forward_and_scores(
    pair_ref, wqkv_ref, wout_ref, bias_ref, gain_ref, shift_ref, gbias_ref,
    normed, gproj, att, dyp, hat, istd, proj, gatt, dyf, head_dim,
):
    width = gproj.shape[1] // 3
    rows, groups, chunk = gproj.shape[0], gproj.shape[0] // MEMBERS, CHUNK
    per, mem = chunk // MEMBERS, chunk // groups
    bf16, f32 = jnp.bfloat16, jnp.float32
    scale = head_dim ** (-0.5)

    def hat_step(c, carry):
        here = pl.ds(pl.multiple_of(c * chunk, chunk), chunk)
        pair = pair_ref[pl.ds(pl.multiple_of(c * mem, mem), mem)].astype(f32)
        x = pair[:, 0].reshape(chunk, width)
        centred = x - jnp.mean(x, axis=-1, keepdims=True)
        inv = lax.rsqrt(jnp.mean(centred * centred, axis=-1, keepdims=True) + EPSILON)
        put(hat, here, centred * inv)
        istd[here, :] = jnp.broadcast_to(inv, (chunk, 128))
        put(dyf, here, pair[:, 1].reshape(chunk, width))
        return carry

    lax.fori_loop(0, rows // chunk, hat_step, 0)

    def by_group(ref, c):
        return jnp.concatenate(
            [take(ref, pl.ds(c * per + g, MEMBERS, stride=groups)) for g in range(per)], axis=0
        )

    def norm_step(c, carry):
        here = pl.ds(pl.multiple_of(c * chunk, chunk), chunk)
        nb = (by_group(hat, c) * gain_ref[...] + shift_ref[...]).astype(bf16)
        dy = by_group(dyf, c).astype(bf16)
        dyp[here, :] = dy
        normed[here, :] = nb
        proj[here, :] = dot(nb, wqkv_ref[...], 1, 0).astype(bf16)
        gatt[here, :] = dot(dy, wout_ref[...], 1, 1).astype(bf16)
        return carry

    lax.fori_loop(0, rows // chunk, norm_step, 0, unroll=True)

    lane = lax.broadcasted_iota(jnp.int32, (MEMBERS, 128), 1) // head_dim

    def spread(a):
        zero = jnp.zeros_like(a)
        return jnp.concatenate([jnp.where(lane == h, a, zero) for h in range(PACK)], axis=0)

    def gather(a):
        out = a[:MEMBERS]
        for h in range(1, PACK):
            out = jnp.where(lane == h, a[h * MEMBERS : (h + 1) * MEMBERS], out)
        return out

    blocks = range(width // 128)

    def group_step(g, carry):
        here = pl.ds(pl.multiple_of(g * MEMBERS, MEMBERS), MEMBERS)
        cols = [slice(b * 128, (b + 1) * 128) for b in blocks]
        kcols = [slice(width + b * 128, width + (b + 1) * 128) for b in blocks]
        vcols = [slice(2 * width + b * 128, 2 * width + (b + 1) * 128) for b in blocks]
        ks = [proj[here, c] for c in kcols]
        vs = [proj[here, c] for c in vcols]
        none = jnp.zeros_like(ks[0])
        ws = [jnp.concatenate([spread(proj[here, c]), spread(gatt[here, c])], axis=1) for c in cols]
        both = [
            dot(
                jnp.concatenate(
                    [jnp.concatenate([k, none], axis=1), jnp.concatenate([none, v], axis=1)], axis=0
                ),
                w, 1, 1,
            )
            for k, v, w in zip(ks, vs, ws)
        ]
        pds = []
        for b in blocks:
            scores = both[b][:MEMBERS] * scale + bias_ref[b]
            gp = both[b][MEMBERS:]
            e = jnp.exp(scores - jnp.max(scores, axis=0, keepdims=True))
            p = e * (1.0 / jnp.sum(e, axis=0, keepdims=True))
            gs = p * (gp - jnp.sum(gp * p, axis=0, keepdims=True))
            gbias_ref[b] += gs
            pds.append(jnp.concatenate([p.astype(bf16), (gs * scale).astype(bf16)], axis=0))
        keyed = [dot(pd, w, 1, 0) for pd, w in zip(pds, ws)]
        queried = [
            dot(
                pd,
                jnp.concatenate(
                    [jnp.concatenate([v, none], axis=1), jnp.concatenate([none, k], axis=1)], axis=0
                ),
                0, 0,
            )
            for k, v, pd in zip(ks, vs, pds)
        ]
        for b in blocks:
            att[here, cols[b]] = gather(queried[b][:, :128]).astype(bf16)
            gproj[here, cols[b]] = gather(queried[b][:, 128:]).astype(bf16)
            gproj[here, kcols[b]] = keyed[b][MEMBERS:, :128].astype(bf16)
            gproj[here, vcols[b]] = keyed[b][:MEMBERS, 128:].astype(bf16)
        return carry

    lax.fori_loop(0, groups, group_step, 0, unroll=4)


def back_to_input(wqkv_ref, gain_ref, branch_ref, gproj, hat, istd, dyf):
    width = gproj.shape[1] // 3
    rows, groups, chunk = gproj.shape[0], gproj.shape[0] // MEMBERS, CHUNK
    per, mem = chunk // MEMBERS, chunk // groups
    bf16, f32 = jnp.bfloat16, jnp.float32

    def gn_step(c, carry):
        here = pl.ds(pl.multiple_of(c * chunk, chunk), chunk)
        gn = dot(gproj[here, :], wqkv_ref[...], 1, 1)
        for g in range(per):
            put(dyf, pl.ds(c * per + g, MEMBERS, stride=groups), gn[g * MEMBERS : (g + 1) * MEMBERS])
        return carry

    lax.fori_loop(0, rows // chunk, gn_step, 0, unroll=True)

    def back_step(c, carry):
        gg, gsh = carry
        here = pl.ds(pl.multiple_of(c * chunk, chunk), chunk)
        gn = take(dyf, here)
        normalized = take(hat, here)
        prod = gn * normalized
        gg = gg + jnp.sum(prod.reshape(chunk // 8, 8, width), axis=0)
        gsh = gsh + jnp.sum(gn.reshape(chunk // 8, 8, width), axis=0)
        gh = gn * gain_ref[...]
        m1 = jnp.mean(gh, axis=-1, keepdims=True)
        m2 = jnp.mean(prod * gain_ref[...], axis=-1, keepdims=True)
        inv = istd[here, :][:, :1]
        branch = (inv * (gh - m1 - normalized * m2)).astype(bf16)
        branch_ref[pl.ds(pl.multiple_of(c * mem, mem), mem)] = branch.reshape(mem, groups, width)
        return gg, gsh

    zero = jnp.zeros((8, width), f32)
    gg, gsh = lax.fori_loop(0, rows // chunk, back_step, (zero, zero))
    return jnp.sum(gg, axis=0, keepdims=True), jnp.sum(gsh, axis=0, keepdims=True)


def offset_sums(gbias_ref):
    f32, bf16 = jnp.float32, jnp.bfloat16
    blocks, members, lanes = gbias_ref.shape
    i = lax.broadcasted_iota(jnp.int32, (lanes, 2 * lanes), 0)
    o = lax.broadcasted_iota(jnp.int32, (lanes, 2 * lanes), 1)
    query = i % members
    place = (i // members) * 128 + query // GRID * 16 + query % GRID
    wide = (o == place).astype(f32).astype(bf16)
    frames = []
    for b in range(blocks):
        value = gbias_ref[b]
        high = value.astype(bf16)
        rest = value - high.astype(f32)
        low = rest.astype(bf16)
        lowest = (rest - low.astype(f32)).astype(bf16)
        spread = dot(jnp.concatenate([high, low, lowest], axis=0), wide, 1, 0)
        spread = spread[:members] + (spread[members : 2 * members] + spread[2 * members :])
        frames += [spread[None, :, h * 128 : (h + 1) * 128] for h in range(PACK)]
    frame = jnp.concatenate(frames, axis=0)
    heads = frame.shape[0]
    frame = jnp.concatenate([frame, jnp.zeros_like(frame)], axis=2).reshape(heads * members, 256)
    column = GRID - 1 - lax.broadcasted_iota(jnp.int32, frame.shape, 0) % GRID
    for bit in (1, 2, 4):
        frame = jnp.where((column & bit) != 0, pltpu.roll(frame, bit, 1), frame)
    frame = jnp.sum(frame.reshape(heads * GRID, GRID, 256), axis=1)
    row = GRID - 1 - lax.broadcasted_iota(jnp.int32, frame.shape, 0) % GRID
    for bit in (1, 2, 4):
        frame = jnp.where((row & bit) != 0, pltpu.roll(frame, 16 * bit, 1), frame)
    return jnp.sum(frame.reshape(heads, GRID, 256), axis=1)


def scores_kernel(
    core_ref, pair_ref, wqkv_ref, wout_ref, bias_ref, gain_ref, shift_ref,
    keep_ref, send_ref, table_ref, gproj, hat, istd,
    gbias_ref, normed, att, dyp, proj, gatt, dyf, *, head_dim,
):
    gbias_ref[...] = jnp.zeros_like(gbias_ref)
    forward_and_scores(
        pair_ref, wqkv_ref, wout_ref, bias_ref, gain_ref, shift_ref, gbias_ref,
        normed, gproj, att, dyp, hat, istd, proj, gatt, dyf, head_dim,
    )
    width = wout_ref.shape[0]
    half = 2 * width
    first = core_ref[0] == 0
    table = offset_sums(gbias_ref)
    heads = table.shape[0] // 2
    table_ref[...] = jnp.where(first, table[:heads], table[heads:])
    send_ref[width:, :] = jnp.zeros((send_ref.shape[0] - width, half), send_ref.dtype)
    send_ref[width : width + heads, :256] = jnp.where(first, table[heads:], table[:heads]).astype(send_ref.dtype)

    @pl.when(first)
    def _():
        keep_ref[...] = dot(normed[...], gproj[:, :half], 0, 0)
        send_ref[:width, :width] = dot(normed[...], gproj[:, half:], 0, 0).astype(send_ref.dtype)
        send_ref[:width, width:] = dot(att[...], dyp[...], 0, 0).astype(send_ref.dtype)

    @pl.when(jnp.logical_not(first))
    def _():
        send_ref[:width, :] = dot(normed[...], gproj[:, :half], 0, 0).astype(send_ref.dtype)
        keep_ref[:, :width] = dot(normed[...], gproj[:, half:], 0, 0)
        keep_ref[:, width:] = dot(att[...], dyp[...], 0, 0)


def back_kernel(wqkv_ref, gain_ref, gproj, hat, istd, branch_ref, gvec_ref, dyf):
    sums = back_to_input(wqkv_ref, gain_ref, branch_ref, gproj, hat, istd, dyf)
    lanes = hat.shape[0]
    for i in range(2):
        for b in range(lanes):
            gvec_ref[i * lanes + b : i * lanes + b + 1, :] = sums[i][:, b * 128 : (b + 1) * 128]


VMEM = pl.BlockSpec(memory_space=pltpu.VMEM)
SMEM = pl.BlockSpec(memory_space=pltpu.SMEM)
MIB = 1024 * 1024


def shaped(*shape, dtype=jnp.float32):
    return jax.ShapeDtypeStruct(shape, dtype)


def cost(flops, size):
    return pl.CostEstimate(flops=flops, bytes_accessed=size, transcendentals=0)


def part_buffers(rows, width):
    bf16, f32 = jnp.bfloat16, jnp.float32
    tall, lanes = (rows, width), (width // 128, rows, 128)
    return [
        (tall, bf16), ((rows, 3 * width), bf16), (tall, bf16), (tall, bf16), (lanes, f32), ((rows, 128), f32),
        ((rows, 3 * width), bf16), (tall, bf16), (lanes, f32),
    ]


def local_scores(core, pair, wqkv, wout, bias, gain, shift, head_dim):
    members, _, groups, width = pair.shape
    bf16, f32 = jnp.bfloat16, jnp.float32
    normed, gproj, att, dyp, hat, istd, proj, gatt, dyf = part_buffers(groups * MEMBERS, width)
    half_heads = width // head_dim // 2
    return pl.pallas_call(
        functools.partial(scores_kernel, head_dim=head_dim),
        out_shape=(
            shaped(width, 2 * width), shaped(width + 16, 2 * width, dtype=bf16), shaped(half_heads, 256)
        )
        + tuple(jax.ShapeDtypeStruct(*b) for b in (gproj, hat, istd)),
        in_specs=[SMEM] + [VMEM] * 6,
        out_specs=(VMEM,) * 6,
        scratch_shapes=[pltpu.VMEM(bias.shape, f32)]
        + [pltpu.VMEM(*b) for b in (normed, att, dyp, proj, gatt, dyf)],
        compiler_params=pltpu.CompilerParams(vmem_limit_bytes=28 * MIB),
        cost_estimate=cost(20_000_000_000, 8 << 20),
        name="scores",
    )(core.reshape(1), pair, wqkv, wout, bias, gain.reshape(1, width), shift.reshape(1, width))


def local_back(wqkv, gain, gproj, hat, istd, groups):
    width = gain.shape[0]
    return pl.pallas_call(
        back_kernel,
        out_shape=(shaped(MEMBERS, groups, width, dtype=gproj.dtype), shaped(2 * width // 128, 128)),
        in_specs=[VMEM] * 5,
        out_specs=(VMEM,) * 2,
        scratch_shapes=[pltpu.VMEM(hat.shape, jnp.float32)],
        compiler_params=pltpu.CompilerParams(vmem_limit_bytes=16 * MIB),
        cost_estimate=cost(6_000_000_000, 4 << 20),
        name="back",
    )(wqkv, gain.reshape(1, width), gproj, hat, istd)


def pair_kernel(x_ref, dy_ref, out_ref):
    out_ref[:, 0] = x_ref[...]
    out_ref[:, 1] = dy_ref[...]


def pair_of(x, dy):
    chips, groups, width = x.shape
    step = chips // 4
    source = pl.BlockSpec((step, groups, width), lambda i: (i, 0, 0))
    return pl.pallas_call(
        pair_kernel,
        grid=(chips // step,),
        out_shape=shaped(chips, 2, groups, width, dtype=x.dtype),
        in_specs=[source, source],
        out_specs=pl.BlockSpec((step, 2, groups, width), lambda i: (i, 0, 0, 0)),
        cost_estimate=cost(0, 4 << 20),
        name="pair",
    )(x, dy)


def outgoing_kernel(branch_ref, keep_ref, recv_ref, table_ref, gvec_ref, out_ref):
    chips, _, share, _ = out_ref.shape
    _, groups, width = branch_ref.shape
    f32, bf16 = jnp.float32, jnp.bfloat16
    slot = 0
    for b in range(width // 128):
        for t in range(groups // share):
            out_ref[:, slot] = branch_ref[:, t * share : (t + 1) * share, b * 128 : (b + 1) * 128]
            slot += 1
    for b in range(2 * width // 128):
        cols = slice(b * 128, (b + 1) * 128)
        total = (keep_ref[:, cols] + recv_ref[:width, cols].astype(f32)).astype(bf16)
        out_ref[:, slot] = total.reshape(chips, share, 128)
        slot += 1
    table = table_ref[...] + recv_ref[width : width + share, :256].astype(f32)
    for value in (table[:, :128], table[:, 128:], gvec_ref[...]):
        out_ref[:, slot] = jnp.broadcast_to(value.astype(bf16)[None], (chips, share, 128))
        slot += 1


def outgoing(branch, keep, recv, table, gvec):
    chips, groups, width = branch.shape
    share = width // chips
    slots = groups // share * width // 128 + 2 * width // 128 + 3
    return pl.pallas_call(
        outgoing_kernel,
        out_shape=shaped(chips, slots, share, 128, dtype=branch.dtype),
        in_specs=[VMEM] * 5,
        out_specs=VMEM,
        compiler_params=pltpu.CompilerParams(vmem_limit_bytes=16 * MIB),
        cost_estimate=cost(0, 6 << 20),
        name="outgoing",
    )(branch, keep, recv, table, gvec)


def sums_kernel(core_ref, got_ref, keep_ref, send_ref, *, begin, factor):
    f32 = jnp.float32
    chips, slots, share, _ = got_ref.shape
    total = got_ref[0, begin:].astype(f32)
    for chip in range(1, chips):
        total = total + got_ref[chip, begin:].astype(f32)
    total = total * factor
    part = share // 2
    weights = slots - begin - 3
    for b in range(weights):
        rows = slice(b * part, (b + 1) * part)
        low, high = total[b, :part], total[b, part:]
        keep_ref[rows, :] = jnp.where(core_ref[0] == 0, low, high)
        send_ref[rows, :] = jnp.where(core_ref[0] == 0, high, low)
    for i in range(3):
        rows = slice(weights * part + i * share, weights * part + (i + 1) * share)
        keep_ref[rows, :] = total[weights + i]
        send_ref[rows, :] = total[weights + i]


def sums_of(core, got, begin, factor):
    chips, slots, share, _ = got.shape
    rows = (slots - begin - 3) * share // 2 + 3 * share
    return pl.pallas_call(
        functools.partial(sums_kernel, begin=begin, factor=factor),
        out_shape=(shaped(rows, 128), shaped(rows, 128)),
        in_specs=[SMEM, VMEM],
        out_specs=(VMEM,) * 2,
        compiler_params=pltpu.CompilerParams(vmem_limit_bytes=16 * MIB),
        cost_estimate=cost(0, 2 << 20),
        name="sums",
    )(core.reshape(1), got)


def input_kernel(got_ref, dy_ref, grad_ref):
    _, groups, width = dy_ref.shape
    share = got_ref.shape[2]
    f32 = jnp.float32
    slot = 0
    for b in range(width // 128):
        cols = slice(b * 128, (b + 1) * 128)
        for t in range(groups // share):
            rows = slice(t * share, (t + 1) * share)
            branch = got_ref[:, slot].astype(f32)
            grad_ref[:, rows, cols] = (dy_ref[:, rows, cols].astype(f32) + branch).astype(grad_ref.dtype)
            slot += 1


def input_gradient(got, dy):
    return pl.pallas_call(
        input_kernel,
        out_shape=jax.ShapeDtypeStruct(dy.shape, dy.dtype),
        in_specs=[VMEM] * 2,
        out_specs=VMEM,
        compiler_params=pltpu.CompilerParams(vmem_limit_bytes=16 * MIB),
        cost_estimate=cost(0, 4 << 20),
        name="input_gradient",
    )(got, dy)


def finish_kernel(core_ref, keep_ref, recv_ref, qkv_ref, out_ref, table_ref, gain_ref, shift_ref):
    width = out_ref.shape[1]
    lanes = width // 128
    part, heads = out_ref.shape[0], table_ref.shape[0] // 2
    first = core_ref[0] == 0

    def ordered(mine, other):
        return jnp.where(first, mine, other), jnp.where(first, other, mine)

    for b in range(2 * lanes):
        rows = slice(b * part, (b + 1) * part)
        low, high = ordered(keep_ref[rows, :], recv_ref[rows, :])
        qkv_ref[:, b * 128 : (b + 1) * 128] = low
        if b < lanes:
            qkv_ref[:, 2 * width + b * 128 : 2 * width + (b + 1) * 128] = high
        else:
            out_ref[:, (b - lanes) * 128 : (b - lanes + 1) * 128] = high
    at = 2 * lanes * part
    halves = [jnp.concatenate([ref[at : at + heads], ref[at + heads : at + 2 * heads]], axis=1) for ref in (keep_ref, recv_ref)]
    table = jnp.concatenate(ordered(*halves), axis=0)
    side = 2 * GRID - 1
    place = lax.broadcasted_iota(jnp.int32, (256, side * side), 0)
    offset = lax.broadcasted_iota(jnp.int32, (256, side * side), 1)
    pick = (place == offset // side * 16 + offset % side).astype(jnp.float32)
    table_ref[...] = lax.dot_general(
        table, pick, (((1,), (0,)), ((), ())), precision=lax.Precision.HIGHEST, preferred_element_type=jnp.float32
    )
    at += 2 * heads
    vectors = keep_ref[at:, :] + recv_ref[at:, :]
    for ref, row in ((gain_ref, 0), (shift_ref, lanes)):
        for b in range(lanes):
            ref[:, b * 128 : (b + 1) * 128] = vectors[row + b : row + b + 1]


def finish(core, keep, recv, part, width, heads, offsets):
    return pl.pallas_call(
        finish_kernel,
        out_shape=(
            shaped(part, 3 * width), shaped(part, width), shaped(heads, offsets), shaped(1, width), shaped(1, width)
        ),
        in_specs=[SMEM, VMEM, VMEM],
        out_specs=(VMEM,) * 5,
        name="finish",
    )(core.reshape(1), keep, recv)


AXES = ("x_lo", "y", "x_hi", "z", "core")
CHIPS = AXES[:4]


def relative_onehot(members):
    span = 2 * GRID - 1
    second = jnp.arange(members, dtype=jnp.int32)[:, None]
    first = jnp.arange(members, dtype=jnp.int32)[None, :]
    row_delta = first // GRID - second // GRID + GRID - 1
    col_delta = first % GRID - second % GRID + GRID - 1
    rel_index = row_delta * span + col_delta
    offsets = jnp.arange(span * span, dtype=jnp.int32)
    return (rel_index[:, :, None] == offsets).astype(jnp.float32)


def swap(a, axis, mask):
    size = lax.axis_size(axis)
    return lax.ppermute(a, axis, [(i, i ^ mask) for i in range(size)])


def local(block_input, cotangent, qkv_weight, out_weight, bias_table, norm_gain, norm_shift):
    tile_h, tile_w, width = block_input.shape
    heads, offsets = bias_table.shape
    chips = lax.axis_size(CHIPS)
    devices = chips * lax.axis_size("core")
    owned = tile_h * tile_w // chips
    core = lax.axis_index("core")
    onehot = relative_onehot(MEMBERS)
    bias = jnp.einsum(
        "bhr,kqr->bkhq",
        bias_table.reshape(heads // PACK, PACK, offsets),
        onehot,
        precision=lax.Precision.HIGHEST,
    ).reshape(heads // PACK, MEMBERS, PACK * MEMBERS)
    x = block_input.reshape(chips, owned, width)
    dy = cotangent.reshape(chips, owned, width)
    exchange = functools.partial(lax.all_to_all, axis_name=CHIPS, split_axis=0, concat_axis=0, tiled=True)
    got = exchange(pair_of(x, dy))
    keep, send, table, gproj, hat, istd = local_scores(
        core, got, qkv_weight, out_weight, bias, norm_gain, norm_shift, width // heads
    )
    recv = swap(send, "core", 1)
    branch, gvec = local_back(qkv_weight, norm_gain, gproj, hat, istd, owned)
    got = exchange(outgoing(branch, keep, recv, table, gvec))
    factor = float(tile_h * tile_w * devices) ** (-0.5)
    share = width // chips
    mine, theirs = sums_of(core, got, owned // share * width // 128, factor)
    recv = swap(theirs, "core", 1)
    grad_input = input_gradient(got, dy)
    grad_qkv, grad_out, table, gain, shift = finish(core, mine, recv, share // 2, width, heads, offsets)
    return (
        grad_input.reshape(tile_h, tile_w, width),
        grad_qkv,
        grad_out,
        table,
        gain.reshape(width),
        shift.reshape(width),
    )


def solution(mesh):
    fine = Mesh(mesh.devices.reshape(2, 4, 2, 4, 2), AXES)
    tile = P(("x_lo", "y"), ("x_hi", "z", "core"), None)
    return jax.shard_map(
        local,
        mesh=fine,
        in_specs=(tile, tile, P(), P(), P(), P(), P()),
        out_specs=(tile, P(AXES, None), P(AXES, None), P(), P(), P()),
        check_vma=False,
    )
```

time: 128 us -> 118 us (0.922)
  waiting for transfers between devices: 11 us -> 21.5 us
  starting transfers between devices: 24.5 us -> 16.9 us
  local copies, waits for them, and re-layouts: 10.2 us -> 3.48 us
  blocking collectives: 45.5 us -> 41.9 us
  Pallas kernels: 32.2 us -> 28.9 us
    all_to_all x2 -> x1, waiting for transfers between devices: 10.1 us -> 21.5 us  [local(): got = exchange(pair_of(x, dy))]
    unnamed x28 -> x16, local copies, waits for them, and re-layouts: 9.82 us -> 2.04 us
    all_to_all x2 -> x1, starting transfers between devices: 18.4 us -> 12.1 us  [local(): got = exchange(pair_of(x, dy))]
    all_to_all x1, blocking collectives: 45.5 us -> 41.9 us  [local(): got = exchange(outgoing(branch, keep, recv, table, gvec))]
    pallas_call x8 -> x7, Pallas kernels: 32.2 us -> 28.9 us  [the longest x1 17.5 us: local_scores(): pl.pallas_call(functools.partial(scores_kernel, head_dim=head_dim), out_s...]
  transfers between devices with their start and end apart: 4 -> 3, of which waited for: 2 -> 1; matrix products, arithmetic and copies ran while one was open for 3% -> 5% of each run, Pallas kernels for 13% -> 5%
where the time goes in v5:
time: 118 us; the launch traced here: 117 us
  blocking collectives  41.9 us (36%)
  Pallas kernels  28.9 us (24%)
  waiting for transfers between devices  21.5 us (18%)
  starting transfers between devices  16.9 us (14%)
  matrix products  3.91 us (3%)
  local copies, waits for them, and re-layouts  3.48 us (3%)
    all_to_all x1, blocking collectives, local(): got = exchange(outgoing(branch, keep, recv, table, gvec))  41.9 us
    all_to_all x1, waiting for transfers between devices, local(): got = exchange(pair_of(x, dy))  21.5 us
    pallas_call x1, Pallas kernels, local_scores(): pl.pallas_call(functools.partial(scores_kernel, head_dim=head_dim), out_s...  17.5 us
    all_to_all x1, starting transfers between devices, local(): got = exchange(pair_of(x, dy))  12.1 us
    ppermute x2, starting transfers between devices, swap(): return lax.ppermute(a, axis, [(i, i ^ mask) for i in range(size)])  4.76 us
    pallas_call x1, Pallas kernels, local_back(): pl.pallas_call(back_kernel, out_shape=(shaped(MEMBERS, groups, width, dty...  4.02 us
    dot_general x1, matrix products, local(): jnp.einsum('bhr,kqr->bkhq', bias_table.reshape(heads // PACK, PACK, offse...  3.91 us
    pallas_call x1, Pallas kernels, pair_of(): pl.pallas_call(pair_kernel, grid=(chips // step,), out_shape=shaped(chips...  3.79 us
  transfers between devices with their start and end apart: 3, of which 1 were waited for; matrix products, arithmetic and copies ran while one was open for 5% of the time, Pallas kernels for 5%

profile of v5, /device:TPU:1, one launch (start us, length us, event | category | flops | bytes accessed | tf_op | source)
XLA Modules:
  0.0 117.5 jit_solution(4149239432994199226)
XLA Ops:
  0.6 3.8 %pair.1 = bf16[64,2,16,512]{3,2,1,0:T(8,128)(2,1)} custom-call(bf16[64,16,512]{2,1,0:T(8,128)(2,1)} %bitcast.25, bf16[64,16,512]{2,1,0:T(8,128)(2,1)} %bitcast.20), custom_call_target="tpu_custom_call" | custom-call | bytes 4194304 | tf_op jit(solution)/shard_map/pair/pallas_call | solution.py:304
  4.4 12.1 %all-to-all-start = ((bf16[64,2,16,512]{3,2,1,0:T(8,128)(2,1)}), bf16[64,2,16,512]{3,2,1,0:T(8,128)(2,1)S(1)}, u32[]{:S(2)}, u32[]{:S(2)}) async-start(bf16[64,2,16,512]{3,2,1,0:T(8,128)(2,1)} %pair.1), calls=%async_computation | async-start | bytes 4194304 | tf_op jit(solution)/shard_map/all_to_all | solution.py:493
  16.5 0.0 copy-start.3
  16.5 0.0 copy-start.4
  16.6 0.0 copy-start.5
  16.6 0.1 add_add_fusion
  16.7 3.9 %fusion.4 = f32[4,64,4,64]{3,2,0,1:T(4,128)} fusion(f32[4,4,225,1]{2,1,0,3:T(4,128)S(1)} %reshape.218, s32[64,64]{1,0:T(8,128)S(1)} %add_add_fusion), kind=kOutput, calls=%fused_computation.4 | convolution fusion | flops 177868800 | bytes 292928 | tf_op jit(solution)/shard_map/bhr,kqr->bkhq/dot_general | solution.py:484
  20.6 1.4 %reshape.220 = f32[4,64,256]{2,0,1:T(4,128)S(1)} reshape(f32[4,64,4,64]{3,2,0,1:T(4,128)} %fusion.4) | data formatting | bytes 524288 | tf_op jit(solution)/shard_map/reshape | solution.py:489
  22.0 0.1 copy.15.bias_ref
  22.1 21.5 %all-to-all-done.pair_ref = bf16[64,2,16,512]{3,2,1,0:T(8,128)(2,1)S(1)} async-done(((bf16[64,2,16,512]{3,2,1,0:T(8,128)(2,1)}), bf16[64,2,16,512]{3,2,1,0:T(8,128)(2,1)S(1)}, u32[]{:S(2)}, u32[]{:S(2)}) %all-to-all-start) | async-done | bytes 2097184 | tf_op jit(solution)/shard_map/all_to_all | solution.py:493
  43.6 0.0 copy-start.2
  43.6 1.4 %copy-done.2 = bf16[512,1536]{1,0:T(8,128)(2,1)S(1)} copy-done((bf16[512,1536]{1,0:T(8,128)(2,1)S(1)}, bf16[512,1536]{1,0:T(8,128)(2,1)}, u32[]{:S(2)}) %copy-start.2) | copy-done | bytes 1572888
  45.0 17.5 %scores.1 = (f32[512,1024]{1,0:T(8,128)S(1)}, bf16[528,1024]{1,0:T(8,128)(2,1)S(1)}, f32[8,256]{1,0:T(8,128)S(1)}, bf16[1024,1536]{1,0:T(8,128)(2,1)S(1)}, f32[4...) custom-call(s32[1]{0:T(128)} %bitcast.1.core_ref, bf16[64,2,16,512]{3,2,1,0:T(8,128)(2,1)S(1)} %all-to-all-done.pair_ref, ...), custom_call_target="tpu_custom_call" | custom-call | flops 20000000000 | bytes 8388608 | tf_op jit(solution)/shard_map/scores/pallas_call | solution.py:265
  62.5 2.8 %collective-permute-start = (bf16[528,1024]{1,0:T(8,128)(2,1)S(1)}, bf16[528,1024]{1,0:T(8,128)(2,1)S(1)}, u32[]{:S(2)}, u32[]{:S(2)}) collective-permute-start(bf16[528,1024]{1,0:T(8,128)(2,1)S(1)} %get-tuple-element.26), channel_id=1, source_target_pairs={{0,1},{1,0},{2,3},{3,2},{4,5},{5,4},{6,7},{7,6},{8,9},{9,8},{10,11... | collective-permute-start | bytes 3244040 | tf_op jit(solution)/shard_map/ppermute | solution.py:473
  65.3 4.0 %back.1 = (bf16[64,16,512]{2,1,0:T(8,128)(2,1)S(1)}, f32[8,128]{1,0:T(8,128)S(1)}) custom-call(bf16[512,1536]{1,0:T(8,128)(2,1)S(1)} %copy-done.2, f32[1,512]{1,0:T(1,128)S(1)} %bitcast.24, bf16[1024,1536]{1,0:T(8,128)(2,1)S(1)} %get-tuple-element.21.gproj, f32[4,1024,128]{2,1,0:T(8,128)S(1)} %get-tuple-element.22.hat, f32[1024,128]{1,0:T(8,128)S(1)} %get-tuple-element.23.istd), custom_call_target="tpu_custom_call" | custom-call | flops 6000000000 | bytes 4194304 | tf_op jit(solution)/shard_map/back/pallas_call | solution.py:283
  69.3 0.0 collective-permute-done.recv_ref
  69.3 0.5 outgoing.1
  69.9 41.9 %all_to_all.10.got_ref = bf16[64,19,8,128]{3,2,1,0:T(8,128)(2,1)S(1)} all-to-all(bf16[64,19,8,128]{3,2,1,0:T(8,128)(2,1)S(1)} %outgoing.1), channel_id=1, replica_groups=mesh['x_lo'=2,'y'=4,'x_hi'=2,'z'=4,'core'=2] {'x_lo','y','x_hi','z'}, dimensions={0} | all-to-all | bytes 4980736 | tf_op jit(solution)/shard_map/all_to_all | solution.py:499
  111.7 0.2 sums.1
  112.0 1.9 %collective-permute-start.1 = (f32[56,128]{1,0:T(8,128)S(1)}, f32[56,128]{1,0:T(8,128)S(1)}, u32[]{:S(2)}, u32[]{:S(2)}) collective-permute-start(f32[56,128]{1,0:T(8,128)S(1)} %get-tuple-element.30), channel_id=1, source_target_pairs={{0,1},{1,0},{2,3},{3,2},{4,5},{5,4},{6,7},{7,6},{8,9},{9,8},{10,11... | collective-permute-start | bytes 86024 | tf_op jit(solution)/shard_map/ppermute | solution.py:473
  113.9 1.3 %input_gradient.1 = bf16[64,16,512]{2,1,0:T(8,128)(2,1)} custom-call(bf16[64,19,8,128]{3,2,1,0:T(8,128)(2,1)S(1)} %all_to_all.10.got_ref, bf16[64,16,512]{2,1,0:T(8,128)(2,1)S(1)} %bitcast.21), custom_call_target="tpu_custom_call" | custom-call | bytes 4194304 | tf_op jit(solution)/shard_map/input_gradient/pallas_call | solution.py:399
  115.2 0.0 collective-permute-done.1.recv_ref
  115.2 0.6 copy-done.6
  115.9 1.6 %finish.1 = (f32[4,1536]{1,0:T(4,128)}, f32[4,512]{1,0:T(4,128)}, f32[16,225]{1,0:T(8,128)}, f32[1,512]{1,0:T(1,128)}, f32[1,512]{1,0:T(1,128)}) custom-call(s32[1]{0:T(128)} %bitcast.1.core_ref, f32[56,128]{1,0:T(8,128)} %copy-done.1, f32[56,128]{1,0:T(8,128)} %copy-done.6), custom_call_target="tpu_custom_call" | custom-call | tf_op jit(solution)/shard_map/finish/pallas_call | solution.py:445
  (12 shorter events, 0.0 us)
Async XLA Ops:
  4.4 12.1 %copy-start.7 = (f32[16,225]{1,0:T(8,128)S(1)}, f32[16,225]{1,0:T(8,128)}, u32[]{:S(2)}) copy-start(f32[16,225]{1,0:T(8,128)} %param.11) | copy-start | bytes 43204
  4.4 39.2 %all-to-all-start = ((bf16[64,2,16,512]{3,2,1,0:T(8,128)(2,1)}), bf16[64,2,16,512]{3,2,1,0:T(8,128)(2,1)S(1)}, u32[]{:S(2)}, u32[]{:S(2)}) async-start(bf16[64,2,16,512]{3,2,1,0:T(8,128)(2,1)} %pair.1), calls=%async_computation | async-start | bytes 4194304 | tf_op jit(solution)/shard_map/all_to_all | solution.py:493
  16.5 27.1 %copy-start.3 = (bf16[512,512]{1,0:T(8,128)(2,1)S(1)}, bf16[512,512]{1,0:T(8,128)(2,1)}, u32[]{:S(2)}) copy-start(bf16[512,512]{1,0:T(8,128)(2,1)} %wout_ref.1) | copy-start | bytes 1572868
  16.5 27.0 %copy-start.4 = (f32[512]{0:T(512)S(1)}, f32[512]{0:T(512)}, u32[]{:S(2)}) copy-start(f32[512]{0:T(512)} %param.13) | copy-start | bytes 6148
  16.6 27.0 %copy-start.5 = (f32[512]{0:T(512)S(1)}, f32[512]{0:T(512)}, u32[]{:S(2)}) copy-start(f32[512]{0:T(512)} %param.12) | copy-start | bytes 6148
  43.6 1.4 %copy-start.2 = (bf16[512,1536]{1,0:T(8,128)(2,1)S(1)}, bf16[512,1536]{1,0:T(8,128)(2,1)}, u32[]{:S(2)}) copy-start(bf16[512,1536]{1,0:T(8,128)(2,1)} %wqkv_ref.3) | copy-start | bytes 4718596
  62.5 6.8 %collective-permute-start = (bf16[528,1024]{1,0:T(8,128)(2,1)S(1)}, bf16[528,1024]{1,0:T(8,128)(2,1)S(1)}, u32[]{:S(2)}, u32[]{:S(2)}) collective-permute-start(bf16[528,1024]{1,0:T(8,128)(2,1)S(1)} %get-tuple-element.26), channel_id=1, source_target_pairs={{0,1},{1,0},{2,3},{3,2},{4,5},{5,4},{6,7},{7,6},{8,9},{9,8},{10,11... | collective-permute-start | bytes 3244040 | tf_op jit(solution)/shard_map/ppermute | solution.py:473
  111.7 2.2 %copy-start = (bf16[16,64,512]{2,1,0:T(8,128)(2,1)S(1)}, bf16[16,64,512]{2,1,0:T(8,128)(2,1)}, u32[]{:S(2)}) copy-start(bf16[16,64,512]{2,1,0:T(8,128)(2,1)} %param.8) | copy-start | bytes 3145732
  112.0 3.3 %copy-start.1 = (f32[56,128]{1,0:T(8,128)}, f32[56,128]{1,0:T(8,128)S(1)}, u32[]{:S(2)}) copy-start(f32[56,128]{1,0:T(8,128)S(1)} %get-tuple-element.29.keep_ref) | copy-start | bytes 86020
  112.0 3.3 %collective-permute-start.1 = (f32[56,128]{1,0:T(8,128)S(1)}, f32[56,128]{1,0:T(8,128)S(1)}, u32[]{:S(2)}, u32[]{:S(2)}) collective-permute-start(f32[56,128]{1,0:T(8,128)S(1)} %get-tuple-element.30), channel_id=1, source_target_pairs={{0,1},{1,0},{2,3},{3,2},{4,5},{5,4},{6,7},{7,6},{8,9},{9,8},{10,11... | collective-permute-start | bytes 86024 | tf_op jit(solution)/shard_map/ppermute | solution.py:473
  115.2 0.6 copy-start.6

commit v6 on v5

--- a/solution.py
+++ b/solution.py
@@ -26,106 +26,169 @@
     return jnp.concatenate([ref[b, at, :] for b in range(ref.shape[0])], axis=1)
 
 
-def forward_and_scores(
-    pair_ref, wqkv_ref, wout_ref, bias_ref, gain_ref, shift_ref, gbias_ref,
-    normed, gproj, att, dyp, hat, istd, proj, gatt, dyf, head_dim,
+def by_group(ref, c, per, groups):
+    return jnp.concatenate([take(ref, pl.ds(c * per + g, MEMBERS, stride=groups)) for g in range(per)], axis=0)
+
+
+def spread(a, lane):
+    zero = jnp.zeros_like(a)
+    return jnp.concatenate([jnp.where(lane == h, a, zero) for h in range(PACK)], axis=0)
+
+
+def gather(a, lane):
+    out = a[:MEMBERS]
+    for h in range(1, PACK):
+        out = jnp.where(lane == h, a[h * MEMBERS : (h + 1) * MEMBERS], out)
+    return out
+
+
+def by_query(weights, values):
+    none = jnp.zeros_like(values[0])
+    out = []
+    for b in range(0, len(weights), 2):
+        pair = jnp.concatenate(
+            [
+                jnp.concatenate([values[b], none], axis=1),
+                jnp.concatenate([none, values[b + 1]], axis=1),
+            ],
+            axis=0,
+        )
+        both = dot(jnp.concatenate(weights[b : b + 2], axis=0), pair, 0, 0)
+        out += [both[:, :128], both[:, 128:]]
+    return out
+
+
+def head_lanes(head_dim):
+    return lax.broadcasted_iota(jnp.int32, (MEMBERS, 128), 1) // head_dim
+
+
+def column_blocks(width):
+    blocks = range(width // 128)
+    return [[slice(i * width + b * 128, i * width + (b + 1) * 128) for b in blocks] for i in range(3)]
+
+
+def forward_kernel(
+    x_ref, wqkv_ref, bias_ref, gain_ref, shift_ref, normed, proj, hat, istd, prob_ref, att, *, head_dim
 ):
-    width = gproj.shape[1] // 3
-    rows, groups, chunk = gproj.shape[0], gproj.shape[0] // MEMBERS, CHUNK
+    _, groups, width = x_ref.shape
+    rows, chunk = groups * MEMBERS, CHUNK
     per, mem = chunk // MEMBERS, chunk // groups
     bf16, f32 = jnp.bfloat16, jnp.float32
     scale = head_dim ** (-0.5)
 
     def hat_step(c, carry):
         here = pl.ds(pl.multiple_of(c * chunk, chunk), chunk)
-        pair = pair_ref[pl.ds(pl.multiple_of(c * mem, mem), mem)].astype(f32)
-        x = pair[:, 0].reshape(chunk, width)
+        x = x_ref[pl.ds(pl.multiple_of(c * mem, mem), mem)].astype(f32).reshape(chunk, width)
         centred = x - jnp.mean(x, axis=-1, keepdims=True)
         inv = lax.rsqrt(jnp.mean(centred * centred, axis=-1, keepdims=True) + EPSILON)
         put(hat, here, centred * inv)
         istd[here, :] = jnp.broadcast_to(inv, (chunk, 128))
-        put(dyf, here, pair[:, 1].reshape(chunk, width))
         return carry
 
     lax.fori_loop(0, rows // chunk, hat_step, 0)
-
-    def by_group(ref, c):
-        return jnp.concatenate(
-            [take(ref, pl.ds(c * per + g, MEMBERS, stride=groups)) for g in range(per)], axis=0
-        )
 
     def norm_step(c, carry):
         here = pl.ds(pl.multiple_of(c * chunk, chunk), chunk)
-        nb = (by_group(hat, c) * gain_ref[...] + shift_ref[...]).astype(bf16)
-        dy = by_group(dyf, c).astype(bf16)
-        dyp[here, :] = dy
+        nb = (by_group(hat, c, per, groups) * gain_ref[...] + shift_ref[...]).astype(bf16)
         normed[here, :] = nb
         proj[here, :] = dot(nb, wqkv_ref[...], 1, 0).astype(bf16)
-        gatt[here, :] = dot(dy, wout_ref[...], 1, 1).astype(bf16)
         return carry
 
     lax.fori_loop(0, rows // chunk, norm_step, 0, unroll=True)
 
-    lane = lax.broadcasted_iota(jnp.int32, (MEMBERS, 128), 1) // head_dim
-
-    def spread(a):
-        zero = jnp.zeros_like(a)
-        return jnp.concatenate([jnp.where(lane == h, a, zero) for h in range(PACK)], axis=0)
-
-    def gather(a):
-        out = a[:MEMBERS]
-        for h in range(1, PACK):
-            out = jnp.where(lane == h, a[h * MEMBERS : (h + 1) * MEMBERS], out)
-        return out
-
-    blocks = range(width // 128)
+    lane = head_lanes(head_dim)
+    qcols, kcols, vcols = column_blocks(width)
 
     def group_step(g, carry):
         here = pl.ds(pl.multiple_of(g * MEMBERS, MEMBERS), MEMBERS)
-        cols = [slice(b * 128, (b + 1) * 128) for b in blocks]
-        kcols = [slice(width + b * 128, width + (b + 1) * 128) for b in blocks]
-        vcols = [slice(2 * width + b * 128, 2 * width + (b + 1) * 128) for b in blocks]
-        ks = [proj[here, c] for c in kcols]
-        vs = [proj[here, c] for c in vcols]
-        none = jnp.zeros_like(ks[0])
-        ws = [jnp.concatenate([spread(proj[here, c]), spread(gatt[here, c])], axis=1) for c in cols]
-        both = [
-            dot(
-                jnp.concatenate(
-                    [jnp.concatenate([k, none], axis=1), jnp.concatenate([none, v], axis=1)], axis=0
-                ),
-                w, 1, 1,
-            )
-            for k, v, w in zip(ks, vs, ws)
-        ]
-        pds = []
+        probs = []
+        scores = [dot(proj[here, k], spread(proj[here, q], lane), 1, 1) for q, k in zip(qcols, kcols)]
+        for b, score in enumerate(scores):
+            score = score * scale + bias_ref[b]
+            e = jnp.exp(score - jnp.max(score, axis=0, keepdims=True))
+            p = e * (1.0 / jnp.sum(e, axis=0, keepdims=True))
+            prob_ref[b, here, :] = p
+            probs.append(p.astype(bf16))
+        attended = by_query(probs, [proj[here, c] for c in vcols])
+        for b, value in enumerate(attended):
+            att[here, qcols[b]] = gather(value, lane).astype(bf16)
+        return carry
+
+    lax.fori_loop(0, groups, group_step, 0, unroll=4)
+
+
+def scores_kernel(
+    core_ref, dy_ref, wout_ref, normed, proj, prob_ref, att,
+    keep_ref, send_ref, table_ref, gproj, gbias_ref, dyp, gatt, dyf, *, head_dim,
+):
+    _, groups, width = dy_ref.shape
+    rows, chunk = groups * MEMBERS, CHUNK
+    per, mem = chunk // MEMBERS, chunk // groups
+    bf16, f32 = jnp.bfloat16, jnp.float32
+    scale = head_dim ** (-0.5)
+
+    def float_step(c, carry):
+        here = pl.ds(pl.multiple_of(c * chunk, chunk), chunk)
+        put(dyf, here, dy_ref[pl.ds(pl.multiple_of(c * mem, mem), mem)].astype(f32).reshape(chunk, width))
+        return carry
+
+    lax.fori_loop(0, rows // chunk, float_step, 0)
+
+    def cotangent_step(c, carry):
+        here = pl.ds(pl.multiple_of(c * chunk, chunk), chunk)
+        dy = by_group(dyf, c, per, groups).astype(bf16)
+        dyp[here, :] = dy
+        gatt[here, :] = dot(dy, wout_ref[...], 1, 1).astype(bf16)
+        return carry
+
+    lax.fori_loop(0, rows // chunk, cotangent_step, 0, unroll=True)
+
+    gbias_ref[...] = jnp.zeros_like(gbias_ref)
+    lane = head_lanes(head_dim)
+    qcols, kcols, vcols = column_blocks(width)
+    blocks = range(width // 128)
+
+    def group_step(g, carry):
+        here = pl.ds(pl.multiple_of(g * MEMBERS, MEMBERS), MEMBERS)
+        gas = [spread(gatt[here, c], lane) for c in qcols]
+        gps = [dot(proj[here, c], ga, 1, 1) for c, ga in zip(vcols, gas)]
+        ws = [jnp.concatenate([spread(proj[here, c], lane), ga], axis=1) for c, ga in zip(qcols, gas)]
+        probs, grads = [], []
         for b in blocks:
-            scores = both[b][:MEMBERS] * scale + bias_ref[b]
-            gp = both[b][MEMBERS:]
-            e = jnp.exp(scores - jnp.max(scores, axis=0, keepdims=True))
-            p = e * (1.0 / jnp.sum(e, axis=0, keepdims=True))
-            gs = p * (gp - jnp.sum(gp * p, axis=0, keepdims=True))
+            p = prob_ref[b, here, :]
+            gs = p * (gps[b] - jnp.sum(gps[b] * p, axis=0, keepdims=True))
             gbias_ref[b] += gs
-            pds.append(jnp.concatenate([p.astype(bf16), (gs * scale).astype(bf16)], axis=0))
-        keyed = [dot(pd, w, 1, 0) for pd, w in zip(pds, ws)]
-        queried = [
-            dot(
-                pd,
-                jnp.concatenate(
-                    [jnp.concatenate([v, none], axis=1), jnp.concatenate([none, k], axis=1)], axis=0
-                ),
-                0, 0,
-            )
-            for k, v, pd in zip(ks, vs, pds)
-        ]
+            probs.append(p.astype(bf16))
+            grads.append((gs * scale).astype(bf16))
+        keyed = [dot(jnp.concatenate([p, gs], axis=0), w, 1, 0) for p, gs, w in zip(probs, grads, ws)]
+        queried = by_query(grads, [proj[here, c] for c in kcols])
         for b in blocks:
-            att[here, cols[b]] = gather(queried[b][:, :128]).astype(bf16)
-            gproj[here, cols[b]] = gather(queried[b][:, 128:]).astype(bf16)
+            gproj[here, qcols[b]] = gather(queried[b], lane).astype(bf16)
             gproj[here, kcols[b]] = keyed[b][MEMBERS:, :128].astype(bf16)
             gproj[here, vcols[b]] = keyed[b][:MEMBERS, 128:].astype(bf16)
         return carry
 
     lax.fori_loop(0, groups, group_step, 0, unroll=4)
+
+    half = 2 * width
+    first = core_ref[0] == 0
+    table = offset_sums(gbias_ref)
+    heads = table.shape[0] // 2
+    table_ref[...] = jnp.where(first, table[:heads], table[heads:])
+    send_ref[width:, :] = jnp.zeros((send_ref.shape[0] - width, half), send_ref.dtype)
+    send_ref[width : width + heads, :256] = jnp.where(first, table[heads:], table[:heads]).astype(send_ref.dtype)
+
+    @pl.when(first)
+    def _():
+        keep_ref[...] = dot(normed[...], gproj[:, :half], 0, 0)
+        send_ref[:width, :width] = dot(normed[...], gproj[:, half:], 0, 0).astype(send_ref.dtype)
+        send_ref[:width, width:] = dot(att[...], dyp[...], 0, 0).astype(send_ref.dtype)
+
+    @pl.when(jnp.logical_not(first))
+    def _():
+        send_ref[:width, :] = dot(normed[...], gproj[:, :half], 0, 0).astype(send_ref.dtype)
+        keep_ref[:, :width] = dot(normed[...], gproj[:, half:], 0, 0)
+        keep_ref[:, width:] = dot(att[...], dyp[...], 0, 0)
 
 
 def back_to_input(wqkv_ref, gain_ref, branch_ref, gproj, hat, istd, dyf):
@@ -169,62 +232,29 @@
     blocks, members, lanes = gbias_ref.shape
     i = lax.broadcasted_iota(jnp.int32, (lanes, 2 * lanes), 0)
     o = lax.broadcasted_iota(jnp.int32, (lanes, 2 * lanes), 1)
-    query = i % members
-    place = (i // members) * 128 + query // GRID * 16 + query % GRID
-    wide = (o == place).astype(f32).astype(bf16)
-    frames = []
+    query = GRID * GRID - 1 - i % members
+    wide = (o == i // members * 128 + query // GRID * 16 + query % GRID).astype(f32).astype(bf16)
+    spreads = []
     for b in range(blocks):
         value = gbias_ref[b]
         high = value.astype(bf16)
         rest = value - high.astype(f32)
         low = rest.astype(bf16)
         lowest = (rest - low.astype(f32)).astype(bf16)
-        spread = dot(jnp.concatenate([high, low, lowest], axis=0), wide, 1, 0)
-        spread = spread[:members] + (spread[members : 2 * members] + spread[2 * members :])
-        frames += [spread[None, :, h * 128 : (h + 1) * 128] for h in range(PACK)]
-    frame = jnp.concatenate(frames, axis=0)
-    heads = frame.shape[0]
-    frame = jnp.concatenate([frame, jnp.zeros_like(frame)], axis=2).reshape(heads * members, 256)
-    column = GRID - 1 - lax.broadcasted_iota(jnp.int32, frame.shape, 0) % GRID
-    for bit in (1, 2, 4):
-        frame = jnp.where((column & bit) != 0, pltpu.roll(frame, bit, 1), frame)
-    frame = jnp.sum(frame.reshape(heads * GRID, GRID, 256), axis=1)
-    row = GRID - 1 - lax.broadcasted_iota(jnp.int32, frame.shape, 0) % GRID
-    for bit in (1, 2, 4):
-        frame = jnp.where((row & bit) != 0, pltpu.roll(frame, 16 * bit, 1), frame)
-    return jnp.sum(frame.reshape(heads, GRID, 256), axis=1)
-
-
-def scores_kernel(
-    core_ref, pair_ref, wqkv_ref, wout_ref, bias_ref, gain_ref, shift_ref,
-    keep_ref, send_ref, table_ref, gproj, hat, istd,
-    gbias_ref, normed, att, dyp, proj, gatt, dyf, *, head_dim,
-):
-    gbias_ref[...] = jnp.zeros_like(gbias_ref)
-    forward_and_scores(
-        pair_ref, wqkv_ref, wout_ref, bias_ref, gain_ref, shift_ref, gbias_ref,
-        normed, gproj, att, dyp, hat, istd, proj, gatt, dyf, head_dim,
-    )
-    width = wout_ref.shape[0]
-    half = 2 * width
-    first = core_ref[0] == 0
-    table = offset_sums(gbias_ref)
-    heads = table.shape[0] // 2
-    table_ref[...] = jnp.where(first, table[:heads], table[heads:])
-    send_ref[width:, :] = jnp.zeros((send_ref.shape[0] - width, half), send_ref.dtype)
-    send_ref[width : width + heads, :256] = jnp.where(first, table[heads:], table[:heads]).astype(send_ref.dtype)
-
-    @pl.when(first)
-    def _():
-        keep_ref[...] = dot(normed[...], gproj[:, :half], 0, 0)
-        send_ref[:width, :width] = dot(normed[...], gproj[:, half:], 0, 0).astype(send_ref.dtype)
-        send_ref[:width, width:] = dot(att[...], dyp[...], 0, 0).astype(send_ref.dtype)
-
-    @pl.when(jnp.logical_not(first))
-    def _():
-        send_ref[:width, :] = dot(normed[...], gproj[:, :half], 0, 0).astype(send_ref.dtype)
-        keep_ref[:, :width] = dot(normed[...], gproj[:, half:], 0, 0)
-        keep_ref[:, width:] = dot(att[...], dyp[...], 0, 0)
+        parts = dot(jnp.concatenate([high, low, lowest], axis=0), wide, 1, 0)
+        spreads.append(parts[:members] + (parts[members : 2 * members] + parts[2 * members :]))
+    sums = []
+    for b in range(blocks):
+        for h in range(PACK):
+            frame = spreads[b][:, h * 128 : (h + 1) * 128]
+            total = None
+            for row in range(GRID):
+                piece = frame[row * GRID : (row + 1) * GRID]
+                piece = jnp.concatenate([piece, jnp.zeros_like(piece)], axis=1)
+                piece = pltpu.roll(piece, row * 16, 1, stride=1, stride_axis=0)
+                total = piece if total is None else total + piece
+            sums.append(jnp.sum(total, axis=0, keepdims=True))
+    return jnp.concatenate(sums, axis=0)
 
 
 def back_kernel(wqkv_ref, gain_ref, gproj, hat, istd, branch_ref, gvec_ref, dyf):
@@ -248,34 +278,46 @@
     return pl.CostEstimate(flops=flops, bytes_accessed=size, transcendentals=0)
 
 
-def part_buffers(rows, width):
-    bf16, f32 = jnp.bfloat16, jnp.float32
-    tall, lanes = (rows, width), (width // 128, rows, 128)
-    return [
-        (tall, bf16), ((rows, 3 * width), bf16), (tall, bf16), (tall, bf16), (lanes, f32), ((rows, 128), f32),
-        ((rows, 3 * width), bf16), (tall, bf16), (lanes, f32),
-    ]
-
-
-def local_scores(core, pair, wqkv, wout, bias, gain, shift, head_dim):
-    members, _, groups, width = pair.shape
-    bf16, f32 = jnp.bfloat16, jnp.float32
-    normed, gproj, att, dyp, hat, istd, proj, gatt, dyf = part_buffers(groups * MEMBERS, width)
+def local_forward(x, wqkv, bias, gain, shift, head_dim):
+    members, groups, width = x.shape
+    rows, bf16 = groups * MEMBERS, jnp.bfloat16
+    blocks = width // 128
+    return pl.pallas_call(
+        functools.partial(forward_kernel, head_dim=head_dim),
+        out_shape=(
+            shaped(rows, width, dtype=bf16), shaped(rows, 3 * width, dtype=bf16),
+            shaped(blocks, rows, 128), shaped(rows, 128), shaped(blocks, rows, PACK * MEMBERS),
+            shaped(rows, width, dtype=bf16),
+        ),
+        in_specs=[VMEM] * 5,
+        out_specs=(VMEM,) * 6,
+        compiler_params=pltpu.CompilerParams(vmem_limit_bytes=24 * MIB),
+        cost_estimate=cost(10_000_000_000, 8 << 20),
+        name="forward",
+    )(x, wqkv, bias, gain.reshape(1, width), shift.reshape(1, width))
+
+
+def local_scores(core, dy, wout, normed, proj, prob, att, head_dim):
+    members, groups, width = dy.shape
+    rows, bf16, f32 = groups * MEMBERS, jnp.bfloat16, jnp.float32
     half_heads = width // head_dim // 2
+    tall = pltpu.VMEM((rows, width), bf16)
     return pl.pallas_call(
         functools.partial(scores_kernel, head_dim=head_dim),
         out_shape=(
-            shaped(width, 2 * width), shaped(width + 16, 2 * width, dtype=bf16), shaped(half_heads, 256)
-        )
-        + tuple(jax.ShapeDtypeStruct(*b) for b in (gproj, hat, istd)),
+            shaped(width, 2 * width), shaped(width + 16, 2 * width, dtype=bf16), shaped(half_heads, 256),
+            shaped(rows, 3 * width, dtype=bf16),
+        ),
         in_specs=[SMEM] + [VMEM] * 6,
-        out_specs=(VMEM,) * 6,
-        scratch_shapes=[pltpu.VMEM(bias.shape, f32)]
-        + [pltpu.VMEM(*b) for b in (normed, att, dyp, proj, gatt, dyf)],
+        out_specs=(VMEM,) * 4,
+        scratch_shapes=[
+            pltpu.VMEM((width // 128, MEMBERS, PACK * MEMBERS), f32), tall, tall,
+            pltpu.VMEM((width // 128, rows, 128), f32),
+        ],
         compiler_params=pltpu.CompilerParams(vmem_limit_bytes=28 * MIB),
         cost_estimate=cost(20_000_000_000, 8 << 20),
         name="scores",
-    )(core.reshape(1), pair, wqkv, wout, bias, gain.reshape(1, width), shift.reshape(1, width))
+    )(core.reshape(1), dy, wout, normed, proj, prob, att)
 
 
 def local_back(wqkv, gain, gproj, hat, istd, groups):
@@ -290,26 +332,6 @@
         cost_estimate=cost(6_000_000_000, 4 << 20),
         name="back",
     )(wqkv, gain.reshape(1, width), gproj, hat, istd)
-
-
-def pair_kernel(x_ref, dy_ref, out_ref):
-    out_ref[:, 0] = x_ref[...]
-    out_ref[:, 1] = dy_ref[...]
-
-
-def pair_of(x, dy):
-    chips, groups, width = x.shape
-    step = chips // 4
-    source = pl.BlockSpec((step, groups, width), lambda i: (i, 0, 0))
-    return pl.pallas_call(
-        pair_kernel,
-        grid=(chips // step,),
-        out_shape=shaped(chips, 2, groups, width, dtype=x.dtype),
-        in_specs=[source, source],
-        out_specs=pl.BlockSpec((step, 2, groups, width), lambda i: (i, 0, 0, 0)),
-        cost_estimate=cost(0, 4 << 20),
-        name="pair",
-    )(x, dy)
 
 
 def outgoing_kernel(branch_ref, keep_ref, recv_ref, table_ref, gvec_ref, out_ref):
@@ -430,7 +452,8 @@
     side = 2 * GRID - 1
     place = lax.broadcasted_iota(jnp.int32, (256, side * side), 0)
     offset = lax.broadcasted_iota(jnp.int32, (256, side * side), 1)
-    pick = (place == offset // side * 16 + offset % side).astype(jnp.float32)
+    row, column = side - 1 - offset // side, side - 1 - offset % side
+    pick = (place == row * 16 + column).astype(jnp.float32)
     table_ref[...] = lax.dot_general(
         table, pick, (((1,), (0,)), ((), ())), precision=lax.Precision.HIGHEST, preferred_element_type=jnp.float32
     )
@@ -490,9 +513,11 @@
     x = block_input.reshape(chips, owned, width)
     dy = cotangent.reshape(chips, owned, width)
     exchange = functools.partial(lax.all_to_all, axis_name=CHIPS, split_axis=0, concat_axis=0, tiled=True)
-    got = exchange(pair_of(x, dy))
-    keep, send, table, gproj, hat, istd = local_scores(
-        core, got, qkv_weight, out_weight, bias, norm_gain, norm_shift, width // heads
+    got = exchange(x)
+    got, bias, dy_sent = lax.optimization_barrier((got, bias, dy))
+    normed, proj, hat, istd, prob, att = local_forward(got, qkv_weight, bias, norm_gain, norm_shift, width // heads)
+    keep, send, table, gproj = local_scores(
+        core, exchange(dy_sent), out_weight, normed, proj, prob, att, width // heads
     )
     recv = swap(send, "core", 1)
     branch, gvec = local_back(qkv_weight, norm_gain, gproj, hat, istd, owned)

time: 118 us -> 129 us (1.093)
  local copies, waits for them, and re-layouts: 3.48 us -> 17.3 us
  waiting for transfers between devices: 21.5 us -> 11.5 us
  starting transfers between devices: 16.9 us -> 22.5 us
  blocking collectives: 41.9 us -> 44.6 us
    unnamed x16 -> x34, local copies, waits for them, and re-layouts: 2.04 us -> 16.2 us
    all_to_all x1 -> x2, waiting for transfers between devices: 21.5 us -> 11.5 us  [the longest x1 11.5 us: local(): got = exchange(x)]
    pallas_call x1, Pallas kernels: 17.5 us -> 10.2 us  [local_scores(): pl.pallas_call(functools.partial(scores_kernel, head_dim=head_dim), out_s...]
    all_to_all x1 -> x2, starting transfers between devices: 12.1 us -> 18.3 us  [the longest x1 12 us: local(): got = exchange(x)]
    pallas_call x1, Pallas kernels: 3.79 us -> 9.17 us  [local_forward(): pl.pallas_call(functools.partial(forward_kernel, head_dim=head_dim), out_...]
    all_to_all x1, blocking collectives: 41.9 us -> 44.6 us  [local(): got = exchange(outgoing(branch, keep, recv, table, gvec))]
  transfers between devices with their start and end apart: 3 -> 4, of which waited for: 1 -> 1; matrix products, arithmetic and copies ran while one was open for 5% -> 3% of each run, Pallas kernels for 5% -> 12%
where the time goes in v6:
time: 129 us; the launch traced here: 128 us
  blocking collectives  44.6 us (35%)
  Pallas kernels  28.2 us (22%)
  starting transfers between devices  22.5 us (17%)
  local copies, waits for them, and re-layouts  17.3 us (13%)
  waiting for transfers between devices  11.5 us (9%)
  matrix products  3.2 us (2%)
    all_to_all x1, blocking collectives, local(): got = exchange(outgoing(branch, keep, recv, table, gvec))  44.6 us
    unnamed x34, local copies, waits for them, and re-layouts  16.2 us
    all_to_all x1, starting transfers between devices, local(): got = exchange(x)  12 us
    all_to_all x1, waiting for transfers between devices, local(): got = exchange(x)  11.5 us
    pallas_call x1, Pallas kernels, local_scores(): pl.pallas_call(functools.partial(scores_kernel, head_dim=head_dim), out_s...  10.2 us
    pallas_call x1, Pallas kernels, local_forward(): pl.pallas_call(functools.partial(forward_kernel, head_dim=head_dim), out_...  9.17 us
    all_to_all x1, starting transfers between devices, local(): exchange(dy_sent)  6.34 us
    ppermute x2, starting transfers between devices, swap(): return lax.ppermute(a, axis, [(i, i ^ mask) for i in range(size)])  4.23 us
  transfers between devices with their start and end apart: 4, of which 1 were waited for; matrix products, arithmetic and copies ran while one was open for 3% of the time, Pallas kernels for 12%

profile of v6, /device:TPU:1, one launch (start us, length us, event | category | flops | bytes accessed | tf_op | source)
XLA Modules:
  0.0 128.1 jit_solution(12484243866447218957)
XLA Ops:
  0.6 12.0 %all-to-all-start = ((bf16[64,16,512]{2,1,0:T(8,128)(2,1)}), bf16[64,16,512]{2,1,0:T(8,128)(2,1)S(1)}, u32[]{:S(2)}, u32[]{:S(2)}) async-start(bf16[64,16,512]{2,1,0:T(8,128)(2,1)} %bitcast.23), calls=%async_computation | async-start | bytes 2097152 | tf_op jit(solution)/shard_map/all_to_all | solution.py:516
  12.6 0.7 reshape.218
  13.5 3.2 %fusion.4 = f32[4,64,4,64]{3,2,0,1:T(4,128)S(1)} fusion(f32[4,4,225,1]{2,1,0,3:T(4,128)S(1)} %reshape.218, s32[64,64]{1,0:T(8,128)S(1)} %add_add_fusion), kind=kOutput, calls=%fused_computation.4 | convolution fusion | flops 177868800 | bytes 292928 | tf_op jit(solution)/shard_map/bhr,kqr->bkhq/dot_general | solution.py:507
  17.1 11.5 %all-to-all-done.x_ref = bf16[64,16,512]{2,1,0:T(8,128)(2,1)S(1)} async-done(((bf16[64,16,512]{2,1,0:T(8,128)(2,1)}), bf16[64,16,512]{2,1,0:T(8,128)(2,1)S(1)}, u32[]{:S(2)}, u32[]{:S(2)}) %all-to-all-start) | async-done | bytes 1048608 | tf_op jit(solution)/shard_map/all_to_all | solution.py:516
  28.6 6.3 %all-to-all-start.1 = ((bf16[64,16,512]{2,1,0:T(8,128)(2,1)}), bf16[64,16,512]{2,1,0:T(8,128)(2,1)S(1)}, u32[]{:S(2)}, u32[]{:S(2)}) async-start(bf16[64,16,512]{2,1,0:T(8,128)(2,1)} %bitcast.6.dy_ref), calls=%async_computation.1 | async-start | bytes 2097152 | tf_op jit(solution)/shard_map/all_to_all | solution.py:520
  34.9 1.4 %copy-done.1 = bf16[512,1536]{1,0:T(8,128)(2,1)S(1)} copy-done((bf16[512,1536]{1,0:T(8,128)(2,1)S(1)}, bf16[512,1536]{1,0:T(8,128)(2,1)}, u32[]{:S(2)}) %copy-start.1) | copy-done | bytes 1572888
  36.4 9.2 %forward.1 = (bf16[1024,512]{1,0:T(8,128)(2,1)S(1)}, bf16[1024,1536]{1,0:T(8,128)(2,1)S(1)}, f32[4,1024,128]{2,1,0:T(8,128)S(1)}, f32[1024,128]{1,0:T(8,128)S(1)...) custom-call(bf16[64,16,512]{2,1,0:T(8,128)(2,1)S(1)} %all-to-all-done.x_ref, ...), custom_call_target="tpu_custom_call" | custom-call | flops 10000000000 | bytes 8388608 | tf_op jit(solution)/shard_map/forward/pallas_call | solution.py:285
  45.5 1.4 %copy-done.6 = f32[4,1024,128]{2,1,0:T(8,128)} copy-done((f32[4,1024,128]{2,1,0:T(8,128)}, f32[4,1024,128]{2,1,0:T(8,128)S(1)}, u32[]{:S(2)}) %copy-start.6) | copy-done | bytes 2097176
  46.9 1.9 %copy-done.8 = f32[4,1024,256]{2,1,0:T(8,128)} copy-done((f32[4,1024,256]{2,1,0:T(8,128)}, f32[4,1024,256]{2,1,0:T(8,128)S(1)}, u32[]{:S(2)}) %copy-start.8) | copy-done | bytes 4194328
  48.9 1.7 %copy-done.10 = bf16[1024,1536]{1,0:T(8,128)(2,1)} copy-done((bf16[1024,1536]{1,0:T(8,128)(2,1)}, bf16[1024,1536]{1,0:T(8,128)(2,1)S(1)}, u32[]{:S(2)}) %copy-start.10) | copy-done | bytes 3145752
  50.6 1.0 copy-done.12
  51.5 1.0 copy-done.14
  52.5 2.2 %copy-done.9 = f32[4,1024,256]{2,1,0:T(8,128)S(1)} copy-done((f32[4,1024,256]{2,1,0:T(8,128)S(1)}, f32[4,1024,256]{2,1,0:T(8,128)}, u32[]{:S(2)}) %copy-start.9) | copy-done | bytes 4194328
  54.7 1.9 %copy-done.11 = bf16[1024,1536]{1,0:T(8,128)(2,1)S(1)} copy-done((bf16[1024,1536]{1,0:T(8,128)(2,1)S(1)}, bf16[1024,1536]{1,0:T(8,128)(2,1)}, u32[]{:S(2)}) %copy-start.11) | copy-done | bytes 3145752
  56.6 1.2 copy-done.13
  57.9 1.2 copy-done.15
  59.1 10.2 %scores.1 = (f32[512,1024]{1,0:T(8,128)S(1)}, bf16[528,1024]{1,0:T(8,128)(2,1)S(1)}, f32[8,256]{1,0:T(8,128)S(1)}, bf16[1024,1536]{1,0:T(8,128)(2,1)S(1)}) custom-call(s32[1]{0:T(128)} %bitcast.1.core_ref, bf16[64,16,512]{2,1,0:T(8,128)(2,1)S(1)} %all-to-all-done.1.dy_ref, bf16[512,512]{1,0:T(8,128)(2,1)S(1)} %copy-done.3, bf16[1024,512]{1,0:T(8,128)(2,1)S(1)} %copy-done.13, ...), custom_call_target="tpu_custom_call" | custom-call | flops 20000000000 | bytes 8388608 | tf_op jit(solution)/shard_map/scores/pallas_call | solution.py:305
  69.3 2.3 %collective-permute-start = (bf16[528,1024]{1,0:T(8,128)(2,1)S(1)}, bf16[528,1024]{1,0:T(8,128)(2,1)S(1)}, u32[]{:S(2)}, u32[]{:S(2)}) collective-permute-start(bf16[528,1024]{1,0:T(8,128)(2,1)S(1)} %get-tuple-element.40), channel_id=1, source_target_pairs={{0,1},{1,0},{2,3},{3,2},{4,5},{5,4},{6,7},{7,6},{8,9},{9,8},{10,11... | collective-permute-start | bytes 3244040 | tf_op jit(solution)/shard_map/ppermute | solution.py:496
  71.6 3.9 %back.1 = (bf16[64,16,512]{2,1,0:T(8,128)(2,1)S(1)}, f32[8,128]{1,0:T(8,128)S(1)}) custom-call(bf16[512,1536]{1,0:T(8,128)(2,1)S(1)} %copy-done.2, f32[1,512]{1,0:T(1,128)S(1)} %bitcast.22, bf16[1024,1536]{1,0:T(8,128)(2,1)S(1)} %get-tuple-element.35.gproj, f32[4,1024,128]{2,1,0:T(8,128)S(1)} %copy-done.7, f32[1024,128]{1,0:T(8,128)S(1)} %get-tuple-element.37.istd), custom_call_target="tpu_custom_call" | custom-call | flops 6000000000 | bytes 4194304 | tf_op jit(solution)/shard_map/back/pallas_call | solution.py:325
  76.1 44.6 %all_to_all.15.got_ref = bf16[64,19,8,128]{3,2,1,0:T(8,128)(2,1)S(1)} all-to-all(bf16[64,19,8,128]{3,2,1,0:T(8,128)(2,1)S(1)} %outgoing.1), channel_id=1, replica_groups=mesh['x_lo'=2,'y'=4,'x_hi'=2,'z'=4,'core'=2] {'x_lo','y','x_hi','z'}, dimensions={0} | all-to-all | bytes 4980736 | tf_op jit(solution)/shard_map/all_to_all | solution.py:524
  121.5 1.9 %collective-permute-start.1 = (f32[56,128]{1,0:T(8,128)S(1)}, f32[56,128]{1,0:T(8,128)S(1)}, u32[]{:S(2)}, u32[]{:S(2)}) collective-permute-start(f32[56,128]{1,0:T(8,128)S(1)} %get-tuple-element.44), channel_id=1, source_target_pairs={{0,1},{1,0},{2,3},{3,2},{4,5},{5,4},{6,7},{7,6},{8,9},{9,8},{10,11... | collective-permute-start | bytes 86024 | tf_op jit(solution)/shard_map/ppermute | solution.py:496
  123.4 2.5 %input_gradient.1 = bf16[64,16,512]{2,1,0:T(8,128)(2,1)} custom-call(bf16[64,19,8,128]{3,2,1,0:T(8,128)(2,1)S(1)} %all_to_all.15.got_ref, bf16[64,16,512]{2,1,0:T(8,128)(2,1)} %bitcast.6.dy_ref), custom_call_target="tpu_custom_call" | custom-call | bytes 4194304 | tf_op jit(solution)/shard_map/input_gradient/pallas_call | solution.py:421
  125.9 0.6 copy-done.16
  126.5 1.6 %finish.1 = (f32[4,1536]{1,0:T(4,128)}, f32[4,512]{1,0:T(4,128)}, f32[16,225]{1,0:T(8,128)}, f32[1,512]{1,0:T(1,128)}, f32[1,512]{1,0:T(1,128)}) custom-call(s32[1]{0:T(128)} %bitcast.1.core_ref, f32[56,128]{1,0:T(8,128)} %copy-done, f32[56,128]{1,0:T(8,128)} %copy-done.16), custom_call_target="tpu_custom_call" | custom-call | tf_op jit(solution)/shard_map/finish/pallas_call | solution.py:468
  (32 shorter events, 1.9 us)
Async XLA Ops:
  0.6 27.9 %all-to-all-start = ((bf16[64,16,512]{2,1,0:T(8,128)(2,1)}), bf16[64,16,512]{2,1,0:T(8,128)(2,1)S(1)}, u32[]{:S(2)}, u32[]{:S(2)}) async-start(bf16[64,16,512]{2,1,0:T(8,128)(2,1)} %bitcast.23), calls=%async_computation | async-start | bytes 2097152 | tf_op jit(solution)/shard_map/all_to_all | solution.py:516
  12.6 22.3 %copy-start.4 = (f32[512]{0:T(512)S(1)}, f32[512]{0:T(512)}, u32[]{:S(2)}) copy-start(f32[512]{0:T(512)} %param.13) | copy-start | bytes 6148
  12.6 22.3 %copy-start.5 = (f32[512]{0:T(512)S(1)}, f32[512]{0:T(512)}, u32[]{:S(2)}) copy-start(f32[512]{0:T(512)} %param.12) | copy-start | bytes 6148
  28.6 24.0 %all-to-all-start.1 = ((bf16[64,16,512]{2,1,0:T(8,128)(2,1)}), bf16[64,16,512]{2,1,0:T(8,128)(2,1)S(1)}, u32[]{:S(2)}, u32[]{:S(2)}) async-start(bf16[64,16,512]{2,1,0:T(8,128)(2,1)} %bitcast.6.dy_ref), calls=%async_computation.1 | async-start | bytes 2097152 | tf_op jit(solution)/shard_map/all_to_all | solution.py:520
  34.9 1.4 %copy-start.1 = (bf16[512,1536]{1,0:T(8,128)(2,1)S(1)}, bf16[512,1536]{1,0:T(8,128)(2,1)}, u32[]{:S(2)}) copy-start(bf16[512,1536]{1,0:T(8,128)(2,1)} %wqkv_ref.3) | copy-start | bytes 4718596
  36.3 16.2 %copy-start.3 = (bf16[512,512]{1,0:T(8,128)(2,1)S(1)}, bf16[512,512]{1,0:T(8,128)(2,1)}, u32[]{:S(2)}) copy-start(bf16[512,512]{1,0:T(8,128)(2,1)} %wout_ref.1) | copy-start | bytes 1572868
  45.5 1.4 %copy-start.6 = (f32[4,1024,128]{2,1,0:T(8,128)}, f32[4,1024,128]{2,1,0:T(8,128)S(1)}, u32[]{:S(2)}) copy-start(f32[4,1024,128]{2,1,0:T(8,128)S(1)} %get-tuple-element.36.hat) | copy-start | bytes 6291460
  46.9 1.9 %copy-start.8 = (f32[4,1024,256]{2,1,0:T(8,128)}, f32[4,1024,256]{2,1,0:T(8,128)S(1)}, u32[]{:S(2)}) copy-start(f32[4,1024,256]{2,1,0:T(8,128)S(1)} %get-tuple-element.33.prob_ref) | copy-start | bytes 12582916
  48.9 1.7 %copy-start.10 = (bf16[1024,1536]{1,0:T(8,128)(2,1)}, bf16[1024,1536]{1,0:T(8,128)(2,1)S(1)}, u32[]{:S(2)}) copy-start(bf16[1024,1536]{1,0:T(8,128)(2,1)S(1)} %get-tuple-element.32.proj) | copy-start | bytes 9437188
  50.6 1.0 copy-start.12
  51.5 1.0 copy-start.14
  52.5 2.2 %copy-start.9 = (f32[4,1024,256]{2,1,0:T(8,128)S(1)}, f32[4,1024,256]{2,1,0:T(8,128)}, u32[]{:S(2)}) copy-start(f32[4,1024,256]{2,1,0:T(8,128)} %copy-done.8) | copy-start | bytes 12582916
  54.7 1.9 %copy-start.11 = (bf16[1024,1536]{1,0:T(8,128)(2,1)S(1)}, bf16[1024,1536]{1,0:T(8,128)(2,1)}, u32[]{:S(2)}) copy-start(bf16[1024,1536]{1,0:T(8,128)(2,1)} %copy-done.10) | copy-start | bytes 9437188
  56.6 1.2 copy-start.13
  57.9 1.2 copy-start.15
  59.1 12.5 %copy-start.2 = (bf16[512,1536]{1,0:T(8,128)(2,1)S(1)}, bf16[512,1536]{1,0:T(8,128)(2,1)}, u32[]{:S(2)}) copy-start(bf16[512,1536]{1,0:T(8,128)(2,1)} %wqkv_ref.3) | copy-start | bytes 4718596
  59.1 12.5 %copy-start.7 = (f32[4,1024,128]{2,1,0:T(8,128)S(1)}, f32[4,1024,128]{2,1,0:T(8,128)}, u32[]{:S(2)}) copy-start(f32[4,1024,128]{2,1,0:T(8,128)} %copy-done.6) | copy-start | bytes 6291460
  69.3 6.3 %collective-permute-start = (bf16[528,1024]{1,0:T(8,128)(2,1)S(1)}, bf16[528,1024]{1,0:T(8,128)(2,1)S(1)}, u32[]{:S(2)}, u32[]{:S(2)}) collective-permute-start(bf16[528,1024]{1,0:T(8,128)(2,1)S(1)} %get-tuple-element.40), channel_id=1, source_target_pairs={{0,1},{1,0},{2,3},{3,2},{4,5},{5,4},{6,7},{7,6},{8,9},{9,8},{10,11... | collective-permute-start | bytes 3244040 | tf_op jit(solution)/shard_map/ppermute | solution.py:496
  120.9 0.6 copy-start
  121.5 4.4 %collective-permute-start.1 = (f32[56,128]{1,0:T(8,128)S(1)}, f32[56,128]{1,0:T(8,128)S(1)}, u32[]{:S(2)}, u32[]{:S(2)}) collective-permute-start(f32[56,128]{1,0:T(8,128)S(1)} %get-tuple-element.44), channel_id=1, source_target_pairs={{0,1},{1,0},{2,3},{3,2},{4,5},{5,4},{6,7},{7,6},{8,9},{9,8},{10,11... | collective-permute-start | bytes 86024 | tf_op jit(solution)/shard_map/ppermute | solution.py:496
  125.9 0.6 copy-start.16

commit v7 on v5

--- a/solution.py
+++ b/solution.py
@@ -28,7 +28,7 @@
 
 def forward_and_scores(
     pair_ref, wqkv_ref, wout_ref, bias_ref, gain_ref, shift_ref, gbias_ref,
-    normed, gproj, att, dyp, hat, istd, proj, gatt, dyf, head_dim,
+    normed, gproj, att, dyp, hat, istd, proj, gatt, dyf, head_dim, fetches,
 ):
     width = gproj.shape[1] // 3
     rows, groups, chunk = gproj.shape[0], gproj.shape[0] // MEMBERS, CHUNK
@@ -48,6 +48,8 @@
         return carry
 
     lax.fori_loop(0, rows // chunk, hat_step, 0)
+    for fetch in fetches:
+        fetch.wait()
 
     def by_group(ref, c):
         return jnp.concatenate(
@@ -169,41 +171,46 @@
     blocks, members, lanes = gbias_ref.shape
     i = lax.broadcasted_iota(jnp.int32, (lanes, 2 * lanes), 0)
     o = lax.broadcasted_iota(jnp.int32, (lanes, 2 * lanes), 1)
-    query = i % members
-    place = (i // members) * 128 + query // GRID * 16 + query % GRID
-    wide = (o == place).astype(f32).astype(bf16)
-    frames = []
+    query = GRID * GRID - 1 - i % members
+    wide = (o == i // members * 128 + query // GRID * 16 + query % GRID).astype(f32).astype(bf16)
+    spreads = []
     for b in range(blocks):
         value = gbias_ref[b]
         high = value.astype(bf16)
         rest = value - high.astype(f32)
         low = rest.astype(bf16)
         lowest = (rest - low.astype(f32)).astype(bf16)
-        spread = dot(jnp.concatenate([high, low, lowest], axis=0), wide, 1, 0)
-        spread = spread[:members] + (spread[members : 2 * members] + spread[2 * members :])
-        frames += [spread[None, :, h * 128 : (h + 1) * 128] for h in range(PACK)]
-    frame = jnp.concatenate(frames, axis=0)
-    heads = frame.shape[0]
-    frame = jnp.concatenate([frame, jnp.zeros_like(frame)], axis=2).reshape(heads * members, 256)
-    column = GRID - 1 - lax.broadcasted_iota(jnp.int32, frame.shape, 0) % GRID
-    for bit in (1, 2, 4):
-        frame = jnp.where((column & bit) != 0, pltpu.roll(frame, bit, 1), frame)
-    frame = jnp.sum(frame.reshape(heads * GRID, GRID, 256), axis=1)
-    row = GRID - 1 - lax.broadcasted_iota(jnp.int32, frame.shape, 0) % GRID
-    for bit in (1, 2, 4):
-        frame = jnp.where((row & bit) != 0, pltpu.roll(frame, 16 * bit, 1), frame)
-    return jnp.sum(frame.reshape(heads, GRID, 256), axis=1)
+        parts = dot(jnp.concatenate([high, low, lowest], axis=0), wide, 1, 0)
+        spreads.append(parts[:members] + (parts[members : 2 * members] + parts[2 * members :]))
+    sums = []
+    for b in range(blocks):
+        for h in range(PACK):
+            frame = spreads[b][:, h * 128 : (h + 1) * 128]
+            total = None
+            for row in range(GRID):
+                piece = frame[row * GRID : (row + 1) * GRID]
+                piece = jnp.concatenate([piece, jnp.zeros_like(piece)], axis=1)
+                piece = pltpu.roll(piece, row * 16, 1, stride=1, stride_axis=0)
+                total = piece if total is None else total + piece
+            sums.append(jnp.sum(total, axis=0, keepdims=True))
+    return jnp.concatenate(sums, axis=0)
 
 
 def scores_kernel(
-    core_ref, pair_ref, wqkv_ref, wout_ref, bias_ref, gain_ref, shift_ref,
-    keep_ref, send_ref, table_ref, gproj, hat, istd,
-    gbias_ref, normed, att, dyp, proj, gatt, dyf, *, head_dim,
+    core_ref, pair_ref, wqkv_hbm, wout_hbm, bias_ref, gain_ref, shift_ref,
+    keep_ref, send_ref, table_ref, gproj, hat, istd, wqkv_ref,
+    wout_ref, gbias_ref, normed, att, dyp, proj, gatt, dyf, sems, *, head_dim,
 ):
+    fetches = [
+        pltpu.make_async_copy(wqkv_hbm, wqkv_ref, sems.at[0]),
+        pltpu.make_async_copy(wout_hbm, wout_ref, sems.at[1]),
+    ]
+    for fetch in fetches:
+        fetch.start()
     gbias_ref[...] = jnp.zeros_like(gbias_ref)
     forward_and_scores(
         pair_ref, wqkv_ref, wout_ref, bias_ref, gain_ref, shift_ref, gbias_ref,
-        normed, gproj, att, dyp, hat, istd, proj, gatt, dyf, head_dim,
+        normed, gproj, att, dyp, hat, istd, proj, gatt, dyf, head_dim, fetches,
     )
     width = wout_ref.shape[0]
     half = 2 * width
@@ -237,7 +244,12 @@
 
 VMEM = pl.BlockSpec(memory_space=pltpu.VMEM)
 SMEM = pl.BlockSpec(memory_space=pltpu.SMEM)
+HBM = pl.BlockSpec(memory_space=pltpu.HBM)
 MIB = 1024 * 1024
+
+
+def in_hbm(a):
+    return pltpu.with_memory_space_constraint(a, pltpu.HBM)
 
 
 def shaped(*shape, dtype=jnp.float32):
@@ -267,15 +279,17 @@
         out_shape=(
             shaped(width, 2 * width), shaped(width + 16, 2 * width, dtype=bf16), shaped(half_heads, 256)
         )
-        + tuple(jax.ShapeDtypeStruct(*b) for b in (gproj, hat, istd)),
-        in_specs=[SMEM] + [VMEM] * 6,
-        out_specs=(VMEM,) * 6,
-        scratch_shapes=[pltpu.VMEM(bias.shape, f32)]
-        + [pltpu.VMEM(*b) for b in (normed, att, dyp, proj, gatt, dyf)],
+        + tuple(jax.ShapeDtypeStruct(*b) for b in (gproj, hat, istd))
+        + (jax.ShapeDtypeStruct(wqkv.shape, wqkv.dtype),),
+        in_specs=[SMEM, VMEM, HBM, HBM] + [VMEM] * 3,
+        out_specs=(VMEM,) * 7,
+        scratch_shapes=[pltpu.VMEM(wout.shape, wout.dtype), pltpu.VMEM(bias.shape, f32)]
+        + [pltpu.VMEM(*b) for b in (normed, att, dyp, proj, gatt, dyf)]
+        + [pltpu.SemaphoreType.DMA((2,))],
         compiler_params=pltpu.CompilerParams(vmem_limit_bytes=28 * MIB),
         cost_estimate=cost(20_000_000_000, 8 << 20),
         name="scores",
-    )(core.reshape(1), pair, wqkv, wout, bias, gain.reshape(1, width), shift.reshape(1, width))
+    )(core.reshape(1), pair, in_hbm(wqkv), in_hbm(wout), bias, gain.reshape(1, width), shift.reshape(1, width))
 
 
 def local_back(wqkv, gain, gproj, hat, istd, groups):
@@ -299,7 +313,7 @@
 
 def pair_of(x, dy):
     chips, groups, width = x.shape
-    step = chips // 4
+    step = chips // 2
     source = pl.BlockSpec((step, groups, width), lambda i: (i, 0, 0))
     return pl.pallas_call(
         pair_kernel,
@@ -430,7 +444,8 @@
     side = 2 * GRID - 1
     place = lax.broadcasted_iota(jnp.int32, (256, side * side), 0)
     offset = lax.broadcasted_iota(jnp.int32, (256, side * side), 1)
-    pick = (place == offset // side * 16 + offset % side).astype(jnp.float32)
+    row, column = side - 1 - offset // side, side - 1 - offset % side
+    pick = (place == row * 16 + column).astype(jnp.float32)
     table_ref[...] = lax.dot_general(
         table, pick, (((1,), (0,)), ((), ())), precision=lax.Precision.HIGHEST, preferred_element_type=jnp.float32
     )
@@ -449,6 +464,7 @@
         ),
         in_specs=[SMEM, VMEM, VMEM],
         out_specs=(VMEM,) * 5,
+        compiler_params=pltpu.CompilerParams(vmem_limit_bytes=8 * MIB),
         name="finish",
     )(core.reshape(1), keep, recv)
 
@@ -491,11 +507,11 @@
     dy = cotangent.reshape(chips, owned, width)
     exchange = functools.partial(lax.all_to_all, axis_name=CHIPS, split_axis=0, concat_axis=0, tiled=True)
     got = exchange(pair_of(x, dy))
-    keep, send, table, gproj, hat, istd = local_scores(
+    keep, send, table, gproj, hat, istd, qkv_copy = local_scores(
         core, got, qkv_weight, out_weight, bias, norm_gain, norm_shift, width // heads
     )
     recv = swap(send, "core", 1)
-    branch, gvec = local_back(qkv_weight, norm_gain, gproj, hat, istd, owned)
+    branch, gvec = local_back(qkv_copy, norm_gain, gproj, hat, istd, owned)
     got = exchange(outgoing(branch, keep, recv, table, gvec))
     factor = float(tile_h * tile_w * devices) ** (-0.5)
     share = width // chips

time: 118 us -> 113 us (0.958)
  local copies, waits for them, and re-layouts: 3.48 us -> 0.42 us
  Pallas kernels: 28.9 us -> 26.2 us
  waiting for transfers between devices: 21.5 us -> 23.3 us
    unnamed x16 -> x8, local copies, waits for them, and re-layouts: 2.04 us -> 0.02 us
    all_to_all x1, waiting for transfers between devices: 21.5 us -> 23.3 us  [local(): got = exchange(pair_of(x, dy))]
    pallas_call x1, Pallas kernels: 3.79 us -> 2.61 us  [pair_of(): pl.pallas_call(pair_kernel, grid=(chips // step,), out_shape=shaped(chips...]
  transfers between devices with their start and end apart: 3 -> 3, of which waited for: 1 -> 1; matrix products, arithmetic and copies ran while one was open for 5% -> 3% of each run, Pallas kernels for 5% -> 5%
where the time goes in v7:
time: 113 us
  blocking collectives  41.9 us (37%)
  Pallas kernels  26.2 us (23%)
  waiting for transfers between devices  23.3 us (21%)
  starting transfers between devices  17 us (15%)
  matrix products  3.2 us (3%)
    all_to_all x1, blocking collectives, local(): got = exchange(outgoing(branch, keep, recv, table, gvec))  41.9 us
    all_to_all x1, waiting for transfers between devices, local(): got = exchange(pair_of(x, dy))  23.3 us
    pallas_call x1, Pallas kernels, local_scores(): pl.pallas_call(functools.partial(scores_kernel, head_dim=head_dim), out_s...  16.7 us
    all_to_all x1, starting transfers between devices, local(): got = exchange(pair_of(x, dy))  12.1 us
    ppermute x2, starting transfers between devices, swap(): return lax.ppermute(a, axis, [(i, i ^ mask) for i in range(size)])  4.93 us
    pallas_call x1, Pallas kernels, local_back(): pl.pallas_call(back_kernel, out_shape=(shaped(MEMBERS, groups, width, dty...  4.02 us
    dot_general x1, matrix products, local(): jnp.einsum('bhr,kqr->bkhq', bias_table.reshape(heads // PACK, PACK, offse...  3.2 us
    pallas_call x1, Pallas kernels, pair_of(): pl.pallas_call(pair_kernel, grid=(chips // step,), out_shape=shaped(chips...  2.61 us
  transfers between devices with their start and end apart: 3, of which 1 were waited for; matrix products, arithmetic and copies ran while one was open for 3% of the time, Pallas kernels for 5%

profile of v7, /device:TPU:1, one launch (start us, length us, event | category | flops | bytes accessed | tf_op | source)
XLA Modules:
  0.0 112.9 jit_solution(14940660181347389449)
XLA Ops:
  0.6 2.6 %pair.1 = bf16[64,2,16,512]{3,2,1,0:T(8,128)(2,1)} custom-call(bf16[64,16,512]{2,1,0:T(8,128)(2,1)} %bitcast.25, bf16[64,16,512]{2,1,0:T(8,128)(2,1)} %bitcast.20), custom_call_target="tpu_custom_call" | custom-call | bytes 4194304 | tf_op jit(solution)/shard_map/pair/pallas_call | solution.py:318
  3.2 12.1 %all-to-all-start = ((bf16[64,2,16,512]{3,2,1,0:T(8,128)(2,1)}), bf16[64,2,16,512]{3,2,1,0:T(8,128)(2,1)S(1)}, u32[]{:S(2)}, u32[]{:S(2)}) async-start(bf16[64,2,16,512]{3,2,1,0:T(8,128)(2,1)} %pair.1), calls=%async_computation | async-start | bytes 4194304 | tf_op jit(solution)/shard_map/all_to_all | solution.py:509
  15.3 0.0 copy-start.1
  15.4 0.0 copy-start.2
  15.4 0.0 copy-done.3
  15.4 0.1 add_add_fusion
  15.5 3.2 %fusion.4 = f32[4,64,4,64]{3,2,0,1:T(4,128)S(1)} fusion(f32[4,4,225,1]{2,1,0,3:T(4,128)S(1)} %reshape.218, s32[64,64]{1,0:T(8,128)S(1)} %add_add_fusion), kind=kOutput, calls=%fused_computation.4 | convolution fusion | flops 177868800 | bytes 292928 | tf_op jit(solution)/shard_map/bhr,kqr->bkhq/dot_general | solution.py:500
  18.7 0.3 reshape.220
  19.1 0.1 copy.15.bias_ref
  19.1 23.3 %all-to-all-done.pair_ref = bf16[64,2,16,512]{3,2,1,0:T(8,128)(2,1)S(1)} async-done(((bf16[64,2,16,512]{3,2,1,0:T(8,128)(2,1)}), bf16[64,2,16,512]{3,2,1,0:T(8,128)(2,1)S(1)}, u32[]{:S(2)}, u32[]{:S(2)}) %all-to-all-start) | async-done | bytes 2097184 | tf_op jit(solution)/shard_map/all_to_all | solution.py:509
  42.4 0.0 copy-done.1
  42.4 0.0 copy-done.2
  42.4 16.7 %scores.1 = (f32[512,1024]{1,0:T(8,128)S(1)}, bf16[528,1024]{1,0:T(8,128)(2,1)S(1)}, f32[8,256]{1,0:T(8,128)S(1)}, bf16[1024,1536]{1,0:T(8,128)(2,1)S(1)}, f32[4...) custom-call(s32[1]{0:T(128)} %bitcast.core_ref, ...), custom_call_target="tpu_custom_call" | custom-call | flops 20000000000 | bytes 8388608 | tf_op jit(solution)/shard_map/scores/pallas_call | solution.py:277
  59.1 3.0 %collective-permute-start = (bf16[528,1024]{1,0:T(8,128)(2,1)S(1)}, bf16[528,1024]{1,0:T(8,128)(2,1)S(1)}, u32[]{:S(2)}, u32[]{:S(2)}) collective-permute-start(bf16[528,1024]{1,0:T(8,128)(2,1)S(1)} %get-tuple-element.28), channel_id=1, source_target_pairs={{0,1},{1,0},{2,3},{3,2},{4,5},{5,4},{6,7},{7,6},{8,9},{9,8},{10,11... | collective-permute-start | bytes 3244040 | tf_op jit(solution)/shard_map/ppermute | solution.py:489
  62.1 4.0 %back.1 = (bf16[64,16,512]{2,1,0:T(8,128)(2,1)S(1)}, f32[8,128]{1,0:T(8,128)S(1)}) custom-call(bf16[512,1536]{1,0:T(8,128)(2,1)S(1)} %get-tuple-element.22.wqkv_ref, f32[1,512]{1,0:T(1,128)S(1)} %bitcast.24, bf16[1024,1536]{1,0:T(8,128)(2,1)S(1)} %get-tuple-element.23.gproj, f32[4,1024,128]{2,1,0:T(8,128)S(1)} %get-tuple-element.24.hat, ...), custom_call_target="tpu_custom_call" | custom-call | flops 6000000000 | bytes 4194304 | tf_op jit(solution)/shard_map/back/pallas_call | solution.py:297
  66.1 0.0 collective-permute-done.recv_ref
  66.1 0.5 outgoing.1
  66.6 41.9 %all_to_all.10.got_ref = bf16[64,19,8,128]{3,2,1,0:T(8,128)(2,1)S(1)} all-to-all(bf16[64,19,8,128]{3,2,1,0:T(8,128)(2,1)S(1)} %outgoing.1), channel_id=1, replica_groups=mesh['x_lo'=2,'y'=4,'x_hi'=2,'z'=4,'core'=2] {'x_lo','y','x_hi','z'}, dimensions={0} | all-to-all | bytes 4980736 | tf_op jit(solution)/shard_map/all_to_all | solution.py:515
  108.5 0.2 sums.1
  108.8 1.9 %collective-permute-start.1 = (f32[56,128]{1,0:T(8,128)S(1)}, f32[56,128]{1,0:T(8,128)S(1)}, u32[]{:S(2)}, u32[]{:S(2)}) collective-permute-start(f32[56,128]{1,0:T(8,128)S(1)} %get-tuple-element.32), channel_id=1, source_target_pairs={{0,1},{1,0},{2,3},{3,2},{4,5},{5,4},{6,7},{7,6},{8,9},{9,8},{10,11... | collective-permute-start | bytes 86024 | tf_op jit(solution)/shard_map/ppermute | solution.py:489
  110.7 0.0 copy-done
  110.7 1.3 %input_gradient.1 = bf16[64,16,512]{2,1,0:T(8,128)(2,1)} custom-call(bf16[64,19,8,128]{3,2,1,0:T(8,128)(2,1)S(1)} %all_to_all.10.got_ref, bf16[64,16,512]{2,1,0:T(8,128)(2,1)S(1)} %bitcast.21), custom_call_target="tpu_custom_call" | custom-call | bytes 4194304 | tf_op jit(solution)/shard_map/input_gradient/pallas_call | solution.py:413
  112.0 0.0 collective-permute-done.1.recv_ref
  112.0 0.8 finish.1
  (4 shorter events, 0.0 us)
Async XLA Ops:
  3.2 12.1 %copy-start.3 = (f32[16,225]{1,0:T(8,128)S(1)}, f32[16,225]{1,0:T(8,128)}, u32[]{:S(2)}) copy-start(f32[16,225]{1,0:T(8,128)} %param.11) | copy-start | bytes 43204
  3.2 39.2 %all-to-all-start = ((bf16[64,2,16,512]{3,2,1,0:T(8,128)(2,1)}), bf16[64,2,16,512]{3,2,1,0:T(8,128)(2,1)S(1)}, u32[]{:S(2)}, u32[]{:S(2)}) async-start(bf16[64,2,16,512]{3,2,1,0:T(8,128)(2,1)} %pair.1), calls=%async_computation | async-start | bytes 4194304 | tf_op jit(solution)/shard_map/all_to_all | solution.py:509
  15.3 27.1 %copy-start.1 = (f32[512]{0:T(512)S(1)}, f32[512]{0:T(512)}, u32[]{:S(2)}) copy-start(f32[512]{0:T(512)} %param.13) | copy-start | bytes 6148
  15.4 27.0 %copy-start.2 = (f32[512]{0:T(512)S(1)}, f32[512]{0:T(512)}, u32[]{:S(2)}) copy-start(f32[512]{0:T(512)} %param.12) | copy-start | bytes 6148
  59.1 7.0 %collective-permute-start = (bf16[528,1024]{1,0:T(8,128)(2,1)S(1)}, bf16[528,1024]{1,0:T(8,128)(2,1)S(1)}, u32[]{:S(2)}, u32[]{:S(2)}) collective-permute-start(bf16[528,1024]{1,0:T(8,128)(2,1)S(1)} %get-tuple-element.28), channel_id=1, source_target_pairs={{0,1},{1,0},{2,3},{3,2},{4,5},{5,4},{6,7},{7,6},{8,9},{9,8},{10,11... | collective-permute-start | bytes 3244040 | tf_op jit(solution)/shard_map/ppermute | solution.py:489
  108.5 2.2 %copy-start = (bf16[16,64,512]{2,1,0:T(8,128)(2,1)S(1)}, bf16[16,64,512]{2,1,0:T(8,128)(2,1)}, u32[]{:S(2)}) copy-start(bf16[16,64,512]{2,1,0:T(8,128)(2,1)} %param.8) | copy-start | bytes 3145732
  108.8 3.2 %collective-permute-start.1 = (f32[56,128]{1,0:T(8,128)S(1)}, f32[56,128]{1,0:T(8,128)S(1)}, u32[]{:S(2)}, u32[]{:S(2)}) collective-permute-start(f32[56,128]{1,0:T(8,128)S(1)} %get-tuple-element.32), channel_id=1, source_target_pairs={{0,1},{1,0},{2,3},{3,2},{4,5},{5,4},{6,7},{7,6},{8,9},{9,8},{10,11... | collective-permute-start | bytes 86024 | tf_op jit(solution)/shard_map/ppermute | solution.py:489

commit v8 on v7

--- a/solution.py
+++ b/solution.py
@@ -82,52 +82,54 @@
 
     blocks = range(width // 128)
 
-    def group_step(g, carry):
-        here = pl.ds(pl.multiple_of(g * MEMBERS, MEMBERS), MEMBERS)
-        cols = [slice(b * 128, (b + 1) * 128) for b in blocks]
-        kcols = [slice(width + b * 128, width + (b + 1) * 128) for b in blocks]
-        vcols = [slice(2 * width + b * 128, 2 * width + (b + 1) * 128) for b in blocks]
-        ks = [proj[here, c] for c in kcols]
-        vs = [proj[here, c] for c in vcols]
-        none = jnp.zeros_like(ks[0])
-        ws = [jnp.concatenate([spread(proj[here, c]), spread(gatt[here, c])], axis=1) for c in cols]
-        both = [
-            dot(
-                jnp.concatenate(
-                    [jnp.concatenate([k, none], axis=1), jnp.concatenate([none, v], axis=1)], axis=0
-                ),
-                w, 1, 1,
-            )
-            for k, v, w in zip(ks, vs, ws)
-        ]
-        pds = []
+    qcols = [slice(b * 128, (b + 1) * 128) for b in blocks]
+    kcols = [slice(width + b * 128, width + (b + 1) * 128) for b in blocks]
+    vcols = [slice(2 * width + b * 128, 2 * width + (b + 1) * 128) for b in blocks]
+
+    def stacked(top, low):
+        none = jnp.zeros_like(top)
+        return jnp.concatenate(
+            [jnp.concatenate([top, none], axis=1), jnp.concatenate([none, low], axis=1)], axis=0
+        )
+
+    def products(g):
+        here = slice(g * MEMBERS, (g + 1) * MEMBERS)
+        ws = [jnp.concatenate([spread(proj[here, c]), spread(gatt[here, c])], axis=1) for c in qcols]
+        return ws, [dot(stacked(proj[here, k], proj[here, v]), w, 1, 1) for k, v, w in zip(kcols, vcols, ws)]
+
+    def softmax(b, both):
+        scores = both[:MEMBERS] * scale + bias_ref[b]
+        gp = both[MEMBERS:]
+        e = jnp.exp(scores - jnp.max(scores, axis=0, keepdims=True))
+        p = e * (1.0 / jnp.sum(e, axis=0, keepdims=True))
+        gs = p * (gp - jnp.sum(gp * p, axis=0, keepdims=True))
+        gbias_ref[b] += gs
+        return jnp.concatenate([p.astype(bf16), (gs * scale).astype(bf16)], axis=0)
+
+    def store(g, keyed, queried):
+        here = slice(g * MEMBERS, (g + 1) * MEMBERS)
         for b in blocks:
-            scores = both[b][:MEMBERS] * scale + bias_ref[b]
-            gp = both[b][MEMBERS:]
-            e = jnp.exp(scores - jnp.max(scores, axis=0, keepdims=True))
-            p = e * (1.0 / jnp.sum(e, axis=0, keepdims=True))
-            gs = p * (gp - jnp.sum(gp * p, axis=0, keepdims=True))
-            gbias_ref[b] += gs
-            pds.append(jnp.concatenate([p.astype(bf16), (gs * scale).astype(bf16)], axis=0))
-        keyed = [dot(pd, w, 1, 0) for pd, w in zip(pds, ws)]
-        queried = [
-            dot(
-                pd,
-                jnp.concatenate(
-                    [jnp.concatenate([v, none], axis=1), jnp.concatenate([none, k], axis=1)], axis=0
-                ),
-                0, 0,
-            )
-            for k, v, pd in zip(ks, vs, pds)
-        ]
-        for b in blocks:
-            att[here, cols[b]] = gather(queried[b][:, :128]).astype(bf16)
-            gproj[here, cols[b]] = gather(queried[b][:, 128:]).astype(bf16)
+            att[here, qcols[b]] = gather(queried[b][:, :128]).astype(bf16)
+            gproj[here, qcols[b]] = gather(queried[b][:, 128:]).astype(bf16)
             gproj[here, kcols[b]] = keyed[b][MEMBERS:, :128].astype(bf16)
             gproj[here, vcols[b]] = keyed[b][:MEMBERS, 128:].astype(bf16)
-        return carry
-
-    lax.fori_loop(0, groups, group_step, 0, unroll=4)
+
+    ahead, behind = products(0), None
+    for g in range(groups):
+        here = slice(g * MEMBERS, (g + 1) * MEMBERS)
+        ws, both = ahead
+        keyed, queried, ws_next, both_next = [], [], [], []
+        more = products(g + 1) if g + 1 < groups else ([], [])
+        ws_next, both_next = more
+        for b in blocks:
+            pd = softmax(b, both[b])
+            keyed.append(dot(pd, ws[b], 1, 0))
+            queried.append(dot(pd, stacked(proj[here, vcols[b]], proj[here, kcols[b]]), 0, 0))
+        if behind is not None:
+            store(g - 1, *behind)
+        behind = (keyed, queried)
+        ahead = (ws_next, both_next)
+    store(groups - 1, *behind)
 
 
 def back_to_input(wqkv_ref, gain_ref, branch_ref, gproj, hat, istd, dyf):

time: 113 us -> 110 us (0.973)
  Pallas kernels: 26.2 us -> 22.9 us
    pallas_call x1, Pallas kernels: 16.7 us -> 13.3 us  [local_scores(): pl.pallas_call(functools.partial(scores_kernel, head_dim=head_dim), out_s...]
where the time goes in v8:
time: 110 us; the launch traced here: 109 us
  blocking collectives  41.9 us (38%)
  waiting for transfers between devices  23.3 us (21%)
  Pallas kernels  22.9 us (21%)
  starting transfers between devices  16.9 us (15%)
  matrix products  3.2 us (3%)
    all_to_all x1, blocking collectives, local(): got = exchange(outgoing(branch, keep, recv, table, gvec))  41.9 us
    all_to_all x1, waiting for transfers between devices, local(): got = exchange(pair_of(x, dy))  23.3 us
    pallas_call x1, Pallas kernels, local_scores(): pl.pallas_call(functools.partial(scores_kernel, head_dim=head_dim), out_s...  13.3 us
    all_to_all x1, starting transfers between devices, local(): got = exchange(pair_of(x, dy))  12.1 us
    ppermute x2, starting transfers between devices, swap(): return lax.ppermute(a, axis, [(i, i ^ mask) for i in range(size)])  4.77 us
    pallas_call x1, Pallas kernels, local_back(): pl.pallas_call(back_kernel, out_shape=(shaped(MEMBERS, groups, width, dty...  4.02 us
    dot_general x1, matrix products, local(): jnp.einsum('bhr,kqr->bkhq', bias_table.reshape(heads // PACK, PACK, offse...  3.2 us
    pallas_call x1, Pallas kernels, pair_of(): pl.pallas_call(pair_kernel, grid=(chips // step,), out_shape=shaped(chips...  2.61 us
  transfers between devices with their start and end apart: 3, of which 1 were waited for; matrix products, arithmetic and copies ran while one was open for 3% of the time, Pallas kernels for 5%

profile of v8, /device:TPU:1, one launch (start us, length us, event | category | flops | bytes accessed | tf_op | source)
XLA Modules:
  0.0 109.3 jit_solution(17567939866314810263)
XLA Ops:
  0.6 2.6 %pair.1 = bf16[64,2,16,512]{3,2,1,0:T(8,128)(2,1)} custom-call(bf16[64,16,512]{2,1,0:T(8,128)(2,1)} %bitcast.25, bf16[64,16,512]{2,1,0:T(8,128)(2,1)} %bitcast.20), custom_call_target="tpu_custom_call" | custom-call | bytes 4194304 | tf_op jit(solution)/shard_map/pair/pallas_call | solution.py:320
  3.2 12.1 %all-to-all-start = ((bf16[64,2,16,512]{3,2,1,0:T(8,128)(2,1)}), bf16[64,2,16,512]{3,2,1,0:T(8,128)(2,1)S(1)}, u32[]{:S(2)}, u32[]{:S(2)}) async-start(bf16[64,2,16,512]{3,2,1,0:T(8,128)(2,1)} %pair.1), calls=%async_computation | async-start | bytes 4194304 | tf_op jit(solution)/shard_map/all_to_all | solution.py:511
  15.3 0.0 copy-start.1
  15.4 0.0 copy-start.2
  15.4 0.0 copy-done.3
  15.4 0.1 add_add_fusion
  15.5 3.2 %fusion.4 = f32[4,64,4,64]{3,2,0,1:T(4,128)S(1)} fusion(f32[4,4,225,1]{2,1,0,3:T(4,128)S(1)} %reshape.218, s32[64,64]{1,0:T(8,128)S(1)} %add_add_fusion), kind=kOutput, calls=%fused_computation.4 | convolution fusion | flops 177868800 | bytes 292928 | tf_op jit(solution)/shard_map/bhr,kqr->bkhq/dot_general | solution.py:502
  18.7 0.3 reshape.220
  19.1 0.1 copy.15.bias_ref
  19.1 23.3 %all-to-all-done.pair_ref = bf16[64,2,16,512]{3,2,1,0:T(8,128)(2,1)S(1)} async-done(((bf16[64,2,16,512]{3,2,1,0:T(8,128)(2,1)}), bf16[64,2,16,512]{3,2,1,0:T(8,128)(2,1)S(1)}, u32[]{:S(2)}, u32[]{:S(2)}) %all-to-all-start) | async-done | bytes 2097184 | tf_op jit(solution)/shard_map/all_to_all | solution.py:511
  42.4 0.0 copy-done.1
  42.4 0.0 copy-done.2
  42.4 13.3 %scores.1 = (f32[512,1024]{1,0:T(8,128)S(1)}, bf16[528,1024]{1,0:T(8,128)(2,1)S(1)}, f32[8,256]{1,0:T(8,128)S(1)}, bf16[1024,1536]{1,0:T(8,128)(2,1)S(1)}, f32[4...) custom-call(s32[1]{0:T(128)} %bitcast.core_ref, ...), custom_call_target="tpu_custom_call" | custom-call | flops 20000000000 | bytes 8388608 | tf_op jit(solution)/shard_map/scores/pallas_call | solution.py:279
  55.8 2.8 %collective-permute-start = (bf16[528,1024]{1,0:T(8,128)(2,1)S(1)}, bf16[528,1024]{1,0:T(8,128)(2,1)S(1)}, u32[]{:S(2)}, u32[]{:S(2)}) collective-permute-start(bf16[528,1024]{1,0:T(8,128)(2,1)S(1)} %get-tuple-element.28), channel_id=1, source_target_pairs={{0,1},{1,0},{2,3},{3,2},{4,5},{5,4},{6,7},{7,6},{8,9},{9,8},{10,11... | collective-permute-start | bytes 3244040 | tf_op jit(solution)/shard_map/ppermute | solution.py:491
  58.6 4.0 %back.1 = (bf16[64,16,512]{2,1,0:T(8,128)(2,1)S(1)}, f32[8,128]{1,0:T(8,128)S(1)}) custom-call(bf16[512,1536]{1,0:T(8,128)(2,1)S(1)} %get-tuple-element.22.wqkv_ref, f32[1,512]{1,0:T(1,128)S(1)} %bitcast.24, bf16[1024,1536]{1,0:T(8,128)(2,1)S(1)} %get-tuple-element.23.gproj, f32[4,1024,128]{2,1,0:T(8,128)S(1)} %get-tuple-element.24.hat, ...), custom_call_target="tpu_custom_call" | custom-call | flops 6000000000 | bytes 4194304 | tf_op jit(solution)/shard_map/back/pallas_call | solution.py:299
  62.6 0.0 collective-permute-done.recv_ref
  62.6 0.5 outgoing.1
  63.1 41.9 %all_to_all.10.got_ref = bf16[64,19,8,128]{3,2,1,0:T(8,128)(2,1)S(1)} all-to-all(bf16[64,19,8,128]{3,2,1,0:T(8,128)(2,1)S(1)} %outgoing.1), channel_id=1, replica_groups=mesh['x_lo'=2,'y'=4,'x_hi'=2,'z'=4,'core'=2] {'x_lo','y','x_hi','z'}, dimensions={0} | all-to-all | bytes 4980736 | tf_op jit(solution)/shard_map/all_to_all | solution.py:517
  105.0 0.2 sums.1
  105.2 1.9 %collective-permute-start.1 = (f32[56,128]{1,0:T(8,128)S(1)}, f32[56,128]{1,0:T(8,128)S(1)}, u32[]{:S(2)}, u32[]{:S(2)}) collective-permute-start(f32[56,128]{1,0:T(8,128)S(1)} %get-tuple-element.32), channel_id=1, source_target_pairs={{0,1},{1,0},{2,3},{3,2},{4,5},{5,4},{6,7},{7,6},{8,9},{9,8},{10,11... | collective-permute-start | bytes 86024 | tf_op jit(solution)/shard_map/ppermute | solution.py:491
  107.2 0.0 copy-done
  107.2 1.3 %input_gradient.1 = bf16[64,16,512]{2,1,0:T(8,128)(2,1)} custom-call(bf16[64,19,8,128]{3,2,1,0:T(8,128)(2,1)S(1)} %all_to_all.10.got_ref, bf16[64,16,512]{2,1,0:T(8,128)(2,1)S(1)} %bitcast.21), custom_call_target="tpu_custom_call" | custom-call | bytes 4194304 | tf_op jit(solution)/shard_map/input_gradient/pallas_call | solution.py:415
  108.5 0.0 collective-permute-done.1.recv_ref
  108.5 0.8 finish.1
  (4 shorter events, 0.0 us)
Async XLA Ops:
  3.2 12.1 %copy-start.3 = (f32[16,225]{1,0:T(8,128)S(1)}, f32[16,225]{1,0:T(8,128)}, u32[]{:S(2)}) copy-start(f32[16,225]{1,0:T(8,128)} %param.11) | copy-start | bytes 43204
  3.2 39.2 %all-to-all-start = ((bf16[64,2,16,512]{3,2,1,0:T(8,128)(2,1)}), bf16[64,2,16,512]{3,2,1,0:T(8,128)(2,1)S(1)}, u32[]{:S(2)}, u32[]{:S(2)}) async-start(bf16[64,2,16,512]{3,2,1,0:T(8,128)(2,1)} %pair.1), calls=%async_computation | async-start | bytes 4194304 | tf_op jit(solution)/shard_map/all_to_all | solution.py:511
  15.3 27.1 %copy-start.1 = (f32[512]{0:T(512)S(1)}, f32[512]{0:T(512)}, u32[]{:S(2)}) copy-start(f32[512]{0:T(512)} %param.13) | copy-start | bytes 6148
  15.4 27.0 %copy-start.2 = (f32[512]{0:T(512)S(1)}, f32[512]{0:T(512)}, u32[]{:S(2)}) copy-start(f32[512]{0:T(512)} %param.12) | copy-start | bytes 6148
  55.8 6.8 %collective-permute-start = (bf16[528,1024]{1,0:T(8,128)(2,1)S(1)}, bf16[528,1024]{1,0:T(8,128)(2,1)S(1)}, u32[]{:S(2)}, u32[]{:S(2)}) collective-permute-start(bf16[528,1024]{1,0:T(8,128)(2,1)S(1)} %get-tuple-element.28), channel_id=1, source_target_pairs={{0,1},{1,0},{2,3},{3,2},{4,5},{5,4},{6,7},{7,6},{8,9},{9,8},{10,11... | collective-permute-start | bytes 3244040 | tf_op jit(solution)/shard_map/ppermute | solution.py:491
  105.0 2.2 %copy-start = (bf16[16,64,512]{2,1,0:T(8,128)(2,1)S(1)}, bf16[16,64,512]{2,1,0:T(8,128)(2,1)}, u32[]{:S(2)}) copy-start(bf16[16,64,512]{2,1,0:T(8,128)(2,1)} %param.8) | copy-start | bytes 3145732
  105.2 3.3 %collective-permute-start.1 = (f32[56,128]{1,0:T(8,128)S(1)}, f32[56,128]{1,0:T(8,128)S(1)}, u32[]{:S(2)}, u32[]{:S(2)}) collective-permute-start(f32[56,128]{1,0:T(8,128)S(1)} %get-tuple-element.32), channel_id=1, source_target_pairs={{0,1},{1,0},{2,3},{3,2},{4,5},{5,4},{6,7},{7,6},{8,9},{9,8},{10,11... | collective-permute-start | bytes 86024 | tf_op jit(solution)/shard_map/ppermute | solution.py:491

commit v9 on v8

--- a/solution.py
+++ b/solution.py
@@ -164,7 +164,7 @@
         return gg, gsh
 
     zero = jnp.zeros((8, width), f32)
-    gg, gsh = lax.fori_loop(0, rows // chunk, back_step, (zero, zero))
+    gg, gsh = lax.fori_loop(0, rows // chunk, back_step, (zero, zero), unroll=True)
     return jnp.sum(gg, axis=0, keepdims=True), jnp.sum(gsh, axis=0, keepdims=True)
 
 
@@ -223,17 +223,16 @@
     send_ref[width:, :] = jnp.zeros((send_ref.shape[0] - width, half), send_ref.dtype)
     send_ref[width : width + heads, :256] = jnp.where(first, table[heads:], table[:heads]).astype(send_ref.dtype)
 
-    @pl.when(first)
-    def _():
-        keep_ref[...] = dot(normed[...], gproj[:, :half], 0, 0)
-        send_ref[:width, :width] = dot(normed[...], gproj[:, half:], 0, 0).astype(send_ref.dtype)
-        send_ref[:width, width:] = dot(att[...], dyp[...], 0, 0).astype(send_ref.dtype)
-
-    @pl.when(jnp.logical_not(first))
-    def _():
-        send_ref[:width, :] = dot(normed[...], gproj[:, :half], 0, 0).astype(send_ref.dtype)
-        keep_ref[:, :width] = dot(normed[...], gproj[:, half:], 0, 0)
-        keep_ref[:, width:] = dot(att[...], dyp[...], 0, 0)
+    turned = normed[...].T
+    for piece in range(4):
+        cols = slice(piece * 256, (piece + 1) * 256)
+        low = dot(turned, gproj[:, cols], 1, 0)
+        if piece < 2:
+            high = dot(turned, gproj[:, half + piece * 256 : half + (piece + 1) * 256], 1, 0)
+        else:
+            high = dot(att[...], dyp[:, (piece - 2) * 256 : (piece - 1) * 256], 0, 0)
+        keep_ref[:, cols] = jnp.where(first, low, high)
+        send_ref[:width, cols] = jnp.where(first, high, low).astype(send_ref.dtype)
 
 
 def back_kernel(wqkv_ref, gain_ref, gproj, hat, istd, branch_ref, gvec_ref, dyf):
@@ -398,29 +397,33 @@
 
 
 def input_kernel(got_ref, dy_ref, grad_ref):
-    _, groups, width = dy_ref.shape
+    step, groups, width = dy_ref.shape
     share = got_ref.shape[2]
     f32 = jnp.float32
+    chips = pl.ds(pl.multiple_of(pl.program_id(0) * step, step), step)
     slot = 0
     for b in range(width // 128):
         cols = slice(b * 128, (b + 1) * 128)
         for t in range(groups // share):
             rows = slice(t * share, (t + 1) * share)
-            branch = got_ref[:, slot].astype(f32)
+            branch = got_ref[chips, slot].astype(f32)
             grad_ref[:, rows, cols] = (dy_ref[:, rows, cols].astype(f32) + branch).astype(grad_ref.dtype)
             slot += 1
 
 
 def input_gradient(got, dy):
+    chips, groups, width = dy.shape
+    block = pl.BlockSpec((chips // 2, groups, width), lambda i: (i, 0, 0))
     return pl.pallas_call(
         input_kernel,
+        grid=(2,),
         out_shape=jax.ShapeDtypeStruct(dy.shape, dy.dtype),
-        in_specs=[VMEM] * 2,
-        out_specs=VMEM,
+        in_specs=[VMEM, block],
+        out_specs=block,
         compiler_params=pltpu.CompilerParams(vmem_limit_bytes=16 * MIB),
         cost_estimate=cost(0, 4 << 20),
         name="input_gradient",
-    )(got, dy)
+    )(got, in_hbm(dy))
 
 
 def finish_kernel(core_ref, keep_ref, recv_ref, qkv_ref, out_ref, table_ref, gain_ref, shift_ref):

time: 110 us -> 110 us (level)
  no operation moved by 1% of the time
where the time goes in v9:
time: 110 us
  blocking collectives  41.9 us (38%)
  waiting for transfers between devices  23.3 us (21%)
  Pallas kernels  22.9 us (21%)
  starting transfers between devices  17.1 us (16%)
  matrix products  3.2 us (3%)
    all_to_all x1, blocking collectives, local(): got = exchange(outgoing(branch, keep, recv, table, gvec))  41.9 us
    all_to_all x1, waiting for transfers between devices, local(): got = exchange(pair_of(x, dy))  23.3 us
    pallas_call x1, Pallas kernels, local_scores(): pl.pallas_call(functools.partial(scores_kernel, head_dim=head_dim), out_s...  12.9 us
    all_to_all x1, starting transfers between devices, local(): got = exchange(pair_of(x, dy))  12.1 us
    ppermute x2, starting transfers between devices, swap(): return lax.ppermute(a, axis, [(i, i ^ mask) for i in range(size)])  4.96 us
    pallas_call x1, Pallas kernels, local_back(): pl.pallas_call(back_kernel, out_shape=(shaped(MEMBERS, groups, width, dty...  3.61 us
    dot_general x1, matrix products, local(): jnp.einsum('bhr,kqr->bkhq', bias_table.reshape(heads // PACK, PACK, offse...  3.2 us
    pallas_call x1, Pallas kernels, pair_of(): pl.pallas_call(pair_kernel, grid=(chips // step,), out_shape=shaped(chips...  2.61 us
  transfers between devices with their start and end apart: 3, of which 1 were waited for; matrix products, arithmetic and copies ran while one was open for 3% of the time, Pallas kernels for 5%

profile of v9, /device:TPU:1, one launch (start us, length us, event | category | flops | bytes accessed | tf_op | source)
XLA Modules:
  0.0 109.6 jit_solution(3132749001041674872)
XLA Ops:
  0.6 2.6 %pair.1 = bf16[64,2,16,512]{3,2,1,0:T(8,128)(2,1)} custom-call(bf16[64,16,512]{2,1,0:T(8,128)(2,1)} %bitcast.25, bf16[64,16,512]{2,1,0:T(8,128)(2,1)} %bitcast.23), custom_call_target="tpu_custom_call" | custom-call | bytes 4194304 | tf_op jit(solution)/shard_map/pair/pallas_call | solution.py:319
  3.2 0.0 copy-start.2
  3.2 12.1 %all-to-all-start = ((bf16[64,2,16,512]{3,2,1,0:T(8,128)(2,1)}), bf16[64,2,16,512]{3,2,1,0:T(8,128)(2,1)S(1)}, u32[]{:S(2)}, u32[]{:S(2)}) async-start(bf16[64,2,16,512]{3,2,1,0:T(8,128)(2,1)} %pair.1), calls=%async_computation | async-start | bytes 4194304 | tf_op jit(solution)/shard_map/all_to_all | solution.py:514
  15.3 0.0 copy-start
  15.4 0.0 copy-start.1
  15.4 0.0 copy-done.2
  15.4 0.1 add_add_fusion
  15.5 3.2 %fusion.4 = f32[4,64,4,64]{3,2,0,1:T(4,128)S(1)} fusion(f32[4,4,225,1]{2,1,0,3:T(4,128)S(1)} %reshape.218, s32[64,64]{1,0:T(8,128)S(1)} %add_add_fusion), kind=kOutput, calls=%fused_computation.4 | convolution fusion | flops 177868800 | bytes 292928 | tf_op jit(solution)/shard_map/bhr,kqr->bkhq/dot_general | solution.py:505
  18.7 0.3 reshape.220
  19.1 0.1 copy.15.bias_ref
  19.1 23.3 %all-to-all-done.pair_ref = bf16[64,2,16,512]{3,2,1,0:T(8,128)(2,1)S(1)} async-done(((bf16[64,2,16,512]{3,2,1,0:T(8,128)(2,1)}), bf16[64,2,16,512]{3,2,1,0:T(8,128)(2,1)S(1)}, u32[]{:S(2)}, u32[]{:S(2)}) %all-to-all-start) | async-done | bytes 2097184 | tf_op jit(solution)/shard_map/all_to_all | solution.py:514
  42.4 0.0 copy-done
  42.4 0.0 copy-done.1
  42.4 12.9 %scores.1 = (f32[512,1024]{1,0:T(8,128)S(1)}, bf16[528,1024]{1,0:T(8,128)(2,1)S(1)}, f32[8,256]{1,0:T(8,128)S(1)}, bf16[1024,1536]{1,0:T(8,128)(2,1)S(1)}, f32[4...) custom-call(s32[1]{0:T(128)} %bitcast.core_ref, ...), custom_call_target="tpu_custom_call" | custom-call | flops 20000000000 | bytes 8388608 | tf_op jit(solution)/shard_map/scores/pallas_call | solution.py:278
  55.3 3.0 %collective-permute-start = (bf16[528,1024]{1,0:T(8,128)(2,1)S(1)}, bf16[528,1024]{1,0:T(8,128)(2,1)S(1)}, u32[]{:S(2)}, u32[]{:S(2)}) collective-permute-start(bf16[528,1024]{1,0:T(8,128)(2,1)S(1)} %get-tuple-element.28), channel_id=1, source_target_pairs={{0,1},{1,0},{2,3},{3,2},{4,5},{5,4},{6,7},{7,6},{8,9},{9,8},{10,11... | collective-permute-start | bytes 3244040 | tf_op jit(solution)/shard_map/ppermute | solution.py:494
  58.3 3.6 %back.1 = (bf16[64,16,512]{2,1,0:T(8,128)(2,1)S(1)}, f32[8,128]{1,0:T(8,128)S(1)}) custom-call(bf16[512,1536]{1,0:T(8,128)(2,1)S(1)} %get-tuple-element.22.wqkv_ref, f32[1,512]{1,0:T(1,128)S(1)} %bitcast.22, bf16[1024,1536]{1,0:T(8,128)(2,1)S(1)} %get-tuple-element.23.gproj, f32[4,1024,128]{2,1,0:T(8,128)S(1)} %get-tuple-element.24.hat, ...), custom_call_target="tpu_custom_call" | custom-call | flops 6000000000 | bytes 4194304 | tf_op jit(solution)/shard_map/back/pallas_call | solution.py:298
  61.9 0.0 collective-permute-done.recv_ref
  61.9 0.5 outgoing.1
  62.5 41.9 %all_to_all.10.got_ref = bf16[64,19,8,128]{3,2,1,0:T(8,128)(2,1)S(1)} all-to-all(bf16[64,19,8,128]{3,2,1,0:T(8,128)(2,1)S(1)} %outgoing.1), channel_id=1, replica_groups=mesh['x_lo'=2,'y'=4,'x_hi'=2,'z'=4,'core'=2] {'x_lo','y','x_hi','z'}, dimensions={0} | all-to-all | bytes 4980736 | tf_op jit(solution)/shard_map/all_to_all | solution.py:520
  104.3 0.2 sums.1
  104.6 1.9 %collective-permute-start.1 = (f32[56,128]{1,0:T(8,128)S(1)}, f32[56,128]{1,0:T(8,128)S(1)}, u32[]{:S(2)}, u32[]{:S(2)}) collective-permute-start(f32[56,128]{1,0:T(8,128)S(1)} %get-tuple-element.32), channel_id=1, source_target_pairs={{0,1},{1,0},{2,3},{3,2},{4,5},{5,4},{6,7},{7,6},{8,9},{9,8},{10,11... | collective-permute-start | bytes 86024 | tf_op jit(solution)/shard_map/ppermute | solution.py:494
  106.5 2.2 %input_gradient.1 = bf16[64,16,512]{2,1,0:T(8,128)(2,1)} custom-call(bf16[64,19,8,128]{3,2,1,0:T(8,128)(2,1)S(1)} %all_to_all.10.got_ref, bf16[64,16,512]{2,1,0:T(8,128)(2,1)} %bitcast.24), custom_call_target="tpu_custom_call" | custom-call | bytes 4194304 | tf_op jit(solution)/shard_map/input_gradient/pallas_call | solution.py:417
  108.7 0.0 collective-permute-done.1.recv_ref
  108.8 0.8 finish.1
  (2 shorter events, 0.0 us)
Async XLA Ops:
  3.2 12.1 %copy-start.2 = (f32[16,225]{1,0:T(8,128)S(1)}, f32[16,225]{1,0:T(8,128)}, u32[]{:S(2)}) copy-start(f32[16,225]{1,0:T(8,128)} %param.11) | copy-start | bytes 43204
  3.2 39.2 %all-to-all-start = ((bf16[64,2,16,512]{3,2,1,0:T(8,128)(2,1)}), bf16[64,2,16,512]{3,2,1,0:T(8,128)(2,1)S(1)}, u32[]{:S(2)}, u32[]{:S(2)}) async-start(bf16[64,2,16,512]{3,2,1,0:T(8,128)(2,1)} %pair.1), calls=%async_computation | async-start | bytes 4194304 | tf_op jit(solution)/shard_map/all_to_all | solution.py:514
  15.3 27.1 %copy-start = (f32[512]{0:T(512)S(1)}, f32[512]{0:T(512)}, u32[]{:S(2)}) copy-start(f32[512]{0:T(512)} %param.13) | copy-start | bytes 6148
  15.4 27.0 %copy-start.1 = (f32[512]{0:T(512)S(1)}, f32[512]{0:T(512)}, u32[]{:S(2)}) copy-start(f32[512]{0:T(512)} %param.12) | copy-start | bytes 6148
  55.3 6.6 %collective-permute-start = (bf16[528,1024]{1,0:T(8,128)(2,1)S(1)}, bf16[528,1024]{1,0:T(8,128)(2,1)S(1)}, u32[]{:S(2)}, u32[]{:S(2)}) collective-permute-start(bf16[528,1024]{1,0:T(8,128)(2,1)S(1)} %get-tuple-element.28), channel_id=1, source_target_pairs={{0,1},{1,0},{2,3},{3,2},{4,5},{5,4},{6,7},{7,6},{8,9},{9,8},{10,11... | collective-permute-start | bytes 3244040 | tf_op jit(solution)/shard_map/ppermute | solution.py:494
  104.6 4.2 %collective-permute-start.1 = (f32[56,128]{1,0:T(8,128)S(1)}, f32[56,128]{1,0:T(8,128)S(1)}, u32[]{:S(2)}, u32[]{:S(2)}) collective-permute-start(f32[56,128]{1,0:T(8,128)S(1)} %get-tuple-element.32), channel_id=1, source_target_pairs={{0,1},{1,0},{2,3},{3,2},{4,5},{5,4},{6,7},{7,6},{8,9},{9,8},{10,11... | collective-permute-start | bytes 86024 | tf_op jit(solution)/shard_map/ppermute | solution.py:494

commit v10 on v9

--- a/solution.py
+++ b/solution.py
@@ -396,30 +396,42 @@
     )(core.reshape(1), got)
 
 
-def input_kernel(got_ref, dy_ref, grad_ref):
-    step, groups, width = dy_ref.shape
+def input_kernel(got_ref, dy_hbm, grad_hbm, dy_ref, grad_ref, ins, outs):
+    chips, groups, width = dy_ref.shape
     share = got_ref.shape[2]
+    pieces = ins.shape[0]
+    size = chips // pieces
+    at = [slice(i * size, (i + 1) * size) for i in range(pieces)]
+    fetches = [pltpu.make_async_copy(dy_hbm.at[a], dy_ref.at[a], ins.at[i]) for i, a in enumerate(at)]
+    stores = [pltpu.make_async_copy(grad_ref.at[a], grad_hbm.at[a], outs.at[i]) for i, a in enumerate(at)]
+    for fetch in fetches:
+        fetch.start()
     f32 = jnp.float32
-    chips = pl.ds(pl.multiple_of(pl.program_id(0) * step, step), step)
-    slot = 0
-    for b in range(width // 128):
-        cols = slice(b * 128, (b + 1) * 128)
-        for t in range(groups // share):
-            rows = slice(t * share, (t + 1) * share)
-            branch = got_ref[chips, slot].astype(f32)
-            grad_ref[:, rows, cols] = (dy_ref[:, rows, cols].astype(f32) + branch).astype(grad_ref.dtype)
-            slot += 1
+    for i, a in enumerate(at):
+        fetches[i].wait()
+        slot = 0
+        for b in range(width // 128):
+            cols = slice(b * 128, (b + 1) * 128)
+            for t in range(groups // share):
+                rows = slice(t * share, (t + 1) * share)
+                branch = got_ref[a, slot].astype(f32)
+                grad_ref[a, rows, cols] = (dy_ref[a, rows, cols].astype(f32) + branch).astype(grad_ref.dtype)
+                slot += 1
+        stores[i].start()
+    for store in stores:
+        store.wait()
 
 
 def input_gradient(got, dy):
-    chips, groups, width = dy.shape
-    block = pl.BlockSpec((chips // 2, groups, width), lambda i: (i, 0, 0))
+    pieces = 4
+    whole = pltpu.VMEM(dy.shape, dy.dtype)
+    sems = pltpu.SemaphoreType.DMA((pieces,))
     return pl.pallas_call(
         input_kernel,
-        grid=(2,),
         out_shape=jax.ShapeDtypeStruct(dy.shape, dy.dtype),
-        in_specs=[VMEM, block],
-        out_specs=block,
+        in_specs=[VMEM, HBM],
+        out_specs=HBM,
+        scratch_shapes=[whole, whole, sems, sems],
         compiler_params=pltpu.CompilerParams(vmem_limit_bytes=16 * MIB),
         cost_estimate=cost(0, 4 << 20),
         name="input_gradient",

time: 110 us -> 110 us (level)
  no operation moved by 1% of the time
where the time goes in v10:
time: 110 us; the launch traced here: 109 us
  blocking collectives  41.9 us (38%)
  waiting for transfers between devices  23.3 us (21%)
  Pallas kernels  22.8 us (21%)
  starting transfers between devices  17.1 us (16%)
  matrix products  3.2 us (3%)
    all_to_all x1, blocking collectives, local(): got = exchange(outgoing(branch, keep, recv, table, gvec))  41.9 us
    all_to_all x1, waiting for transfers between devices, local(): got = exchange(pair_of(x, dy))  23.3 us
    pallas_call x1, Pallas kernels, local_scores(): pl.pallas_call(functools.partial(scores_kernel, head_dim=head_dim), out_s...  12.9 us
    all_to_all x1, starting transfers between devices, local(): got = exchange(pair_of(x, dy))  12.1 us
    ppermute x2, starting transfers between devices, swap(): return lax.ppermute(a, axis, [(i, i ^ mask) for i in range(size)])  4.96 us
    pallas_call x1, Pallas kernels, local_back(): pl.pallas_call(back_kernel, out_shape=(shaped(MEMBERS, groups, width, dty...  3.61 us
    dot_general x1, matrix products, local(): jnp.einsum('bhr,kqr->bkhq', bias_table.reshape(heads // PACK, PACK, offse...  3.2 us
    pallas_call x1, Pallas kernels, pair_of(): pl.pallas_call(pair_kernel, grid=(chips // step,), out_shape=shaped(chips...  2.61 us
  transfers between devices with their start and end apart: 3, of which 1 were waited for; matrix products, arithmetic and copies ran while one was open for 3% of the time, Pallas kernels for 5%

profile of v10, /device:TPU:1, one launch (start us, length us, event | category | flops | bytes accessed | tf_op | source)
XLA Modules:
  0.0 109.5 jit_solution(7211424932079343322)
XLA Ops:
  0.6 2.6 %pair.1 = bf16[64,2,16,512]{3,2,1,0:T(8,128)(2,1)} custom-call(bf16[64,16,512]{2,1,0:T(8,128)(2,1)} %bitcast.25, bf16[64,16,512]{2,1,0:T(8,128)(2,1)} %bitcast.23), custom_call_target="tpu_custom_call" | custom-call | bytes 4194304 | tf_op jit(solution)/shard_map/pair/pallas_call | solution.py:319
  3.2 0.0 copy-start.2
  3.2 12.1 %all-to-all-start = ((bf16[64,2,16,512]{3,2,1,0:T(8,128)(2,1)}), bf16[64,2,16,512]{3,2,1,0:T(8,128)(2,1)S(1)}, u32[]{:S(2)}, u32[]{:S(2)}) async-start(bf16[64,2,16,512]{3,2,1,0:T(8,128)(2,1)} %pair.1), calls=%async_computation | async-start | bytes 4194304 | tf_op jit(solution)/shard_map/all_to_all | solution.py:526
  15.3 0.0 copy-start
  15.4 0.0 copy-start.1
  15.4 0.0 copy-done.2
  15.4 0.1 add_add_fusion
  15.5 3.2 %fusion.4 = f32[4,64,4,64]{3,2,0,1:T(4,128)S(1)} fusion(f32[4,4,225,1]{2,1,0,3:T(4,128)S(1)} %reshape.218, s32[64,64]{1,0:T(8,128)S(1)} %add_add_fusion), kind=kOutput, calls=%fused_computation.4 | convolution fusion | flops 177868800 | bytes 292928 | tf_op jit(solution)/shard_map/bhr,kqr->bkhq/dot_general | solution.py:517
  18.7 0.3 reshape.220
  19.1 0.1 copy.15.bias_ref
  19.1 23.3 %all-to-all-done.pair_ref = bf16[64,2,16,512]{3,2,1,0:T(8,128)(2,1)S(1)} async-done(((bf16[64,2,16,512]{3,2,1,0:T(8,128)(2,1)}), bf16[64,2,16,512]{3,2,1,0:T(8,128)(2,1)S(1)}, u32[]{:S(2)}, u32[]{:S(2)}) %all-to-all-start) | async-done | bytes 2097184 | tf_op jit(solution)/shard_map/all_to_all | solution.py:526
  42.4 0.0 copy-done
  42.4 0.0 copy-done.1
  42.4 12.9 %scores.1 = (f32[512,1024]{1,0:T(8,128)S(1)}, bf16[528,1024]{1,0:T(8,128)(2,1)S(1)}, f32[8,256]{1,0:T(8,128)S(1)}, bf16[1024,1536]{1,0:T(8,128)(2,1)S(1)}, f32[4...) custom-call(s32[1]{0:T(128)} %bitcast.core_ref, ...), custom_call_target="tpu_custom_call" | custom-call | flops 20000000000 | bytes 8388608 | tf_op jit(solution)/shard_map/scores/pallas_call | solution.py:278
  55.3 3.0 %collective-permute-start = (bf16[528,1024]{1,0:T(8,128)(2,1)S(1)}, bf16[528,1024]{1,0:T(8,128)(2,1)S(1)}, u32[]{:S(2)}, u32[]{:S(2)}) collective-permute-start(bf16[528,1024]{1,0:T(8,128)(2,1)S(1)} %get-tuple-element.28), channel_id=1, source_target_pairs={{0,1},{1,0},{2,3},{3,2},{4,5},{5,4},{6,7},{7,6},{8,9},{9,8},{10,11... | collective-permute-start | bytes 3244040 | tf_op jit(solution)/shard_map/ppermute | solution.py:506
  58.3 3.6 %back.1 = (bf16[64,16,512]{2,1,0:T(8,128)(2,1)S(1)}, f32[8,128]{1,0:T(8,128)S(1)}) custom-call(bf16[512,1536]{1,0:T(8,128)(2,1)S(1)} %get-tuple-element.22.wqkv_ref, f32[1,512]{1,0:T(1,128)S(1)} %bitcast.22, bf16[1024,1536]{1,0:T(8,128)(2,1)S(1)} %get-tuple-element.23.gproj, f32[4,1024,128]{2,1,0:T(8,128)S(1)} %get-tuple-element.24.hat, ...), custom_call_target="tpu_custom_call" | custom-call | flops 6000000000 | bytes 4194304 | tf_op jit(solution)/shard_map/back/pallas_call | solution.py:298
  61.9 0.0 collective-permute-done.recv_ref
  61.9 0.5 outgoing.1
  62.5 41.9 %all_to_all.10.got_ref = bf16[64,19,8,128]{3,2,1,0:T(8,128)(2,1)S(1)} all-to-all(bf16[64,19,8,128]{3,2,1,0:T(8,128)(2,1)S(1)} %outgoing.1), channel_id=1, replica_groups=mesh['x_lo'=2,'y'=4,'x_hi'=2,'z'=4,'core'=2] {'x_lo','y','x_hi','z'}, dimensions={0} | all-to-all | bytes 4980736 | tf_op jit(solution)/shard_map/all_to_all | solution.py:532
  104.3 0.2 sums.1
  104.6 1.9 %collective-permute-start.1 = (f32[56,128]{1,0:T(8,128)S(1)}, f32[56,128]{1,0:T(8,128)S(1)}, u32[]{:S(2)}, u32[]{:S(2)}) collective-permute-start(f32[56,128]{1,0:T(8,128)S(1)} %get-tuple-element.32), channel_id=1, source_target_pairs={{0,1},{1,0},{2,3},{3,2},{4,5},{5,4},{6,7},{7,6},{8,9},{9,8},{10,11... | collective-permute-start | bytes 86024 | tf_op jit(solution)/shard_map/ppermute | solution.py:506
  106.5 2.1 %input_gradient.1 = bf16[64,16,512]{2,1,0:T(8,128)(2,1)} custom-call(bf16[64,19,8,128]{3,2,1,0:T(8,128)(2,1)S(1)} %all_to_all.10.got_ref, bf16[64,16,512]{2,1,0:T(8,128)(2,1)} %bitcast.24), custom_call_target="tpu_custom_call" | custom-call | bytes 4194304 | tf_op jit(solution)/shard_map/input_gradient/pallas_call | solution.py:429
  108.6 0.0 collective-permute-done.1.recv_ref
  108.6 0.9 finish.1
  (2 shorter events, 0.0 us)
Async XLA Ops:
  3.2 12.1 %copy-start.2 = (f32[16,225]{1,0:T(8,128)S(1)}, f32[16,225]{1,0:T(8,128)}, u32[]{:S(2)}) copy-start(f32[16,225]{1,0:T(8,128)} %param.11) | copy-start | bytes 43204
  3.2 39.2 %all-to-all-start = ((bf16[64,2,16,512]{3,2,1,0:T(8,128)(2,1)}), bf16[64,2,16,512]{3,2,1,0:T(8,128)(2,1)S(1)}, u32[]{:S(2)}, u32[]{:S(2)}) async-start(bf16[64,2,16,512]{3,2,1,0:T(8,128)(2,1)} %pair.1), calls=%async_computation | async-start | bytes 4194304 | tf_op jit(solution)/shard_map/all_to_all | solution.py:526
  15.3 27.1 %copy-start = (f32[512]{0:T(512)S(1)}, f32[512]{0:T(512)}, u32[]{:S(2)}) copy-start(f32[512]{0:T(512)} %param.13) | copy-start | bytes 6148
  15.4 27.0 %copy-start.1 = (f32[512]{0:T(512)S(1)}, f32[512]{0:T(512)}, u32[]{:S(2)}) copy-start(f32[512]{0:T(512)} %param.12) | copy-start | bytes 6148
  55.3 6.6 %collective-permute-start = (bf16[528,1024]{1,0:T(8,128)(2,1)S(1)}, bf16[528,1024]{1,0:T(8,128)(2,1)S(1)}, u32[]{:S(2)}, u32[]{:S(2)}) collective-permute-start(bf16[528,1024]{1,0:T(8,128)(2,1)S(1)} %get-tuple-element.28), channel_id=1, source_target_pairs={{0,1},{1,0},{2,3},{3,2},{4,5},{5,4},{6,7},{7,6},{8,9},{9,8},{10,11... | collective-permute-start | bytes 3244040 | tf_op jit(solution)/shard_map/ppermute | solution.py:506
  104.6 4.0 %collective-permute-start.1 = (f32[56,128]{1,0:T(8,128)S(1)}, f32[56,128]{1,0:T(8,128)S(1)}, u32[]{:S(2)}, u32[]{:S(2)}) collective-permute-start(f32[56,128]{1,0:T(8,128)S(1)} %get-tuple-element.32), channel_id=1, source_target_pairs={{0,1},{1,0},{2,3},{3,2},{4,5},{5,4},{6,7},{7,6},{8,9},{9,8},{10,11... | collective-permute-start | bytes 86024 | tf_op jit(solution)/shard_map/ppermute | solution.py:506

commit v11 on v9

--- a/solution.py
+++ b/solution.py
@@ -397,33 +397,29 @@
 
 
 def input_kernel(got_ref, dy_ref, grad_ref):
-    step, groups, width = dy_ref.shape
+    _, groups, width = dy_ref.shape
     share = got_ref.shape[2]
     f32 = jnp.float32
-    chips = pl.ds(pl.multiple_of(pl.program_id(0) * step, step), step)
     slot = 0
     for b in range(width // 128):
         cols = slice(b * 128, (b + 1) * 128)
         for t in range(groups // share):
             rows = slice(t * share, (t + 1) * share)
-            branch = got_ref[chips, slot].astype(f32)
+            branch = got_ref[:, slot].astype(f32)
             grad_ref[:, rows, cols] = (dy_ref[:, rows, cols].astype(f32) + branch).astype(grad_ref.dtype)
             slot += 1
 
 
 def input_gradient(got, dy):
-    chips, groups, width = dy.shape
-    block = pl.BlockSpec((chips // 2, groups, width), lambda i: (i, 0, 0))
     return pl.pallas_call(
         input_kernel,
-        grid=(2,),
         out_shape=jax.ShapeDtypeStruct(dy.shape, dy.dtype),
-        in_specs=[VMEM, block],
-        out_specs=block,
+        in_specs=[VMEM] * 2,
+        out_specs=VMEM,
         compiler_params=pltpu.CompilerParams(vmem_limit_bytes=16 * MIB),
         cost_estimate=cost(0, 4 << 20),
         name="input_gradient",
-    )(got, in_hbm(dy))
+    )(got, dy)
 
 
 def finish_kernel(core_ref, keep_ref, recv_ref, qkv_ref, out_ref, table_ref, gain_ref, shift_ref):

time: 110 us -> 109 us (level)
  no operation moved by 1% of the time
where the time goes in v11:
time: 109 us
  blocking collectives  41.9 us (38%)
  waiting for transfers between devices  23.3 us (21%)
  Pallas kernels  22 us (20%)
  starting transfers between devices  17.1 us (16%)
  matrix products  3.2 us (3%)
    all_to_all x1, blocking collectives, local(): got = exchange(outgoing(branch, keep, recv, table, gvec))  41.9 us
    all_to_all x1, waiting for transfers between devices, local(): got = exchange(pair_of(x, dy))  23.3 us
    pallas_call x1, Pallas kernels, local_scores(): pl.pallas_call(functools.partial(scores_kernel, head_dim=head_dim), out_s...  12.9 us
    all_to_all x1, starting transfers between devices, local(): got = exchange(pair_of(x, dy))  12.1 us
    ppermute x2, starting transfers between devices, swap(): return lax.ppermute(a, axis, [(i, i ^ mask) for i in range(size)])  4.96 us
    pallas_call x1, Pallas kernels, local_back(): pl.pallas_call(back_kernel, out_shape=(shaped(MEMBERS, groups, width, dty...  3.61 us
    dot_general x1, matrix products, local(): jnp.einsum('bhr,kqr->bkhq', bias_table.reshape(heads // PACK, PACK, offse...  3.2 us
    pallas_call x1, Pallas kernels, pair_of(): pl.pallas_call(pair_kernel, grid=(chips // step,), out_shape=shaped(chips...  2.61 us
  transfers between devices with their start and end apart: 3, of which 1 were waited for; matrix products, arithmetic and copies ran while one was open for 3% of the time, Pallas kernels for 5%

profile of v11, /device:TPU:1, one launch (start us, length us, event | category | flops | bytes accessed | tf_op | source)
XLA Modules:
  0.0 108.7 jit_solution(3640679660909504707)
XLA Ops:
  0.6 2.6 %pair.1 = bf16[64,2,16,512]{3,2,1,0:T(8,128)(2,1)} custom-call(bf16[64,16,512]{2,1,0:T(8,128)(2,1)} %bitcast.25, bf16[64,16,512]{2,1,0:T(8,128)(2,1)} %bitcast.20), custom_call_target="tpu_custom_call" | custom-call | bytes 4194304 | tf_op jit(solution)/shard_map/pair/pallas_call | solution.py:319
  3.2 12.1 %all-to-all-start = ((bf16[64,2,16,512]{3,2,1,0:T(8,128)(2,1)}), bf16[64,2,16,512]{3,2,1,0:T(8,128)(2,1)S(1)}, u32[]{:S(2)}, u32[]{:S(2)}) async-start(bf16[64,2,16,512]{3,2,1,0:T(8,128)(2,1)} %pair.1), calls=%async_computation | async-start | bytes 4194304 | tf_op jit(solution)/shard_map/all_to_all | solution.py:510
  15.3 0.0 copy-start.1
  15.4 0.0 copy-start.2
  15.4 0.0 copy-done.3
  15.4 0.1 add_add_fusion
  15.5 3.2 %fusion.4 = f32[4,64,4,64]{3,2,0,1:T(4,128)S(1)} fusion(f32[4,4,225,1]{2,1,0,3:T(4,128)S(1)} %reshape.218, s32[64,64]{1,0:T(8,128)S(1)} %add_add_fusion), kind=kOutput, calls=%fused_computation.4 | convolution fusion | flops 177868800 | bytes 292928 | tf_op jit(solution)/shard_map/bhr,kqr->bkhq/dot_general | solution.py:501
  18.7 0.3 reshape.220
  19.1 0.1 copy.15.bias_ref
  19.1 23.3 %all-to-all-done.pair_ref = bf16[64,2,16,512]{3,2,1,0:T(8,128)(2,1)S(1)} async-done(((bf16[64,2,16,512]{3,2,1,0:T(8,128)(2,1)}), bf16[64,2,16,512]{3,2,1,0:T(8,128)(2,1)S(1)}, u32[]{:S(2)}, u32[]{:S(2)}) %all-to-all-start) | async-done | bytes 2097184 | tf_op jit(solution)/shard_map/all_to_all | solution.py:510
  42.4 0.0 copy-done.1
  42.4 0.0 copy-done.2
  42.4 12.9 %scores.1 = (f32[512,1024]{1,0:T(8,128)S(1)}, bf16[528,1024]{1,0:T(8,128)(2,1)S(1)}, f32[8,256]{1,0:T(8,128)S(1)}, bf16[1024,1536]{1,0:T(8,128)(2,1)S(1)}, f32[4...) custom-call(s32[1]{0:T(128)} %bitcast.core_ref, ...), custom_call_target="tpu_custom_call" | custom-call | flops 20000000000 | bytes 8388608 | tf_op jit(solution)/shard_map/scores/pallas_call | solution.py:278
  55.3 3.0 %collective-permute-start = (bf16[528,1024]{1,0:T(8,128)(2,1)S(1)}, bf16[528,1024]{1,0:T(8,128)(2,1)S(1)}, u32[]{:S(2)}, u32[]{:S(2)}) collective-permute-start(bf16[528,1024]{1,0:T(8,128)(2,1)S(1)} %get-tuple-element.28), channel_id=1, source_target_pairs={{0,1},{1,0},{2,3},{3,2},{4,5},{5,4},{6,7},{7,6},{8,9},{9,8},{10,11... | collective-permute-start | bytes 3244040 | tf_op jit(solution)/shard_map/ppermute | solution.py:490
  58.3 3.6 %back.1 = (bf16[64,16,512]{2,1,0:T(8,128)(2,1)S(1)}, f32[8,128]{1,0:T(8,128)S(1)}) custom-call(bf16[512,1536]{1,0:T(8,128)(2,1)S(1)} %get-tuple-element.22.wqkv_ref, f32[1,512]{1,0:T(1,128)S(1)} %bitcast.24, bf16[1024,1536]{1,0:T(8,128)(2,1)S(1)} %get-tuple-element.23.gproj, f32[4,1024,128]{2,1,0:T(8,128)S(1)} %get-tuple-element.24.hat, ...), custom_call_target="tpu_custom_call" | custom-call | flops 6000000000 | bytes 4194304 | tf_op jit(solution)/shard_map/back/pallas_call | solution.py:298
  61.9 0.0 collective-permute-done.recv_ref
  61.9 0.5 outgoing.1
  62.4 41.9 %all_to_all.10.got_ref = bf16[64,19,8,128]{3,2,1,0:T(8,128)(2,1)S(1)} all-to-all(bf16[64,19,8,128]{3,2,1,0:T(8,128)(2,1)S(1)} %outgoing.1), channel_id=1, replica_groups=mesh['x_lo'=2,'y'=4,'x_hi'=2,'z'=4,'core'=2] {'x_lo','y','x_hi','z'}, dimensions={0} | all-to-all | bytes 4980736 | tf_op jit(solution)/shard_map/all_to_all | solution.py:516
  104.3 0.2 sums.1
  104.6 1.9 %collective-permute-start.1 = (f32[56,128]{1,0:T(8,128)S(1)}, f32[56,128]{1,0:T(8,128)S(1)}, u32[]{:S(2)}, u32[]{:S(2)}) collective-permute-start(f32[56,128]{1,0:T(8,128)S(1)} %get-tuple-element.32), channel_id=1, source_target_pairs={{0,1},{1,0},{2,3},{3,2},{4,5},{5,4},{6,7},{7,6},{8,9},{9,8},{10,11... | collective-permute-start | bytes 86024 | tf_op jit(solution)/shard_map/ppermute | solution.py:490
  106.5 0.0 copy-done
  106.5 1.3 %input_gradient.1 = bf16[64,16,512]{2,1,0:T(8,128)(2,1)} custom-call(bf16[64,19,8,128]{3,2,1,0:T(8,128)(2,1)S(1)} %all_to_all.10.got_ref, bf16[64,16,512]{2,1,0:T(8,128)(2,1)S(1)} %bitcast.21), custom_call_target="tpu_custom_call" | custom-call | bytes 4194304 | tf_op jit(solution)/shard_map/input_gradient/pallas_call | solution.py:414
  107.8 0.0 collective-permute-done.1.recv_ref
  107.8 0.8 finish.1
  (4 shorter events, 0.0 us)
Async XLA Ops:
  3.2 12.1 %copy-start.3 = (f32[16,225]{1,0:T(8,128)S(1)}, f32[16,225]{1,0:T(8,128)}, u32[]{:S(2)}) copy-start(f32[16,225]{1,0:T(8,128)} %param.11) | copy-start | bytes 43204
  3.2 39.2 %all-to-all-start = ((bf16[64,2,16,512]{3,2,1,0:T(8,128)(2,1)}), bf16[64,2,16,512]{3,2,1,0:T(8,128)(2,1)S(1)}, u32[]{:S(2)}, u32[]{:S(2)}) async-start(bf16[64,2,16,512]{3,2,1,0:T(8,128)(2,1)} %pair.1), calls=%async_computation | async-start | bytes 4194304 | tf_op jit(solution)/shard_map/all_to_all | solution.py:510
  15.3 27.1 %copy-start.1 = (f32[512]{0:T(512)S(1)}, f32[512]{0:T(512)}, u32[]{:S(2)}) copy-start(f32[512]{0:T(512)} %param.13) | copy-start | bytes 6148
  15.4 27.0 %copy-start.2 = (f32[512]{0:T(512)S(1)}, f32[512]{0:T(512)}, u32[]{:S(2)}) copy-start(f32[512]{0:T(512)} %param.12) | copy-start | bytes 6148
  55.3 6.6 %collective-permute-start = (bf16[528,1024]{1,0:T(8,128)(2,1)S(1)}, bf16[528,1024]{1,0:T(8,128)(2,1)S(1)}, u32[]{:S(2)}, u32[]{:S(2)}) collective-permute-start(bf16[528,1024]{1,0:T(8,128)(2,1)S(1)} %get-tuple-element.28), channel_id=1, source_target_pairs={{0,1},{1,0},{2,3},{3,2},{4,5},{5,4},{6,7},{7,6},{8,9},{9,8},{10,11... | collective-permute-start | bytes 3244040 | tf_op jit(solution)/shard_map/ppermute | solution.py:490
  104.3 2.2 %copy-start = (bf16[16,64,512]{2,1,0:T(8,128)(2,1)S(1)}, bf16[16,64,512]{2,1,0:T(8,128)(2,1)}, u32[]{:S(2)}) copy-start(bf16[16,64,512]{2,1,0:T(8,128)(2,1)} %param.8) | copy-start | bytes 3145732
  104.6 3.2 %collective-permute-start.1 = (f32[56,128]{1,0:T(8,128)S(1)}, f32[56,128]{1,0:T(8,128)S(1)}, u32[]{:S(2)}, u32[]{:S(2)}) collective-permute-start(f32[56,128]{1,0:T(8,128)S(1)} %get-tuple-element.32), channel_id=1, source_target_pairs={{0,1},{1,0},{2,3},{3,2},{4,5},{5,4},{6,7},{7,6},{8,9},{9,8},{10,11... | collective-permute-start | bytes 86024 | tf_op jit(solution)/shard_map/ppermute | solution.py:490
